TPU v7x, 32 devices: a whole 2x2x4 slice. The times are simulated.
32 devices in a mesh: expert: 8 (over z, y), shard: 4 (over x, core).
Axes of the slice: x: 2, y: 2, z: 4, core: 2. Of those that a mesh axis runs over, the one named last changes fastest.
Arguments:
- tokens: bfloat16 [16384, 768], P(('expert', 'shard')), may hold values from -6 to 6
- w_qkv: bfloat16 [768, 2304], P('shard'), may hold values from -0.21875 to 0.21875
- w_out: bfloat16 [768, 768], P('shard'), may hold values from -0.875 to 0.875
- router: bfloat16 [768, 8], P('shard'), may hold values from -0.15625 to 0.15625
- gain_attn: bfloat16 [768], P('shard'), may hold values from 0.099609375 to 1.8984375
- gain_ffn: bfloat16 [768], P('shard'), may hold values from 0.099609375 to 1.8984375
- rel_bias: bfloat16 [12, 32], P('shard'), may hold values from -4 to 4
- w_gate: bfloat16 [8, 768, 3072], P('expert', None, 'shard'), may hold values from -0.21875 to 0.21875
- w_up: bfloat16 [8, 768, 3072], P('expert', None, 'shard'), may hold values from -0.21875 to 0.21875
- w_down: bfloat16 [8, 3072, 768], P('expert', 'shard'), may hold values from -0.109375 to 0.109375
- routes: int32 [16384, 2], P(('expert', 'shard')), may hold values from 0 to 7, all different within a row; in each aligned block of 512 rows (0 to 511, 512 to 1023, ...) at most 256 rows name the same one
- lengths: int32 [8, 3], P('expert'), may hold values from 1 to 1792, 2048 in all within a row
- cotangent: bfloat16 [16384, 768], P(('expert', 'shard')), may hold values from -6 to 6
Outputs:
- output: bfloat16 [16384, 768], P(('expert', 'shard'))
- grad_tokens: float32 [16384, 768], P(('expert', 'shard'))
- grad_qkv: float32 [768, 2304], P('shard')
- grad_out: float32 [768, 768], P('shard')
- grad_router: float32 [768, 8], P('shard')
- grad_gain_attn: float32 [768], P('shard')
- grad_gain_ffn: float32 [768], P('shard')
- grad_rel_bias: float32 [12, 32], P('shard')
- grad_gate: float32 [8, 768, 3072], P('expert', None, 'shard')
- grad_up: float32 [8, 768, 3072], P('expert', None, 'shard')
- grad_down: float32 [8, 3072, 768], P('expert', 'shard')
Inputs may be any that keep to these rules, and one draw needn't show every extreme that they name: `routes`: each row names 2 different experts; among the 512 rows of one device no expert is named more than 256 times. Row g gives the lengths of the 3 sequences of group g, which holds the 2048 tokens of 4 consecutive devices in order; each row sums to 2048 and its largest entry is 1792.
All inputs are finite; a program needn't handle non-finite values.
Results may differ from a plain program's by a relative error of at most 0.019.
Values may be sent and summed in bfloat16 or wider, within the bound.
A program may use at most 384 MiB of HBM per device.

v0:
```python
import jax
import jax.numpy as jnp
from jax import lax
from jax.sharding import PartitionSpec as P

norm_epsilon = 1e-06
bucket_borders = (16, 23, 32, 45, 64, 91, 128, 181, 256, 362, 512, 724, 1024, 1448, 2048, 2896)


def bucket_of(distance):
    clipped = jnp.maximum(distance, 0)
    bucket_id = jnp.minimum(clipped, 15)
    for border in bucket_borders:
        bucket_id = bucket_id + (clipped >= border).astype(jnp.int32)
    return bucket_id


def bias_from_table(bias_table, buckets):
    head_count, bucket_count = bias_table.shape
    total = jnp.zeros((head_count,) + buckets.shape, jnp.float32)
    for column in range(bucket_count):
        total = total + jnp.where(
            (buckets == column)[None], bias_table[:, column][:, None, None], 0.0
        )
    return total


def bias_gradient(grad_scores, buckets, bucket_count):
    columns = [
        jnp.sum(jnp.where((buckets == column)[None], grad_scores, 0.0), axis=(1, 2))
        for column in range(bucket_count)
    ]
    return jnp.stack(columns, axis=1)


def sequence_of(positions, seq_ends):
    return jnp.sum((positions[:, None] >= seq_ends[None, :]).astype(jnp.int32), axis=1)


def norm_forward(values):
    inverse = lax.rsqrt(jnp.mean(values * values, axis=-1, keepdims=True) + norm_epsilon)
    return (values * inverse, inverse)


def norm_backward(grad_normed, normalized, inverse, gain_vector):
    grad_gain = jnp.sum(grad_normed * normalized, axis=0)
    scaled = grad_normed * gain_vector
    grad_values = inverse * (
        scaled - normalized * jnp.mean(scaled * normalized, axis=-1, keepdims=True)
    )
    return (grad_values, grad_gain)


def gated_unit(gate_value, up_value):
    return jax.nn.gelu(gate_value) * up_value


def expert_forward(rows_in, gate_weight, up_weight, down_weight):
    gate_proj = jnp.einsum("erd,edf->erf", rows_in, gate_weight, preferred_element_type=jnp.float32)
    up_proj = jnp.einsum("erd,edf->erf", rows_in, up_weight, preferred_element_type=jnp.float32)
    hidden = gated_unit(gate_proj, up_proj).astype(jnp.bfloat16)
    down_sum = jnp.einsum("erf,efd->erd", hidden, down_weight, preferred_element_type=jnp.float32)
    return (gate_proj, up_proj, hidden, down_sum)


def expert_backward(
    rows_in, gate_proj, up_proj, hidden, grad_rows_out, gate_weight, up_weight, down_weight
):
    grad_hid = jnp.einsum(
        "erd,efd->erf", grad_rows_out, down_weight, preferred_element_type=jnp.float32
    )
    grad_down_w = jnp.einsum(
        "erf,erd->efd", hidden, grad_rows_out, preferred_element_type=jnp.float32
    )
    unused, pullback = jax.vjp(gated_unit, gate_proj, up_proj)
    grad_gate_f, grad_up_f = pullback(grad_hid)
    gate_low = grad_gate_f.astype(jnp.bfloat16)
    up_low = grad_up_f.astype(jnp.bfloat16)
    grad_gate_w = jnp.einsum("erd,erf->edf", rows_in, gate_low, preferred_element_type=jnp.float32)
    grad_up_w = jnp.einsum("erd,erf->edf", rows_in, up_low, preferred_element_type=jnp.float32)
    grad_input = jnp.einsum(
        "erf,edf->erd", gate_low, gate_weight, preferred_element_type=jnp.float32
    )
    grad_input = grad_input + jnp.einsum(
        "erf,edf->erd", up_low, up_weight, preferred_element_type=jnp.float32
    )
    return (grad_input, grad_gate_w, grad_up_w, grad_down_w)


def local(
    tokens,
    w_qkv,
    w_out,
    router,
    gain_attn,
    gain_ffn,
    rel_bias,
    w_gate,
    w_up,
    w_down,
    routes,
    lengths,
    cotangent,
):
    shard_index = lax.axis_index("shard")
    full_qkv, full_out, full_router, full_gain_attn, full_gain_ffn, full_table = (
        lax.all_gather(w_qkv, "shard", axis=0, tiled=True),
        lax.all_gather(w_out, "shard", axis=0, tiled=True),
        lax.all_gather(router, "shard", axis=0, tiled=True),
        lax.all_gather(gain_attn, "shard", axis=0, tiled=True),
        lax.all_gather(gain_ffn, "shard", axis=0, tiled=True),
        lax.all_gather(rel_bias, "shard", axis=0, tiled=True),
    )
    tok_count, model_width = tokens.shape
    head_count, bucket_count = full_table.shape
    head_dim = model_width // head_count
    score_scale = head_dim ** (-0.5)
    expert_count = full_router.shape[1]
    route_count = routes.shape[1]
    capacity = 2 * route_count * tok_count // expert_count
    inputs = tokens.astype(jnp.float32)
    attn_gain = full_gain_attn.astype(jnp.float32)
    ffn_gain = full_gain_ffn.astype(jnp.float32)
    bias_table = full_table.astype(jnp.float32)
    normed_one, inverse_one = norm_forward(inputs)
    normed_attn = (normed_one * attn_gain).astype(jnp.bfloat16)
    qkv = jnp.dot(normed_attn, full_qkv, preferred_element_type=jnp.float32).astype(jnp.bfloat16)
    key_local = qkv[:, model_width : 2 * model_width]
    value_local = qkv[:, 2 * model_width :]
    keys_all, values_all = (
        lax.all_gather(key_local, "shard", axis=0, tiled=True),
        lax.all_gather(value_local, "shard", axis=0, tiled=True),
    )
    group_tok = keys_all.shape[0]
    key_heads = keys_all.reshape(group_tok, head_count, head_dim)
    value_heads = values_all.reshape(group_tok, head_count, head_dim)
    seq_ends = jnp.cumsum(lengths[0])
    key_pos = jnp.arange(group_tok, dtype=jnp.int32)
    key_seq = sequence_of(key_pos, seq_ends)
    query_pos = shard_index * tok_count + jnp.arange(tok_count, dtype=jnp.int32)
    block_rows = min(tok_count, 512)
    blocks = tok_count // block_rows
    query_blocks = qkv[:, :model_width].reshape(blocks, block_rows, head_count, head_dim)
    pos_blocks = query_pos.reshape(blocks, block_rows)

    def block_scores(query_block, block_pos):
        products = jnp.einsum(
            "qhd,khd->hqk", query_block, key_heads, preferred_element_type=jnp.float32
        )
        distance = block_pos[:, None] - key_pos[None, :]
        buckets = bucket_of(distance)
        allowed = (sequence_of(block_pos, seq_ends)[:, None] == key_seq[None, :]) & (distance >= 0)
        scores = products * score_scale + bias_from_table(bias_table, buckets)
        return (jnp.where(allowed[None], scores, -1e30), allowed, buckets)

    def attend_block(operands):
        query_block, block_pos = operands
        scores, allowed, buckets = block_scores(query_block, block_pos)
        row_max = jnp.max(scores, axis=2, keepdims=True)
        weights = jnp.where(allowed[None], jnp.exp(scores - row_max), 0.0)
        row_total = jnp.sum(weights, axis=2, keepdims=True)
        probs_low = (weights / row_total).astype(jnp.bfloat16)
        blended = jnp.einsum(
            "hqk,khd->qhd", probs_low, value_heads, preferred_element_type=jnp.float32
        )
        return (blended.astype(jnp.bfloat16), (row_max + jnp.log(row_total))[:, :, 0])

    attended_blocks, log_totals = lax.map(attend_block, (query_blocks, pos_blocks))
    attended = attended_blocks.reshape(tok_count, model_width)
    hidden_one = inputs + jnp.dot(attended, full_out, preferred_element_type=jnp.float32)
    normed_two, inverse_two = norm_forward(hidden_one)
    normed_ffn = (normed_two * ffn_gain).astype(jnp.bfloat16)
    logits = jnp.dot(normed_ffn, full_router, preferred_element_type=jnp.float32)
    expert_ids = jnp.arange(expert_count, dtype=jnp.int32)
    chosen_mask = routes[:, :, None] == expert_ids[None, None, :]
    chosen = jnp.sum(jnp.where(chosen_mask, logits[:, None, :], 0.0), axis=2)
    gate_weights = jax.nn.softmax(chosen, axis=1)
    flat_routes = routes.reshape(-1)
    onehot_rows = (flat_routes[:, None] == expert_ids[None, :]).astype(jnp.int32)
    earlier = jnp.cumsum(onehot_rows, axis=0) - onehot_rows
    position = jnp.sum(earlier * onehot_rows, axis=1)
    slot_index = flat_routes * capacity + position
    copies = jnp.repeat(normed_ffn, route_count, axis=0)
    outgoing = (
        jnp.zeros((expert_count * capacity, model_width), jnp.bfloat16).at[slot_index].set(copies)
    )
    received = lax.all_to_all(
        outgoing.reshape(expert_count, capacity, model_width),
        "expert",
        split_axis=0,
        concat_axis=1,
        tiled=True,
    )
    gate_weight, up_weight, down_weight = (w_gate, w_up, w_down)
    rows_in = lax.all_gather(received, "shard", axis=1, tiled=True)
    gate_proj, up_proj, hidden, down_sum = expert_forward(
        rows_in, gate_weight, up_weight, down_weight
    )
    expert_result = lax.psum_scatter(
        down_sum.astype(jnp.bfloat16), "shard", scatter_dimension=1, tiled=True
    )
    returned = lax.all_to_all(expert_result, "expert", split_axis=1, concat_axis=0, tiled=True)
    routed_out = returned.reshape(expert_count * capacity, model_width)[slot_index]
    routed_out = routed_out.reshape(tok_count, route_count, model_width).astype(jnp.float32)
    mixed_out = hidden_one + jnp.sum(gate_weights[:, :, None] * routed_out, axis=1)
    output = mixed_out.astype(jnp.bfloat16)
    grad_mixed = cotangent.astype(jnp.float32)
    grad_expert = (gate_weights[:, :, None] * grad_mixed[:, None, :]).astype(jnp.bfloat16)
    grad_gate_weights = jnp.sum(grad_mixed[:, None, :] * routed_out, axis=2)
    grad_chosen = gate_weights * (
        grad_gate_weights - jnp.sum(gate_weights * grad_gate_weights, axis=1, keepdims=True)
    )
    grad_logits = jnp.sum(jnp.where(chosen_mask, grad_chosen[:, :, None], 0.0), axis=1).astype(
        jnp.bfloat16
    )
    grad_router_full = jnp.einsum(
        "td,te->de", normed_ffn, grad_logits, preferred_element_type=jnp.float32
    )
    grad_normed_ffn = jnp.einsum(
        "te,de->td", grad_logits, full_router, preferred_element_type=jnp.float32
    )
    grad_outgoing = jnp.zeros((expert_count * capacity, model_width), jnp.bfloat16)
    grad_outgoing = grad_outgoing.at[slot_index].set(
        grad_expert.reshape(tok_count * route_count, model_width)
    )
    grad_received = lax.all_to_all(
        grad_outgoing.reshape(expert_count, capacity, model_width),
        "expert",
        split_axis=0,
        concat_axis=1,
        tiled=True,
    )
    grad_rows_out = lax.all_gather(grad_received, "shard", axis=1, tiled=True)
    grad_input, grad_gate_w, grad_up_w, grad_down_w = expert_backward(
        rows_in, gate_proj, up_proj, hidden, grad_rows_out, gate_weight, up_weight, down_weight
    )
    grad_sent = lax.psum_scatter(
        grad_input.astype(jnp.bfloat16), "shard", scatter_dimension=1, tiled=True
    )
    grad_back = lax.all_to_all(grad_sent, "expert", split_axis=1, concat_axis=0, tiled=True)
    grad_copies = grad_back.reshape(expert_count * capacity, model_width)[slot_index]
    grad_copies = grad_copies.astype(jnp.float32).reshape(tok_count, route_count, model_width)
    grad_normed_ffn = grad_normed_ffn + jnp.sum(grad_copies, axis=1)
    grad_two, grad_gain_ffn_full = norm_backward(grad_normed_ffn, normed_two, inverse_two, ffn_gain)
    grad_hidden_one = grad_mixed + grad_two
    grad_attn_low = grad_hidden_one.astype(jnp.bfloat16)
    grad_out_full = jnp.einsum(
        "td,te->de", attended, grad_attn_low, preferred_element_type=jnp.float32
    )
    grad_attended = jnp.einsum(
        "te,de->td", grad_attn_low, full_out, preferred_element_type=jnp.float32
    ).astype(jnp.bfloat16)
    grad_att_blocks = grad_attended.reshape(blocks, block_rows, head_count, head_dim)

    def attend_back(running, operands):
        grad_keys_acc, grad_values_acc, grad_table_acc = running
        query_block, block_pos, grad_block, log_total = operands
        scores, allowed, buckets = block_scores(query_block, block_pos)
        probs = jnp.where(allowed[None], jnp.exp(scores - log_total[:, :, None]), 0.0)
        probs_low = probs.astype(jnp.bfloat16)
        grad_probs = jnp.einsum(
            "qhd,khd->hqk", grad_block, value_heads, preferred_element_type=jnp.float32
        )
        row_delta = jnp.sum(probs * grad_probs, axis=2, keepdims=True)
        grad_scores = probs * (grad_probs - row_delta)
        table_part = bias_gradient(grad_scores, buckets, bucket_count)
        grad_products = (grad_scores * score_scale).astype(jnp.bfloat16)
        grad_query = jnp.einsum(
            "hqk,khd->qhd", grad_products, key_heads, preferred_element_type=jnp.float32
        )
        keys_part = jnp.einsum(
            "hqk,qhd->khd", grad_products, query_block, preferred_element_type=jnp.float32
        )
        values_part = jnp.einsum(
            "hqk,qhd->khd", probs_low, grad_block, preferred_element_type=jnp.float32
        )
        return (
            (grad_keys_acc + keys_part, grad_values_acc + values_part, grad_table_acc + table_part),
            grad_query,
        )

    start_state = (
        jnp.zeros((group_tok, head_count, head_dim), jnp.float32),
        jnp.zeros((group_tok, head_count, head_dim), jnp.float32),
        jnp.zeros((head_count, bucket_count), jnp.float32),
    )
    (grad_keys_all, grad_values_all, grad_table_full), grad_query_blocks = lax.scan(
        attend_back, start_state, (query_blocks, pos_blocks, grad_att_blocks, log_totals)
    )
    grad_keys_local, grad_values_local = (
        lax.psum_scatter(
            grad_keys_all.reshape(group_tok, model_width).astype(jnp.bfloat16),
            "shard",
            scatter_dimension=0,
            tiled=True,
        ).astype(jnp.float32),
        lax.psum_scatter(
            grad_values_all.reshape(group_tok, model_width).astype(jnp.bfloat16),
            "shard",
            scatter_dimension=0,
            tiled=True,
        ).astype(jnp.float32),
    )
    grad_qkv_cols = jnp.concatenate(
        [grad_query_blocks.reshape(tok_count, model_width), grad_keys_local, grad_values_local],
        axis=1,
    ).astype(jnp.bfloat16)
    grad_qkv_full = jnp.einsum(
        "td,te->de", normed_attn, grad_qkv_cols, preferred_element_type=jnp.float32
    )
    grad_normed_attn = jnp.einsum(
        "te,de->td", grad_qkv_cols, full_qkv, preferred_element_type=jnp.float32
    )
    grad_one, grad_gain_attn_full = norm_backward(
        grad_normed_attn, normed_one, inverse_one, attn_gain
    )
    grad_tokens = grad_hidden_one + grad_one
    shares = (
        lax.psum_scatter(
            grad_qkv_full.astype(jnp.bfloat16), "shard", scatter_dimension=0, tiled=True
        ).astype(jnp.float32),
        lax.psum_scatter(
            grad_out_full.astype(jnp.bfloat16), "shard", scatter_dimension=0, tiled=True
        ).astype(jnp.float32),
        lax.psum_scatter(
            grad_router_full.astype(jnp.bfloat16), "shard", scatter_dimension=0, tiled=True
        ).astype(jnp.float32),
        lax.psum_scatter(
            grad_gain_attn_full.astype(jnp.bfloat16), "shard", scatter_dimension=0, tiled=True
        ).astype(jnp.float32),
        lax.psum_scatter(
            grad_gain_ffn_full.astype(jnp.bfloat16), "shard", scatter_dimension=0, tiled=True
        ).astype(jnp.float32),
        lax.psum_scatter(
            grad_table_full.astype(jnp.bfloat16), "shard", scatter_dimension=0, tiled=True
        ).astype(jnp.float32),
    )
    pieces = lax.psum((shares[0], shares[1], shares[2], shares[3], shares[4], shares[5]), "expert")
    return (
        output,
        grad_tokens,
        pieces[0],
        pieces[1],
        pieces[2],
        pieces[3],
        pieces[4],
        pieces[5],
        grad_gate_w,
        grad_up_w,
        grad_down_w,
    )


def solution(mesh):
    in_specs = (
        P(("expert", "shard"), None),
        P("shard", None),
        P("shard", None),
        P("shard", None),
        P("shard"),
        P("shard"),
        P("shard", None),
        P("expert", None, "shard"),
        P("expert", None, "shard"),
        P("expert", "shard", None),
        P(("expert", "shard"), None),
        P("expert", None),
        P(("expert", "shard"), None),
    )
    out_specs = (
        P(("expert", "shard"), None),
        P(("expert", "shard"), None),
        P("shard", None),
        P("shard", None),
        P("shard", None),
        P("shard"),
        P("shard"),
        P("shard", None),
        P("expert", None, "shard"),
        P("expert", None, "shard"),
        P("expert", "shard", None),
    )
    return jax.shard_map(local, mesh=mesh, in_specs=in_specs, out_specs=out_specs, check_vma=False)
```

profile of v0, /device:TPU:0, one launch (start us, length us, event | category | flops | bytes accessed | tf_op | source)
XLA Modules:
  0.0 1563.0 jit_solution(7165421096537259629)
XLA Ops:
  11.7 8.3 all-reduce.7
  21.5 21.6 %all-gather.9.cloned.1.call-done = bf16[768,2304]{1,0:T(8,128)(2,1)} async-done(((bf16[192,2304]{1,0:T(8,128)(2,1)}), bf16[768,2304]{1,0:T(8,128)(2,1)}) %all-gather.9.cloned.1.call-update) | async-done | bytes 3538960 | tf_op jit(solution)/shard_map/all_gather | solution.py:107
  60.9 31.5 %fusion.58 = (pred[512,2048]{1,0:T(8,128)(4,1)}, pred[512,2048]{1,0:T(8,128)(4,1)}, pred[512,2048]{1,0:T(8,128)(4,1)}, pred[512,2048]{1,0:T(8,128)(4,1)}, pred[5...) fusion(s32[512]{0:T(512)S(1)} %iota_add_fusion, ...), kind=kLoop, calls=%fused_computation.108 | loop fusion | flops 90177536 | bytes 34615296 | tf_op jit(solution)/shard_map/while/body/eval_jaxpr/and | solution.py:152
  100.2 194.4 %fusion.119 = (f32[12,512]{1,0:T(8,128)S(1)}, f32[12,512,2048]{2,1,0:T(8,128)}) fusion(f32[12]{0:T(128)S(1)} %get-tuple-element.205, pred[512,2048]{1,0:T(8,128)(4,1)} %get-tuple-element.286, f32[12]{0:T(128)S(1)} %get-tuple-element.206, pred[512,2048]{1,0:T(8,128)(4,1)} %get-tuple-element.285, f32[12]{0:T(128)S(1)} %get-tuple-element.207, ...), kind=kOutput, calls=%fused_computation.300 | convolution fusion | flops 2453661696 | bytes 88892928 | tf_op jit(solution)/shard_map/while/body/eval_jaxpr/qhd,khd->hqk/dot_general | solution.py:147
  295.3 21.4 %fusion.2 = f32[12,512]{1,0:T(8,128)S(1)} fusion(f32[12,512,2048]{2,1,0:T(8,128)} %get-tuple-element.291, f32[12,512]{1,0:T(8,128)S(1)} %get-tuple-element.290, pred[512,2048]{1,0:T(8,128)(4,1)S(1)} %copy-done.11), kind=kLoop, calls=%fused_computation.45 | loop fusion | flops 37742592 | bytes 51429376 | tf_op jit(solution)/shard_map/while/body/eval_jaxpr/reduce_sum | solution.py:161
  321.5 21.1 %fusion.89 = bf16[12,64,512]{2,1,0:T(8,128)(2,1)} fusion(bf16[2048,12,64]{0,2,1:T(8,128)(2,1)} %bitcast.254, f32[12,512,2048]{2,1,0:T(8,128)} %get-tuple-element.291, f32[12,512]{1,0:T(8,128)S(1)} %fusion.2, f32[12,512]{1,0:T(8,128)} %copy-done.22, pred[512,2048]{1,0:T(8,128)(4,1)S(1)} %copy-done.12), kind=kOutput, calls=%fused_computation.181 | convolution fusion | flops 1661337600 | bytes 55361536 | tf_op jit(solution)/shard_map/while/body/eval_jaxpr/hqk,khd->qhd/dot_general | solution.py:163
  361.1 76.7 %all_to_all.42 = bf16[8,256,768]{2,1,0:T(8,128)(2,1)} all-to-all(bf16[8,256,768]{2,1,0:T(8,128)(2,1)} %bitcast.251), channel_id=1, replica_groups=mesh['expert'=8,'shard'=4] {'expert'}, dimensions={0} | all-to-all | bytes 6291456 | tf_op jit(solution)/shard_map/all_to_all | solution.py:187
  453.5 8.4 scatter_custom_fusion.1
  462.0 75.9 %all_to_all.43 = bf16[8,256,768]{2,1,0:T(8,128)(2,1)} all-to-all(bf16[8,256,768]{2,1,0:T(8,128)(2,1)} %bitcast.250), channel_id=1, replica_groups=mesh['expert'=8,'shard'=4] {'expert'}, dimensions={0} | all-to-all | bytes 6291456 | tf_op jit(solution)/shard_map/all_to_all | solution.py:226
  538.2 19.2 %fusion.30 = f32[8192,768]{1,0:T(8,128)} fusion(bf16[1,8192,768]{2,1,0:T(8,128)(2,1)} %all-gather.17.cloned.1.call-done, bf16[1,768,768]{2,1,0:T(8,128)(2,1)} %param.21), kind=kOutput, calls=%fused_computation.77 | convolution fusion | flops 9663676416 | bytes 38928384 | tf_op jit(solution)/shard_map/erd,edf->erf/dot_general | solution.py:60
  557.4 13.3 fusion.32
  570.8 47.5 %all-gather.19.cloned.1.call-done = bf16[1,8192,768]{2,1,0:T(8,128)(2,1)} async-done(((bf16[1,2048,768]{2,1,0:T(8,128)(2,1)}), bf16[1,8192,768]{2,1,0:T(8,128)(2,1)}) %all-gather.19.cloned.1.call-update) | async-done | bytes 12582928 | tf_op jit(solution)/shard_map/all_gather | solution.py:233
  618.2 43.7 %multiply_convert_fusion.1 = (bf16[8192,768]{1,0:T(8,128)(2,1)}, bf16[8192,768]{1,0:T(8,128)(2,1)}, bf16[8192,768]{1,0:T(8,128)(2,1)}) fusion(f32[8192,768]{1,0:T(8,128)} %fusion.32, f32[8192,768]{1,0:T(8,128)} %fusion.30, bf16[1,768,768]{2,1,0:T(8,128)(2,1)S(1)} %copy-done, bf16[1,8192,768]{2,1,0:T(8,128)(2,1)} %all-gather.19.cloned.1.call-done), kind=kOutput, calls=%fused_computation.60 | convolution fusion | flops 9827254272 | bytes 101842944 | tf_op jit(solution)/shard_map/erd,efd->erf/dot_general | solution.py:69
  662.0 17.2 %fusion.35 = bf16[1,8192,768]{2,1,0:T(8,128)(2,1)} fusion(bf16[8192,768]{1,0:T(8,128)(2,1)} %get-tuple-element.249, bf16[1,768,768]{2,1,0:T(8,128)(2,1)S(1)} %copy-done), kind=kOutput, calls=%fused_computation.82 | convolution fusion | flops 9669967872 | bytes 26345472 | tf_op jit(solution)/shard_map/erf,efd->erd/dot_general | solution.py:62
  679.2 21.5 %fusion.94 = f32[8192,768]{1,0:T(8,128)} fusion(bf16[8192,768]{1,0:T(8,128)(2,1)} %get-tuple-element.248, bf16[1,768,768]{2,1,0:T(8,128)(2,1)S(1)} %copy-done.47), kind=kOutput, calls=%fused_computation.186 | convolution fusion | flops 9663676416 | bytes 38928384 | tf_op jit(solution)/shard_map/erf,edf->erd/dot_general | solution.py:81
  700.7 22.5 %fusion.34 = bf16[1,8192,768]{2,1,0:T(8,128)(2,1)} fusion(f32[8192,768]{1,0:T(8,128)} %fusion.94, bf16[8192,768]{1,0:T(8,128)(2,1)} %get-tuple-element.247, bf16[1,768,768]{2,1,0:T(8,128)(2,1)S(1)} %copy-done.48), kind=kOutput, calls=%fused_computation.81 | convolution fusion | flops 9676259328 | bytes 51511296 | tf_op jit(solution)/shard_map/erf,edf->erd/dot_general | solution.py:84
  723.2 55.2 %reduce-scatter.11.cloned.1.call-done = bf16[1,2048,768]{2,1,0:T(8,128)(2,1)} async-done(((bf16[1,8192,768]{2,1,0:T(8,128)(2,1)}), bf16[1,2048,768]{2,1,0:T(8,128)(2,1)}) %reduce-scatter.11.cloned.1.call-update) | async-done | bytes 3145744 | tf_op jit(solution)/shard_map/reduce_scatter | solution.py:199
  785.8 33.3 %reduce.71 = bf16[2048,768]{1,0:T(8,128)(2,1)} reduce(bf16[2048,1,768]{2,1,0:T(2,128)(2,1)} %bitcast.241, bf16[]{:T(256)} %broadcast.4102), dimensions={1}, to_apply=%bitcast.237.reduce_sub_computation | reduce | bytes 6291458
  831.3 48.8 %reduce-scatter.13.cloned.1.call-done = bf16[1,2048,768]{2,1,0:T(8,128)(2,1)} async-done(((bf16[1,8192,768]{2,1,0:T(8,128)(2,1)}), bf16[1,2048,768]{2,1,0:T(8,128)(2,1)}) %reduce-scatter.13.cloned.1.call-update) | async-done | bytes 3145744 | tf_op jit(solution)/shard_map/reduce_scatter | solution.py:237
  887.0 33.3 %reduce.70 = bf16[2048,768]{1,0:T(8,128)(2,1)} reduce(bf16[2048,1,768]{2,1,0:T(2,128)(2,1)} %bitcast.242, bf16[]{:T(256)} %broadcast.4102), dimensions={1}, to_apply=%bitcast.236.reduce_sub_computation | reduce | bytes 6291458
  959.2 9.5 multiply_reduce_fusion.1
  971.8 31.2 %all-to-all-done.3 = bf16[8,2,98304]{2,1,0:T(2,128)(2,1)} async-done(((bf16[8,2,98304]{2,1,0:T(2,128)(2,1)}), bf16[8,2,98304]{2,1,0:T(2,128)(2,1)}, u32[]{:S(2)}, u32[]{:S(2)}) %all-to-all-start.3) | async-done | bytes 3145760 | tf_op jit(solution)/shard_map/all_to_all | solution.py:240
  1043.9 144.3 %select_reduce_fusion.18 = (bf16[12]{0:T(256)(128)(2,1)}, bf16[12]{0:T(256)(128)(2,1)}, bf16[12]{0:T(256)(128)(2,1)}, bf16[12]{0:T(256)(128)(2,1)}, bf16[12]{0:T...) fusion(pred[512,2048]{1,0:T(8,128)(4,1)} %get-tuple-element.268, ...), kind=kOutput, calls=%fused_computation.23 | convolution fusion | flops 3661635584 | bytes 120349008 | tf_op jit(solution)/shard_map/while/body/eval_jaxpr/sub | solution.py:265
  1188.2 19.2 %fusion.62 = bf16[12,64,2048]{2,1,0:T(8,128)(2,1)} fusion(bf16[512,12,64]{0,2,1:T(8,128)(2,1)S(1)} %bitcast.253, f32[12,512,2048]{2,1,0:T(8,128)} %get-tuple-element.296), kind=kOutput, calls=%fused_computation.110 | convolution fusion | flops 1637351424 | bytes 54263808 | tf_op jit(solution)/shard_map/while/body/eval_jaxpr/hqk,qhd->khd/dot_general | solution.py:271
  1208.8 22.8 %fusion.59 = bf16[12,64,2048]{2,1,0:T(8,128)(2,1)} fusion(bf16[512,12,64]{0,2,1:T(8,128)(2,1)} %bitcast.262, f32[12,512,2048]{2,1,0:T(8,128)} %get-tuple-element.291, f32[12,512]{1,0:T(8,128)S(1)} %copy-done.36, pred[512,2048]{1,0:T(8,128)(4,1)S(1)} %copy-done.13), kind=kOutput, calls=%fused_computation.109 | convolution fusion | flops 1649934336 | bytes 55336960 | tf_op jit(solution)/shard_map/while/body/eval_jaxpr/hqk,qhd->khd/dot_general | solution.py:274
  1231.7 16.5 %fusion.67 = f32[1,768,768]{2,1,0:T(8,128)} fusion(bf16[8192,768]{1,0:T(8,128)(2,1)} %get-tuple-element.249, bf16[1,8192,768]{2,1,0:T(8,128)(2,1)} %all-gather.19.cloned.1.call-done), kind=kOutput, calls=%fused_computation.156 | convolution fusion | flops 9663676416 | bytes 27525120 | tf_op jit(solution)/shard_map/erf,erd->efd/dot_general | solution.py:72
  1248.2 16.9 %fusion.70 = f32[1,768,768]{2,1,0:T(8,128)} fusion(bf16[8192,768]{1,0:T(8,128)(2,1)} %get-tuple-element.248, bf16[1,8192,768]{2,1,0:T(8,128)(2,1)} %all-gather.17.cloned.1.call-done), kind=kOutput, calls=%fused_computation.157 | convolution fusion | flops 9663676416 | bytes 27525120 | tf_op jit(solution)/shard_map/erd,erf->edf/dot_general | solution.py:79
  1265.2 13.8 fusion.73
  1282.0 20.3 %fusion.88 = bf16[12,64,512]{2,1,0:T(8,128)(2,1)} fusion(bf16[2048,12,64]{0,2,1:T(8,128)(2,1)} %bitcast.246, f32[12,512,2048]{2,1,0:T(8,128)} %get-tuple-element.296), kind=kOutput, calls=%fused_computation.180 | convolution fusion | flops 1636171776 | bytes 54263808 | tf_op jit(solution)/shard_map/while/body/eval_jaxpr/hqk,khd->qhd/dot_general | solution.py:268
  1308.0 117.5 %select_reduce_fusion = (bf16[12]{0:T(256)(128)(2,1)}, bf16[12]{0:T(256)(128)(2,1)}, bf16[12]{0:T(256)(128)(2,1)}, bf16[12]{0:T(256)(128)(2,1)}, bf16[12]{0:T(25...) fusion(f32[12,512,2048]{2,1,0:T(8,128)} %get-tuple-element.296,, ...), kind=kLoop, calls=%fused_computation.5 | loop fusion | flops 452984672 | bytes 69206448 | tf_op jit(solution)/shard_map/while/body/eval_jaxpr/reduce_sum | solution.py:30
  1436.6 11.2 all-reduce.6
  1453.6 102.1 %all-reduce.9 = (f32[192,2304]{1,0:T(8,128)}, f32[192,768]{1,0:T(8,128)}, f32[192,8]{0,1:T(8,128)}, f32[192]{0:T(256)}, f32[192]{0:T(256)}, /*index=5*/f32[3,32]{0,1:T(8,128)S(1)}) all-reduce(bf16[192,2304]{1,0:T(8,128)(2,1)} %reduce-scatter.19.cloned.1.call-done, ...), channel_id=1, replica_groups=mesh['expert'=8,'shard'=4] {'expert'}, use_global_device_ids=true, to_apply=%region_28.29 | all-reduce | flops 591840 | bytes 3552000 | tf_op jit(solution)/shard_map/psum | solution.py:338
  (238 shorter events, 206.1 us)
Async XLA Ops:
  7.2 611.1 %copy-start = (bf16[1,768,768]{2,1,0:T(8,128)(2,1)S(1)}, bf16[1,768,768]{2,1,0:T(8,128)(2,1)}, u32[]{:S(2)}) copy-start(bf16[1,768,768]{2,1,0:T(8,128)(2,1)} %param.22) | copy-start | bytes 3538948
  7.2 49.1 %copy-start.29 = (s32[512,2]{0,1:T(2,128)S(1)}, s32[512,2]{0,1:T(2,128)}, u32[]{:S(2)}) copy-start(s32[512,2]{0,1:T(2,128)} %param.23) | copy-start | bytes 12292
  7.2 49.6 %copy-start.50 = (s32[1,3]{1,0:T(1,128)S(1)}, s32[1,3]{1,0:T(1,128)}, u32[]{:S(2)}) copy-start(s32[1,3]{1,0:T(1,128)} %param.24) | copy-start | bytes 40
  7.2 35.9 %all-gather.9.cloned.1.call-start = ((), (), s32[]{:S(2)}) async-start(), calls=%async_computation.11 | async-start | bytes 4423680 | tf_op jit(solution)/shard_map/all_gather | solution.py:107
  8.0 87.5 %all-gather.13.cloned.1.call-start = ((), (), s32[]{:S(2)}) async-start(), calls=%async_computation.13 | async-start | bytes 3932160 | tf_op jit(solution)/shard_map/all_gather | solution.py:131
  48.9 267.8 %all-gather.11.cloned.1.call-start = ((), (), s32[]{:S(2)}) async-start(), calls=%async_computation.12 | async-start | bytes 3932160 | tf_op jit(solution)/shard_map/all_gather | solution.py:132
  49.7 292.9 %all-gather.15.cloned.1.call-start = ((), (), s32[]{:S(2)}) async-start(), calls=%async_computation.14 | async-start | bytes 1474560 | tf_op jit(solution)/shard_map/all_gather | solution.py:108
  50.2 488.0 %all-gather.17.cloned.1.call-start = ((), (), s32[]{:S(2)}) async-start(), calls=%async_computation.15 | async-start | bytes 15728640 | tf_op jit(solution)/shard_map/all_gather | solution.py:195
  92.4 202.2 %copy-start.9 = (pred[512,2048]{1,0:T(8,128)(4,1)}, pred[512,2048]{1,0:T(8,128)(4,1)S(1)}, u32[]{:S(2)}) copy-start(pred[512,2048]{1,0:T(8,128)(4,1)S(1)} %get-tuple-element.269) | copy-start | bytes 3145732
  92.4 202.2 %copy-start.10 = (pred[512,2048]{1,0:T(8,128)(4,1)}, pred[512,2048]{1,0:T(8,128)(4,1)S(1)}, u32[]{:S(2)}) copy-start(pred[512,2048]{1,0:T(8,128)(4,1)S(1)} %get-tuple-element.270) | copy-start | bytes 3145732
  100.2 195.1 %copy-start.11 = (pred[512,2048]{1,0:T(8,128)(4,1)S(1)}, pred[512,2048]{1,0:T(8,128)(4,1)}, u32[]{:S(2)}) copy-start(pred[512,2048]{1,0:T(8,128)(4,1)} %get-tuple-element.255) | copy-start | bytes 3145732
  342.6 95.3 %copy-start.44 = (bf16[192,8]{0,1:T(8,128)(2,1)S(1)}, bf16[192,8]{0,1:T(8,128)(2,1)}, u32[]{:S(2)}) copy-start(bf16[192,8]{0,1:T(8,128)(2,1)} %param.16) | copy-start | bytes 9220
  342.6 100.8 %copy-start.7 = (bf16[512,768]{1,0:T(8,128)(2,1)S(1)}, bf16[512,768]{1,0:T(8,128)(2,1)}, u32[]{:S(2)}) copy-start(bf16[512,768]{1,0:T(8,128)(2,1)} %param.25) | copy-start | bytes 2359300
  345.2 98.1 %copy-start.35 = (f32[512]{0:T(512)}, f32[512]{0:T(512)S(1)}, u32[]{:S(2)}) copy-start(f32[512]{0:T(512)S(1)} %add_rsqrt_fusion) | copy-start | bytes 6148
  346.5 105.2 %copy-start.5 = (bf16[512,768]{1,0:T(8,128)(2,1)}, bf16[512,768]{1,0:T(8,128)(2,1)S(1)}, u32[]{:S(2)}) copy-start(bf16[512,768]{1,0:T(8,128)(2,1)S(1)} %multiply_convert_fusion.9) | copy-start | bytes 2359300
  353.1 98.9 %copy-start.30 = (s32[512,2]{0,1:T(2,128)S(1)}, s32[512,2]{0,1:T(2,128)}, u32[]{:S(2)}) copy-start(s32[512,2]{0,1:T(2,128)} %param.23) | copy-start | bytes 12292
  437.8 180.4 %all-gather.19.cloned.1.call-start = ((), (), s32[]{:S(2)}) async-start(), calls=%async_computation.17 | async-start | bytes 15728640 | tf_op jit(solution)/shard_map/all_gather | solution.py:233
  443.4 94.5 %copy-start.24 = (bf16[768,8]{0,1:T(8,128)(2,1)}, bf16[768,8]{0,1:T(8,128)(2,1)S(1)}, u32[]{:S(2)}) copy-start(bf16[768,8]{0,1:T(8,128)(2,1)S(1)} %reshape.1047) | copy-start | bytes 36868
  453.4 104.1 %copy-start.17 = (f32[512,2]{1,0:T(8,128)}, f32[512,2]{1,0:T(8,128)S(1)}, u32[]{:S(2)}) copy-start(f32[512,2]{1,0:T(8,128)S(1)} %copy.132) | copy-start | bytes 12292
  537.9 240.5 %reduce-scatter.11.cloned.1.call-start = ((), (), s32[]{:S(2)}) async-start(), calls=%async_computation.16 | async-start | bytes 15728640 | tf_op jit(solution)/shard_map/reduce_scatter | solution.py:199
  679.2 200.9 %reduce-scatter.13.cloned.1.call-start = ((), (), s32[]{:S(2)}) async-start(), calls=%async_computation.18 | async-start | bytes 15728640 | tf_op jit(solution)/shard_map/reduce_scatter | solution.py:237
  825.5 101.2 %all-to-all-start.1 = ((bf16[8,2,98304]{2,1,0:T(2,128)(2,1)}), bf16[8,2,98304]{2,1,0:T(2,128)(2,1)}, u32[]{:S(2)}, u32[]{:S(2)}) async-start(bf16[8,2,98304]{2,1,0:T(2,128)(2,1)} %reshape.1099), calls=%async_computation.2 | async-start | bytes 6291456 | tf_op jit(solution)/shard_map/all_to_all | solution.py:202
  887.0 45.3 %copy-start.8 = (bf16[512,768]{1,0:T(8,128)(2,1)S(1)}, bf16[512,768]{1,0:T(8,128)(2,1)}, u32[]{:S(2)}) copy-start(bf16[512,768]{1,0:T(8,128)(2,1)} %param.25) | copy-start | bytes 2359300
  887.0 45.4 %copy-start.38 = (s32[1024,1]{0,1:T(1,128)S(1)}, s32[1024,1]{0,1:T(1,128)}, u32[]{:S(2)}) copy-start(s32[1024,1]{0,1:T(1,128)} %compare_select_fusion) | copy-start | bytes 12292
  926.7 76.3 %all-to-all-start.3 = ((bf16[8,2,98304]{2,1,0:T(2,128)(2,1)}), bf16[8,2,98304]{2,1,0:T(2,128)(2,1)}, u32[]{:S(2)}, u32[]{:S(2)}) async-start(bf16[8,2,98304]{2,1,0:T(2,128)(2,1)} %reshape.1097), calls=%async_computation.5 | async-start | bytes 6291456 | tf_op jit(solution)/shard_map/all_to_all | solution.py:240
  932.2 370.1 %reduce-scatter.15.cloned.1.call-start = ((), (), s32[]{:S(2)}) async-start(), calls=%async_computation.19 | async-start | bytes 3932160 | tf_op jit(solution)/shard_map/reduce_scatter | solution.py:291
  1043.8 144.3 %copy-start.19 = (bf16[512,768]{0,1:T(8,128)(2,1)}, bf16[512,768]{0,1:T(8,128)(2,1)S(1)}, u32[]{:S(2)}) copy-start(bf16[512,768]{0,1:T(8,128)(2,1)S(1)} %copy.141) | copy-start | bytes 2359300
  1043.9 144.3 %copy-start.14 = (bf16[512,768]{0,1:T(8,128)(2,1)S(1)}, bf16[512,768]{0,1:T(8,128)(2,1)}, u32[]{:S(2)}) copy-start(bf16[512,768]{0,1:T(8,128)(2,1)} %copy.129) | copy-start | bytes 2359300
  1207.4 94.9 %reduce-scatter.17.cloned.1.call-start = ((), (), s32[]{:S(2)}) async-start(), calls=%async_computation.20 | async-start | bytes 3932160 | tf_op jit(solution)/shard_map/reduce_scatter | solution.py:297
  1231.6 196.9 %reduce-scatter.23.cloned.1.call-start = ((), (), s32[]{:S(2)}) async-start(), calls=%async_computation.23 | async-start | bytes 245760
  1280.1 149.9 %reduce-scatter.21.cloned.1.call-start = ((), (), s32[]{:S(2)}) async-start(), calls=%async_computation.22 | async-start | bytes 1474560 | tf_op jit(solution)/shard_map/reduce_scatter | solution.py:322
  1282.0 171.6 %reduce-scatter.19.cloned.1.call-start = ((), (), s32[]{:S(2)}) async-start(), calls=%async_computation.21 | async-start | bytes 4423680 | tf_op jit(solution)/shard_map/reduce_scatter | solution.py:319
  (37 other events, 680.8 us)
Sparse Core Ops, SparseCore 0:
  9.6 33.4 all-gather.8
  49.0 28.5 all-gather.12
  79.8 28.5 all-gather.10
  109.7 17.4 all-gather.14
  437.9 80.2 all-gather.16
  538.0 80.2 all-gather.18
  679.3 99.0 reduce-scatter.10
  781.0 99.0 reduce-scatter.12
  1207.5 36.0 reduce-scatter.14
  1246.2 37.9 reduce-scatter.16
  1287.2 19.8 reduce-scatter.22
  1310.1 25.6 reduce-scatter.20
  1338.6 40.4 reduce-scatter.18
where the time goes:
time: 1580 us; the launch traced here: 1560 us
  matrix products  632 us (40%)
  blocking collectives  285 us (18%)
  other arithmetic  280 us (18%)
  waiting for transfers between devices  206 us (13%)
  local copies, waits for them, and re-layouts  132 us (8%)
  between operations  16.8 us (1%)
    dot_general x1, matrix products, block_scores(): jnp.einsum('qhd,khd->hqk', query_block, key_heads, preferred_element_type...  194 us
    sub x1, matrix products, attend_back(): grad_scores = probs * (grad_probs - row_delta)  144 us
    reduce_sum x1, other arithmetic, bias_gradient(): jnp.sum(jnp.where((buckets == column)[None], grad_scores, 0.0), axis=(1, 2))  118 us
    psum x1, blocking collectives, local(): lax.psum((shares[0], shares[1], shares[2], shares[3], shares[4], shares[5...  102 us
    all_to_all x1, blocking collectives, local(): lax.all_to_all(outgoing.reshape(expert_count, capacity, model_width), 'ex...  76.7 us
    all_to_all x1, blocking collectives, local(): lax.all_to_all(grad_outgoing.reshape(expert_count, capacity, model_width)...  75.9 us
    unnamed x4, other arithmetic  66.7 us
    reduce_scatter x1, waiting for transfers between devices, local(): lax.psum_scatter(down_sum.astype(jnp.bfloat16), 'shard', scatter_dimensio...  55.2 us
  transfers between devices with their start and end apart: 15, of which 5 were waited for; matrix products, arithmetic and copies ran while one was open for 48% of the time, Pallas kernels for 0%

commit v1 on v0

v1 whole, which is shorter than its diff:
```python
import functools

import jax
import jax.numpy as jnp
from jax import lax
from jax.experimental import pallas as pl
from jax.experimental.pallas import tpu as pltpu
from jax.sharding import PartitionSpec as P

norm_epsilon = 1e-06
bucket_borders = (16, 23, 32, 45, 64, 91, 128, 181, 256, 362, 512, 724, 1024, 1448, 2048, 2896)


def bucket_of(distance):
    clipped = jnp.maximum(distance, 0)
    bucket_id = jnp.minimum(clipped, 15)
    for border in bucket_borders:
        bucket_id = bucket_id + (clipped >= border).astype(jnp.int32)
    return bucket_id


tile = 256
low_score = -1e30


def toeplitz_vectors(bias_table, diagonals):
    offsets = jnp.arange(2 * tile, dtype=jnp.int32)
    offsets = jnp.where(offsets < tile, offsets, offsets - 2 * tile)
    distance = jnp.arange(diagonals, dtype=jnp.int32)[:, None] * tile + offsets[None, :]
    onehot = bucket_of(distance)[None] == jnp.arange(bias_table.shape[1])[:, None, None]
    return jnp.einsum(
        "hc,cdm->hdm", bias_table, onehot.astype(jnp.bfloat16), preferred_element_type=jnp.float32
    )


def fill_bias(vector_ref, head, bias_ref, diagonals):
    def fill(delta, carry):
        row = vector_ref[head, pl.ds(delta, 1), :]
        wide = jnp.broadcast_to(row, (tile, 2 * tile))
        rolled = pltpu.roll(wide, 0, 1, stride=1, stride_axis=0)
        bias_ref[delta] = rolled[:, :tile]
        return carry

    lax.fori_loop(0, diagonals, fill, 0)


def start_of(position, first_end, second_end):
    return jnp.where(
        position >= second_end, second_end, jnp.where(position >= first_end, first_end, 0)
    )


def contract(left, right, left_dim, right_dim):
    return lax.dot_general(
        left, right, (((left_dim,), (right_dim,)), ((), ())), preferred_element_type=jnp.float32
    )


def attend_kernel(info_ref, q_ref, k_ref, v_ref, vector_ref, out_ref, log_ref, bias_ref, side_ref):
    diagonals = vector_ref.shape[1]
    query_tiles = q_ref.shape[0] // tile
    lanes = lax.broadcasted_iota(jnp.int32, (1, 128), 1)
    for head in range(2):
        mine = (lanes < 64) if head == 0 else (lanes >= 64)
        fill_bias(vector_ref, head, bias_ref, diagonals)
        for block in range(query_tiles):
            rows = pl.ds(block * tile, tile)
            query_tile = info_ref[2] * query_tiles + block
            query = jnp.where(mine, q_ref[rows, :] * 0.125, 0).astype(jnp.bfloat16)
            first_end, second_end = info_ref[0], info_ref[1]
            first_tile = start_of(query_tile * tile, first_end, second_end) // tile
            query_pos = query_tile * tile + lax.broadcasted_iota(jnp.int32, (1, tile), 1)
            query_start = start_of(query_pos, first_end, second_end)

            def step(index, carry):
                top, total = carry
                keys = pl.ds(pl.multiple_of(index * tile, tile), tile)
                key_pos = index * tile + lax.broadcasted_iota(jnp.int32, (tile, 1), 0)
                scores = contract(k_ref[keys, :], query, 1, 1) + bias_ref[query_tile - index]
                allowed = (key_pos >= query_start) & (key_pos <= query_pos)
                scores = jnp.where(allowed, scores, low_score)
                new_top = jnp.maximum(top, jnp.max(scores, axis=0, keepdims=True))
                weights = jnp.exp(scores - new_top).astype(jnp.bfloat16)
                value = jnp.where(mine, v_ref[keys, :], 1).astype(jnp.bfloat16)
                part = contract(value, weights, 0, 0)
                return new_top, total * jnp.exp(top - new_top) + part

            top, total = lax.fori_loop(
                first_tile,
                query_tile + 1,
                step,
                (jnp.full((1, tile), low_score, jnp.float32), jnp.zeros((128, tile), jnp.float32)),
            )
            if head == 0:
                row_total = total[64:65]
                side_ref[0:64, rows] = total[0:64] / row_total
            else:
                row_total = total[0:1]
                side_ref[64:128, rows] = total[64:128] / row_total
            log_ref[0, head : head + 1, rows] = top + jnp.log(row_total)
    for block in range(query_tiles):
        rows = pl.ds(block * tile, tile)
        out_ref[rows, :] = side_ref[:, rows].T.astype(jnp.bfloat16)


def attend_back_kernel(
    info_ref,
    q_ref,
    k_ref,
    v_ref,
    g_ref,
    o_ref,
    log_ref,
    vector_ref,
    dq_ref,
    dk_ref,
    dv_ref,
    diag_ref,
    bias_ref,
    grad_bias_ref,
    dk_acc,
    dv_acc,
    dq_acc,
):
    diagonals = vector_ref.shape[1]
    query_tiles = q_ref.shape[0] // tile
    lanes = lax.broadcasted_iota(jnp.int32, (1, 128), 1)
    dk_acc[...] = jnp.zeros_like(dk_acc)
    dv_acc[...] = jnp.zeros_like(dv_acc)
    dq_acc[...] = jnp.zeros_like(dq_acc)
    for head in range(2):
        mine = (lanes < 64) if head == 0 else (lanes >= 64)
        fill_bias(vector_ref, head, bias_ref, diagonals)
        grad_bias_ref[...] = jnp.zeros_like(grad_bias_ref)
        for block in range(query_tiles):
            rows = pl.ds(block * tile, tile)
            query_tile = info_ref[2] * query_tiles + block
            query = jnp.where(mine, q_ref[rows, :] * 0.125, 0).astype(jnp.bfloat16)
            grad = jnp.where(mine, g_ref[rows, :], 0).astype(jnp.bfloat16)
            product = grad.astype(jnp.float32) * o_ref[rows, :].astype(jnp.float32)
            delta_row = jnp.sum(product.T, axis=0, keepdims=True)
            log_row = log_ref[0, head : head + 1, rows]
            first_end, second_end = info_ref[0], info_ref[1]
            first_tile = start_of(query_tile * tile, first_end, second_end) // tile
            query_pos = query_tile * tile + lax.broadcasted_iota(jnp.int32, (1, tile), 1)
            query_start = start_of(query_pos, first_end, second_end)

            def step(index, carry):
                keys = pl.ds(pl.multiple_of(index * tile, tile), tile)
                key_pos = index * tile + lax.broadcasted_iota(jnp.int32, (tile, 1), 0)
                key = k_ref[keys, :]
                scores = contract(key, query, 1, 1) + bias_ref[query_tile - index]
                allowed = (key_pos >= query_start) & (key_pos <= query_pos)
                probs = jnp.exp(jnp.where(allowed, scores - log_row, low_score))
                grad_probs = contract(v_ref[keys, :], grad, 1, 1)
                grad_scores = probs * (grad_probs - delta_row)
                grad_bias_ref[query_tile - index] += grad_scores
                low = grad_scores.astype(jnp.bfloat16)
                dv_acc[keys, :] += contract(probs.astype(jnp.bfloat16), grad, 1, 0)
                dk_acc[keys, :] += contract(low, query, 1, 0)
                key_mine = jnp.where(mine, key, 0).astype(jnp.bfloat16)
                dq_acc[rows, :] += contract(low, key_mine, 0, 0)
                return carry

            lax.fori_loop(first_tile, query_tile + 1, step, 0)

        def reduce(delta, carry):
            value = grad_bias_ref[delta]
            value = jnp.concatenate([value, jnp.zeros_like(value)], axis=1)
            half = tile // 2
            while half >= 8:
                value = value[:half] + pltpu.roll(value[half:], 2 * tile - half, 1)
                half //= 2
            diag_ref[head, delta] = value
            return carry

        lax.fori_loop(0, diagonals, reduce, 0)
    dq_ref[...] = (dq_acc[...] * 0.125).astype(jnp.bfloat16)
    dk_ref[...] = dk_acc[...].astype(jnp.bfloat16)
    dv_ref[...] = dv_acc[...].astype(jnp.bfloat16)


def head_specs(tok_count, group_tok, model_width):
    pairs = model_width // 128
    return (
        pl.BlockSpec(memory_space=pltpu.SMEM),
        pl.BlockSpec((tok_count, 128), lambda p: (0, p)),
        pl.BlockSpec((group_tok, 128), lambda p: (0, p)),
        pl.BlockSpec((group_tok, 128), lambda p: (0, p + pairs)),
    )


def attend(info, qkv, kv, vectors):
    tok_count, group_tok, model_width = qkv.shape[0], kv.shape[0], kv.shape[1] // 2
    pairs, diagonals = model_width // 128, vectors.shape[1]
    cost = 4 * tok_count * group_tok * model_width
    return pl.pallas_call(
        attend_kernel,
        grid=(pairs,),
        in_specs=[
            *head_specs(tok_count, group_tok, model_width),
            pl.BlockSpec((2, diagonals, 2 * tile), lambda p: (p, 0, 0)),
        ],
        out_specs=[
            pl.BlockSpec((tok_count, 128), lambda p: (0, p)),
            pl.BlockSpec((1, 2, tok_count), lambda p: (p, 0, 0)),
        ],
        out_shape=[
            jax.ShapeDtypeStruct((tok_count, model_width), jnp.bfloat16),
            jax.ShapeDtypeStruct((pairs, 2, tok_count), jnp.float32),
        ],
        scratch_shapes=[
            pltpu.VMEM((diagonals, tile, tile), jnp.float32),
            pltpu.VMEM((128, tok_count), jnp.float32),
        ],
        compiler_params=pltpu.CompilerParams(vmem_limit_bytes=40 * 2**20),
        cost_estimate=pl.CostEstimate(
            flops=16 * cost, bytes_accessed=4 * group_tok * model_width, transcendentals=0
        ),
        name="attend",
    )(info, qkv, kv, kv, vectors)


def attend_back(info, qkv, kv, grad, attended, logs, vectors):
    tok_count, group_tok, model_width = qkv.shape[0], kv.shape[0], kv.shape[1] // 2
    pairs, diagonals = model_width // 128, vectors.shape[1]
    cost = 10 * tok_count * group_tok * model_width
    query_spec = pl.BlockSpec((tok_count, 128), lambda p: (0, p))
    key_spec = pl.BlockSpec((group_tok, 128), lambda p: (0, p))
    return pl.pallas_call(
        attend_back_kernel,
        grid=(pairs,),
        in_specs=[
            *head_specs(tok_count, group_tok, model_width),
            query_spec,
            query_spec,
            pl.BlockSpec((1, 2, tok_count), lambda p: (p, 0, 0)),
            pl.BlockSpec((2, diagonals, 2 * tile), lambda p: (p, 0, 0)),
        ],
        out_specs=[
            query_spec,
            key_spec,
            key_spec,
            pl.BlockSpec((2, diagonals, 8, 2 * tile), lambda p: (p, 0, 0, 0)),
        ],
        out_shape=[
            jax.ShapeDtypeStruct((tok_count, model_width), jnp.bfloat16),
            jax.ShapeDtypeStruct((group_tok, model_width), jnp.bfloat16),
            jax.ShapeDtypeStruct((group_tok, model_width), jnp.bfloat16),
            jax.ShapeDtypeStruct((2 * pairs, diagonals, 8, 2 * tile), jnp.float32),
        ],
        scratch_shapes=[
            pltpu.VMEM((diagonals, tile, tile), jnp.float32),
            pltpu.VMEM((diagonals, tile, tile), jnp.float32),
            pltpu.VMEM((group_tok, 128), jnp.float32),
            pltpu.VMEM((group_tok, 128), jnp.float32),
            pltpu.VMEM((tok_count, 128), jnp.float32),
        ],
        compiler_params=pltpu.CompilerParams(vmem_limit_bytes=48 * 2**20),
        cost_estimate=pl.CostEstimate(
            flops=10 * cost, bytes_accessed=8 * group_tok * model_width, transcendentals=0
        ),
        name="attend_back",
    )(info, qkv, kv, kv, grad, attended, logs, vectors)


def table_gradient(diag, bucket_count):
    head_count, diagonals, fold, width = diag.shape
    offsets = jnp.arange(width, dtype=jnp.int32)
    offsets = jnp.where(offsets < tile, offsets, offsets - width)
    distance = (
        jnp.arange(diagonals, dtype=jnp.int32)[:, None, None] * tile
        + offsets[None, None, :]
        - jnp.arange(fold, dtype=jnp.int32)[None, :, None]
    )
    onehot = bucket_of(distance)[None] == jnp.arange(bucket_count)[:, None, None, None]
    return jnp.einsum(
        "hdrc,bdrc->hb",
        diag,
        onehot.astype(jnp.float32),
        precision=lax.Precision.HIGHEST,
        preferred_element_type=jnp.float32,
    )


def partner(value, flip):
    count = lax.axis_size("shard")
    return lax.ppermute(value, "shard", [(i, i ^ flip) for i in range(count)])


def gather_pieces(value):
    across = partner(value, 2)
    return [value, partner(value, 1), across, partner(across, 1)]


def reduce_pieces(pieces):
    low = [p.astype(jnp.bfloat16) for p in pieces]
    far = (pieces[2] + partner(low[3], 1).astype(jnp.float32)).astype(jnp.bfloat16)
    near = pieces[0] + partner(low[1], 1).astype(jnp.float32)
    return near + partner(far, 2).astype(jnp.float32)


def reduce_rows(value, shard_index):
    count = lax.axis_size("shard")
    split = value.reshape(count, value.shape[0] // count, *value.shape[1:])
    return reduce_pieces(
        [
            lax.dynamic_index_in_dim(split, shard_index ^ r, 0, keepdims=False).astype(jnp.float32)
            for r in range(count)
        ]
    )


def dot32(left, right, spec):
    return jnp.einsum(spec, left, right, preferred_element_type=jnp.float32)


def norm_forward(values):
    inverse = lax.rsqrt(jnp.mean(values * values, axis=-1, keepdims=True) + norm_epsilon)
    return (values * inverse, inverse)


def norm_backward(grad_normed, normalized, inverse, gain_vector):
    grad_gain = jnp.sum(grad_normed * normalized, axis=0)
    scaled = grad_normed * gain_vector
    grad_values = inverse * (
        scaled - normalized * jnp.mean(scaled * normalized, axis=-1, keepdims=True)
    )
    return (grad_values, grad_gain)


def gated_unit(gate_value, up_value):
    return jax.nn.gelu(gate_value) * up_value


def local(
    tokens,
    w_qkv,
    w_out,
    router,
    gain_attn,
    gain_ffn,
    rel_bias,
    w_gate,
    w_up,
    w_down,
    routes,
    lengths,
    cotangent,
):
    shard_index = lax.axis_index("shard")
    full_qkv, full_out, full_router, full_gain_attn, full_gain_ffn, full_table = (
        lax.all_gather(w_qkv, "shard", axis=0, tiled=True),
        lax.all_gather(w_out, "shard", axis=0, tiled=True),
        lax.all_gather(router, "shard", axis=0, tiled=True),
        lax.all_gather(gain_attn, "shard", axis=0, tiled=True),
        lax.all_gather(gain_ffn, "shard", axis=0, tiled=True),
        lax.all_gather(rel_bias, "shard", axis=0, tiled=True),
    )
    tok_count, model_width = tokens.shape
    head_count, bucket_count = full_table.shape
    expert_count = full_router.shape[1]
    route_count = routes.shape[1]
    capacity = 2 * route_count * tok_count // expert_count
    inputs = tokens.astype(jnp.float32)
    attn_gain = full_gain_attn.astype(jnp.float32)
    ffn_gain = full_gain_ffn.astype(jnp.float32)
    normed_one, inverse_one = norm_forward(inputs)
    normed_attn = (normed_one * attn_gain).astype(jnp.bfloat16)
    qkv = jnp.dot(normed_attn, full_qkv, preferred_element_type=jnp.float32).astype(jnp.bfloat16)
    kv = lax.all_gather(qkv[:, model_width:], "shard", axis=0, tiled=True)
    group_tok = kv.shape[0]
    info = jnp.stack([lengths[0, 0], lengths[0, 0] + lengths[0, 1], shard_index]).astype(jnp.int32)
    vectors = toeplitz_vectors(full_table, group_tok // tile)
    weights_in, kv = lax.optimization_barrier(((w_gate[0], w_up[0], w_down[0]), kv))
    gate_pieces, up_pieces, down_pieces = (gather_pieces(w) for w in weights_in)
    attended, logs = attend(info, qkv, kv, vectors)
    hidden_one = inputs + jnp.dot(attended, full_out, preferred_element_type=jnp.float32)
    normed_two, inverse_two = norm_forward(hidden_one)
    normed_ffn = (normed_two * ffn_gain).astype(jnp.bfloat16)
    logits = jnp.dot(normed_ffn, full_router, preferred_element_type=jnp.float32)
    expert_ids = jnp.arange(expert_count, dtype=jnp.int32)
    chosen_mask = routes[:, :, None] == expert_ids[None, None, :]
    chosen = jnp.sum(jnp.where(chosen_mask, logits[:, None, :], 0.0), axis=2)
    gate_weights = jax.nn.softmax(chosen, axis=1)
    flat_routes = routes.reshape(-1)
    onehot_rows = (flat_routes[:, None] == expert_ids[None, :]).astype(jnp.int32)
    earlier = jnp.cumsum(onehot_rows, axis=0) - onehot_rows
    position = jnp.sum(earlier * onehot_rows, axis=1)
    slot_index = flat_routes * capacity + position
    slot_pair = slot_index.reshape(tok_count, route_count)
    slots = jnp.arange(expert_count * capacity, dtype=jnp.int32)
    pick = [(slot_pair[:, k][:, None] == slots[None, :]) for k in range(route_count)]
    pick_any = functools.reduce(jnp.logical_or, pick).astype(jnp.bfloat16)

    def dispatch(rows):
        packed = dot32(pick_any, rows, "ts,td->sd").astype(jnp.bfloat16)
        return lax.all_to_all(
            packed.reshape(expert_count, capacity, model_width),
            "expert",
            split_axis=0,
            concat_axis=0,
            tiled=True,
        ).reshape(expert_count * capacity, model_width)

    def give_back(rows):
        return lax.all_to_all(
            rows.reshape(expert_count, capacity, model_width),
            "expert",
            split_axis=0,
            concat_axis=0,
            tiled=True,
        ).reshape(expert_count * capacity, model_width)

    slot_gates = functools.reduce(
        jnp.add,
        [jnp.sum(jnp.where(pick[k], gate_weights[:, k][:, None], 0.0), axis=0) for k in range(2)],
    )
    slot_gates = lax.all_to_all(
        slot_gates.reshape(expert_count, capacity), "expert", 0, 0, tiled=True
    ).reshape(-1)
    cotangent_rows = dispatch(cotangent)
    rows_in = dispatch(normed_ffn)
    grad_rows_out = (slot_gates[:, None] * cotangent_rows.astype(jnp.float32)).astype(jnp.bfloat16)
    gate_proj = [dot32(rows_in, w, "rd,df->rf") for w in gate_pieces]
    up_proj = [dot32(rows_in, w, "rd,df->rf") for w in up_pieces]
    hidden = [gated_unit(a, b).astype(jnp.bfloat16) for a, b in zip(gate_proj, up_proj)]
    down_sum = sum(dot32(x, w, "rf,fd->rd") for x, w in zip(hidden, down_pieces))
    returned = give_back(down_sum.astype(jnp.bfloat16))
    routed_out = jnp.stack(
        [dot32(p.astype(jnp.bfloat16), returned, "ts,sd->td") for p in pick], axis=1
    )
    mixed_out = hidden_one + jnp.sum(gate_weights[:, :, None] * routed_out, axis=1)
    output = mixed_out.astype(jnp.bfloat16)
    grad_mixed = cotangent.astype(jnp.float32)
    grad_gate_weights = jnp.sum(grad_mixed[:, None, :] * routed_out, axis=2)
    grad_chosen = gate_weights * (
        grad_gate_weights - jnp.sum(gate_weights * grad_gate_weights, axis=1, keepdims=True)
    )
    grad_logits = jnp.sum(jnp.where(chosen_mask, grad_chosen[:, :, None], 0.0), axis=1).astype(
        jnp.bfloat16
    )
    grad_router_full = jnp.einsum(
        "td,te->de", normed_ffn, grad_logits, preferred_element_type=jnp.float32
    )
    grad_normed_ffn = jnp.einsum(
        "te,de->td", grad_logits, full_router, preferred_element_type=jnp.float32
    )
    gate_low, up_low, grad_input = [], [], 0.0
    for r in range(len(hidden)):
        grad_hid = dot32(grad_rows_out, down_pieces[r], "rd,fd->rf")
        unused, pullback = jax.vjp(gated_unit, gate_proj[r], up_proj[r])
        grad_gate_f, grad_up_f = pullback(grad_hid)
        gate_low.append(grad_gate_f.astype(jnp.bfloat16))
        up_low.append(grad_up_f.astype(jnp.bfloat16))
        grad_input = grad_input + dot32(gate_low[r], gate_pieces[r], "rf,df->rd")
        grad_input = grad_input + dot32(up_low[r], up_pieces[r], "rf,df->rd")
    grad_back = give_back(grad_input.astype(jnp.bfloat16))
    grad_gate_w = reduce_pieces([dot32(rows_in, x, "rd,rf->df") for x in gate_low])[None]
    grad_up_w = reduce_pieces([dot32(rows_in, x, "rd,rf->df") for x in up_low])[None]
    grad_down_w = reduce_pieces([dot32(x, grad_rows_out, "rf,rd->fd") for x in hidden])[None]
    grad_normed_ffn = grad_normed_ffn + dot32(pick_any, grad_back, "ts,sd->td")
    grad_two, grad_gain_ffn_full = norm_backward(grad_normed_ffn, normed_two, inverse_two, ffn_gain)
    grad_hidden_one = grad_mixed + grad_two
    grad_attn_low = grad_hidden_one.astype(jnp.bfloat16)
    grad_out_full = jnp.einsum(
        "td,te->de", attended, grad_attn_low, preferred_element_type=jnp.float32
    )
    grad_attended = jnp.einsum(
        "te,de->td", grad_attn_low, full_out, preferred_element_type=jnp.float32
    ).astype(jnp.bfloat16)
    early = (
        reduce_rows(grad_out_full, shard_index).astype(jnp.bfloat16),
        lax.psum_scatter(
            grad_router_full.astype(jnp.bfloat16), "shard", scatter_dimension=0, tiled=True
        ),
        lax.psum_scatter(
            grad_gain_ffn_full.astype(jnp.bfloat16), "shard", scatter_dimension=0, tiled=True
        ),
    )
    early = lax.psum(early, "expert")
    grad_query, grad_keys, grad_values, diag = attend_back(
        info, qkv, kv, grad_attended, attended, logs, vectors
    )
    grad_table_full = table_gradient(diag, bucket_count)
    grad_kv_local = reduce_rows(jnp.concatenate([grad_keys, grad_values], axis=1), shard_index)
    grad_qkv_cols = jnp.concatenate([grad_query, grad_kv_local.astype(jnp.bfloat16)], axis=1)
    grad_qkv_full = jnp.einsum(
        "td,te->de", normed_attn, grad_qkv_cols, preferred_element_type=jnp.float32
    )
    grad_normed_attn = jnp.einsum(
        "te,de->td", grad_qkv_cols, full_qkv, preferred_element_type=jnp.float32
    )
    grad_one, grad_gain_attn_full = norm_backward(
        grad_normed_attn, normed_one, inverse_one, attn_gain
    )
    grad_tokens = grad_hidden_one + grad_one
    late = (
        reduce_rows(grad_qkv_full, shard_index).astype(jnp.bfloat16),
        lax.psum_scatter(
            grad_gain_attn_full.astype(jnp.bfloat16), "shard", scatter_dimension=0, tiled=True
        ),
        lax.psum_scatter(
            grad_table_full.astype(jnp.bfloat16), "shard", scatter_dimension=0, tiled=True
        ),
    )
    late = lax.psum(late, "expert")
    pieces = [x.astype(jnp.float32) for x in (late[0], *early[:2], late[1], early[2], late[2])]
    return (
        output,
        grad_tokens,
        pieces[0],
        pieces[1],
        pieces[2],
        pieces[3],
        pieces[4],
        pieces[5],
        grad_gate_w,
        grad_up_w,
        grad_down_w,
    )


def solution(mesh):
    in_specs = (
        P(("expert", "shard"), None),
        P("shard", None),
        P("shard", None),
        P("shard", None),
        P("shard"),
        P("shard"),
        P("shard", None),
        P("expert", None, "shard"),
        P("expert", None, "shard"),
        P("expert", "shard", None),
        P(("expert", "shard"), None),
        P("expert", None),
        P(("expert", "shard"), None),
    )
    out_specs = (
        P(("expert", "shard"), None),
        P(("expert", "shard"), None),
        P("shard", None),
        P("shard", None),
        P("shard", None),
        P("shard"),
        P("shard"),
        P("shard", None),
        P("expert", None, "shard"),
        P("expert", None, "shard"),
        P("expert", "shard", None),
    )
    return jax.shard_map(local, mesh=mesh, in_specs=in_specs, out_specs=out_specs, check_vma=False)
```

time: 1580 us -> 958 us (0.61)
  matrix products: 632 us -> 274 us
  blocking collectives: 285 us -> 43.2 us
  other arithmetic: 280 us -> 40.1 us
  starting transfers between devices: 12.1 us -> 207 us
  local copies, waits for them, and re-layouts: 132 us -> 19.4 us
  Pallas kernels: 0 us -> 98.7 us
  waiting for transfers between devices: 206 us -> 245 us
    dot_general x14 -> x43, matrix products: 462 us -> 256 us  [the longest x41 253 us: dot32(): return jnp.einsum(spec, left, right, preferred_element_type=jnp.float32)]
    ppermute x0 -> x27, starting transfers between devices: none -> 181 us  [partner(): return lax.ppermute(value, 'shard', [(i, i ^ flip) for i in range(count)])]
    all_to_all x2 -> x0, blocking collectives: 153 us -> none  [the longest x1 76.7 us: local(): lax.all_to_all(outgoing.reshape(expert_count, capacity, model_width), 'ex...]
    reduce_sum x5 -> x1, other arithmetic: 146 us -> 1.39 us  [local(): jnp.sum(jnp.where(pick[k], gate_weights[:, k][:, None], 0.0), axis=0)]
    sub x1 -> x0, matrix products: 144 us -> none  [attend_back(): grad_scores = probs * (grad_probs - row_delta)]
    ppermute x0 -> x27, waiting for transfers between devices: none -> 112 us  [partner(): return lax.ppermute(value, 'shard', [(i, i ^ flip) for i in range(count)])]
    reduce_scatter x6 -> x0, waiting for transfers between devices: 104 us -> none  [the longest x1 55.2 us: local(): lax.psum_scatter(down_sum.astype(jnp.bfloat16), 'shard', scatter_dimensio...]
    pallas_call x0 -> x2, Pallas kernels: none -> 98.7 us  [the longest x1 67 us: attend_back(): pl.pallas_call(attend_back_kernel, grid=(pairs,), in_specs=[*head_specs(t...]
  transfers between devices with their start and end apart: 15 -> 37, of which waited for: 5 -> 15; matrix products, arithmetic and copies ran while one was open for 48% -> 31% of each run, Pallas kernels for 0% -> 10%
where the time goes in v1:
time: 958 us; the launch traced here: 945 us
  matrix products  274 us (29%)
  waiting for transfers between devices  245 us (26%)
  starting transfers between devices  207 us (22%)
  Pallas kernels  98.7 us (10%)
  blocking collectives  43.2 us (5%)
  other arithmetic  40.1 us (4%)
  local copies, waits for them, and re-layouts  19.4 us (2%)
  between operations  18.4 us (2%)
    dot_general x41, matrix products, dot32(): return jnp.einsum(spec, left, right, preferred_element_type=jnp.float32)  253 us
    ppermute x27, starting transfers between devices, partner(): return lax.ppermute(value, 'shard', [(i, i ^ flip) for i in range(count)])  181 us
    ppermute x27, waiting for transfers between devices, partner(): return lax.ppermute(value, 'shard', [(i, i ^ flip) for i in range(count)])  112 us
    pallas_call x1, Pallas kernels, attend_back(): pl.pallas_call(attend_back_kernel, grid=(pairs,), in_specs=[*head_specs(t...  67 us
    psum x1, waiting for transfers between devices, local(): late = lax.psum(late, 'expert')  42.8 us
    all_to_all x2, waiting for transfers between devices, give_back(): lax.all_to_all(rows.reshape(expert_count, capacity, model_width), 'expert...  32.9 us
    pallas_call x1, Pallas kernels, attend(): pl.pallas_call(attend_kernel, grid=(pairs,), in_specs=[*head_specs(tok_co...  31.8 us
    all_gather x1, waiting for transfers between devices, local(): lax.all_gather(w_qkv, 'shard', axis=0, tiled=True)  21.6 us
  transfers between devices with their start and end apart: 37, of which 15 were waited for; matrix products, arithmetic and copies ran while one was open for 31% of the time, Pallas kernels for 10%

profile of v1, /device:TPU:0, one launch (start us, length us, event | category | flops | bytes accessed | tf_op | source)
XLA Modules:
  0.0 945.3 jit_solution(3447873691358940318)
XLA Ops:
  11.6 8.3 all-reduce.8
  21.4 21.6 %all-gather.6.cloned.1.call-done = bf16[768,2304]{1,0:T(8,128)(2,1)} async-done(((bf16[192,2304]{1,0:T(8,128)(2,1)}), bf16[768,2304]{1,0:T(8,128)(2,1)}) %all-gather.6.cloned.1.call-update) | async-done | bytes 3538960 | tf_op jit(solution)/shard_map/all_gather | solution.py:353
  80.5 14.9 %all-gather.8.cloned.1.call-done.k_ref.v_ref = bf16[2048,1536]{1,0:T(8,128)(2,1)} async-done(((bf16[512,1536]{1,0:T(8,128)(2,1)}), bf16[2048,1536]{1,0:T(8,128)(2,1)}) %all-gather.8.cloned.1.call-update) | async-done | bytes 6291472 | tf_op jit(solution)/shard_map/all_gather | solution.py:371
  98.2 31.8 %attend.1 = (bf16[512,768]{1,0:T(8,128)(2,1)S(1)}, f32[6,2,512]{2,1,0:T(2,128)S(1)}) custom-call(s32[3]{0:T(128)S(1)} %pad_add_fusion.info_ref, bf16[512,2304]{1,0:T(8,128)(2,1)S(1)} %convolution_convert_fusion.q_ref, bf16[2048,1536]{1,0:T(8,128)(2,1)S(1)} %copy-done.1, bf16[2048,1536]{1,0:T(8,128)(2,1)S(1)} %copy-done.1, f32[12,8,512]{2,1,0:T(8,128)S(1)} %bitcast.198), custom_call_target="tpu_custom_call" | custom-call | flops 51539607552 | bytes 6291456 | tf_op jit(solution)/shard_map/attend/pallas_call | solution.py:197
  152.9 42.2 %collective-permute-start.5 = (bf16[768,768]{1,0:T(8,128)(2,1)}, bf16[768,768]{1,0:T(8,128)(2,1)}, u32[]{:S(2)}, u32[]{:S(2)}) collective-permute-start(bf16[768,768]{1,0:T(8,128)(2,1)} %bitcast.6), channel_id=1, source_target_pairs={{0,2},{1,3},{2,0},{3,1},{4,6},{5,7},{6,4},{7,5},{8,10},{9,11},{10,... | collective-permute-start | bytes 3538952 | tf_op jit(solution)/shard_map/ppermute | solution.py:288
  198.5 21.4 %collective-permute-start.2 = (bf16[768,768]{1,0:T(8,128)(2,1)}, bf16[768,768]{1,0:T(8,128)(2,1)S(1)}, u32[]{:S(2)}, u32[]{:S(2)}) collective-permute-start(bf16[768,768]{1,0:T(8,128)(2,1)} %bitcast.6), channel_id=1, source_target_pairs={{0,1},{1,0},{2,3},{3,2},{4,5},{5,4},{6,7},{7,6},{8,9},{9,8},{10,11... | collective-permute-start | bytes 3538952 | tf_op jit(solution)/shard_map/ppermute | solution.py:288
  224.4 13.6 %collective-permute-start.8 = (bf16[768,768]{1,0:T(8,128)(2,1)}, bf16[768,768]{1,0:T(8,128)(2,1)S(1)}, u32[]{:S(2)}, u32[]{:S(2)}) collective-permute-start(bf16[768,768]{1,0:T(8,128)(2,1)} %collective-permute-done.5), channel_id=1, source_target_pairs={{0,1},{1,0},{2,3},{3,2},{4,5},{5,4},{6,7},{7,6},{8,9},{9,8},{10,11... | collective-permute-start | bytes 3538952 | tf_op jit(solution)/shard_map/ppermute | solution.py:288
  249.1 14.2 %collective-permute-start = (bf16[768,768]{1,0:T(8,128)(2,1)}, bf16[768,768]{1,0:T(8,128)(2,1)}, u32[]{:S(2)}, u32[]{:S(2)}) collective-permute-start(bf16[768,768]{1,0:T(8,128)(2,1)} %bitcast.4), channel_id=1, source_target_pairs={{0,1},{1,0},{2,3},{3,2},{4,5},{5,4},{6,7},{7,6},{8,9},{9,8},{10,11... | collective-permute-start | bytes 3538952 | tf_op jit(solution)/shard_map/ppermute | solution.py:288
  263.3 11.1 %collective-permute-done.3 = bf16[768,768]{1,0:T(8,128)(2,1)} collective-permute-done((bf16[768,768]{1,0:T(8,128)(2,1)}, bf16[768,768]{1,0:T(8,128)(2,1)}, u32[]{:S(2)}, u32[]{:S(2)}) %collective-permute-start.3) | collective-permute-done | bytes 1179680 | tf_op jit(solution)/shard_map/ppermute | solution.py:288
  274.4 6.5 collective-permute-start.7
  295.1 7.7 fusion.121
  302.8 10.5 %multiply_convert_fusion.3 = (bf16[2048,768]{1,0:T(8,128)(2,1)}, bf16[2048,768]{1,0:T(8,128)(2,1)}, bf16[2048,768]{1,0:T(8,128)(2,1)S(1)}) fusion(f32[2048,768]{1,0:T(8,128)S(1)} %fusion.120, f32[2048,768]{1,0:T(8,128)} %fusion.121, bf16[2048,768]{1,0:T(8,128)(2,1)S(1)} %copy-done.17, bf16[768,768]{1,0:T(8,128)(2,1)} %bitcast.6), kind=kOutput, calls=%fused_computation.43 | convolution fusion | flops 2456813568 | bytes 26345472 | tf_op jit(solution)/shard_map/rd,fd->rf/dot_general | solution.py:315
  319.3 11.6 %fusion.20 = (bf16[2048,768]{1,0:T(8,128)(2,1)}, bf16[2048,768]{1,0:T(8,128)(2,1)}, bf16[2048,768]{1,0:T(8,128)(2,1)}) fusion(f32[2048,768]{1,0:T(8,128)} %fusion.133, f32[2048,768]{1,0:T(8,128)S(1)} %fusion.125, bf16[2048,768]{1,0:T(8,128)(2,1)} %bitcast.14, bf16[768,768]{1,0:T(8,128)(2,1)} %collective-permute-done.3), kind=kOutput, calls=%fused_computation.28 | convolution fusion | flops 2456813568 | bytes 26345472 | tf_op jit(solution)/shard_map/rd,df->rf/dot_general | solution.py:315
  334.9 7.2 fusion.127
  347.0 11.8 %fusion.13 = (bf16[2048,768]{1,0:T(8,128)(2,1)}, bf16[2048,768]{1,0:T(8,128)(2,1)}, bf16[2048,768]{1,0:T(8,128)(2,1)S(1)}) fusion(f32[2048,768]{1,0:T(8,128)} %fusion.130, f32[2048,768]{1,0:T(8,128)S(1)} %fusion.123, bf16[2048,768]{1,0:T(8,128)(2,1)} %bitcast.14, bf16[768,768]{1,0:T(8,128)(2,1)} %collective-permute-done), kind=kOutput, calls=%fused_computation.21 | convolution fusion | flops 2456813568 | bytes 26345472 | tf_op jit(solution)/shard_map/rd,df->rf/dot_general | solution.py:315
  365.8 13.5 %fusion.27 = (bf16[2048,768]{1,0:T(8,128)(2,1)}, bf16[2048,768]{1,0:T(8,128)(2,1)}, bf16[2048,768]{1,0:T(8,128)(2,1)}) fusion(f32[2048,768]{1,0:T(8,128)} %fusion.136, f32[2048,768]{1,0:T(8,128)} %fusion.127, bf16[2048,768]{1,0:T(8,128)(2,1)} %bitcast.14, bf16[768,768]{1,0:T(8,128)(2,1)} %collective-permute-done.6), kind=kOutput, calls=%fused_computation.35 | convolution fusion | flops 2456813568 | bytes 26345472 | tf_op jit(solution)/shard_map/rd,df->rf/dot_general | solution.py:315
  379.3 6.9 add_convert_fusion.1
  392.2 7.6 fusion.128
  439.5 18.1 %add_convert_fusion = bf16[2048,768]{1,0:T(8,128)(2,1)} fusion(f32[2048,768]{1,0:T(8,128)} %fusion.137, f32[2048,768]{1,0:T(8,128)} %fusion.135, f32[2048,768]{1,0:T(8,128)} %fusion.134, f32[2048,768]{1,0:T(8,128)} %fusion.132, f32[2048,768]{1,0:T(8,128)} %fusion.131, f32[2048,768]{1,0:T(8,128)} %fusion.128, f32[2048,768]{1,0:T(8,128)} %fusion.129, ...), kind=kOutput, calls=%fused_computation.39 | convolution fusion | flops 2428502016 | bytes 51511296 | tf_op jit(solution)/shard_map/rf,df->rd/dot_general | solution.py:315
  468.5 6.7 convolution_convert_fusion.4
  511.6 26.9 %all-to-all-done.4 = bf16[8,256,768]{2,1,0:T(8,128)(2,1)} async-done(((bf16[8,256,768]{2,1,0:T(8,128)(2,1)}), bf16[8,256,768]{2,1,0:T(8,128)(2,1)}, u32[]{:S(2)}, u32[]{:S(2)}) %all-to-all-start.4) | async-done | bytes 3145760 | tf_op jit(solution)/shard_map/all_to_all | solution.py:407
  546.2 67.0 %attend_back.1 = (bf16[512,768]{1,0:T(8,128)(2,1)S(1)}, bf16[2048,768]{1,0:T(8,128)(2,1)}, bf16[2048,768]{1,0:T(8,128)(2,1)}, f32[12,8,8,512]{3,2,1,0:T(8,128)S(1)}) custom-call(s32[3]{0:T(128)S(1)} %pad_add_fusion.info_ref, bf16[512,2304]{1,0:T(8,128)(2,1)} %copy-done, bf16[2048,1536]{1,0:T(8,128)(2,1)} %all-gather.8.cloned.1.call-done.k_ref.v_ref, ...), custom_call_target="tpu_custom_call" | custom-call | flops 80530636800 | bytes 12582912 | tf_op jit(solution)/shard_map/attend_back/pallas_call | solution.py:230
  616.8 22.5 %collective-permute-start.10 = (bf16[512,1536]{1,0:T(8,128)(2,1)S(1)}, bf16[512,1536]{1,0:T(8,128)(2,1)S(1)}, u32[]{:S(2)}, u32[]{:S(2)}) collective-permute-start(bf16[512,1536]{1,0:T(8,128)(2,1)S(1)} %get-tuple-element.63), channel_id=1, source_target_pairs={{0,1},{1,0},{2,3},{3,2},{4,5},{5,4},{6,7},{7,6},{8,9},{9,8},{10,11... | collective-permute-start | bytes 4718600 | tf_op jit(solution)/shard_map/ppermute | solution.py:288
  655.5 49.8 %collective-permute-start.26 = (bf16[768,768]{1,0:T(8,128)(2,1)S(1)}, bf16[768,768]{1,0:T(8,128)(2,1)S(1)}, u32[]{:S(2)}, u32[]{:S(2)}) collective-permute-start(bf16[768,768]{1,0:T(8,128)(2,1)S(1)} %add_convert_fusion.2), channel_id=1, source_target_pairs={{0,2},{1,3},{2,0},{3,1},{4,6},{5,7},{6,4},{7,5},{8,10},{9,11},{10,... | collective-permute-start | bytes 3538952 | tf_op jit(solution)/shard_map/ppermute | solution.py:288
  717.0 15.1 %collective-permute-done.26 = bf16[768,768]{1,0:T(8,128)(2,1)S(1)} collective-permute-done((bf16[768,768]{1,0:T(8,128)(2,1)S(1)}, bf16[768,768]{1,0:T(8,128)(2,1)S(1)}, u32[]{:S(2)}, u32[]{:S(2)}) %collective-permute-start.26) | collective-permute-done | bytes 1179680 | tf_op jit(solution)/shard_map/ppermute | solution.py:288
  736.0 29.8 %collective-permute-done.11 = bf16[512,1536]{1,0:T(8,128)(2,1)S(1)} collective-permute-done((bf16[512,1536]{1,0:T(8,128)(2,1)S(1)}, bf16[512,1536]{1,0:T(8,128)(2,1)S(1)}, u32[]{:S(2)}, u32[]{:S(2)}) %collective-permute-start.11) | collective-permute-done | bytes 1572896 | tf_op jit(solution)/shard_map/ppermute | solution.py:288
  769.8 21.3 %collective-permute-done.23 = bf16[768,768]{1,0:T(8,128)(2,1)S(1)} collective-permute-done((bf16[768,768]{1,0:T(8,128)(2,1)S(1)}, bf16[768,768]{1,0:T(8,128)(2,1)S(1)}, u32[]{:S(2)}, u32[]{:S(2)}) %collective-permute-start.23) | collective-permute-done | bytes 1179680 | tf_op jit(solution)/shard_map/ppermute | solution.py:288
  792.8 23.3 %collective-permute-done.20 = bf16[768,768]{1,0:T(8,128)(2,1)S(1)} collective-permute-done((bf16[768,768]{1,0:T(8,128)(2,1)S(1)}, bf16[768,768]{1,0:T(8,128)(2,1)S(1)}, u32[]{:S(2)}, u32[]{:S(2)}) %collective-permute-start.20) | collective-permute-done | bytes 1179680 | tf_op jit(solution)/shard_map/ppermute | solution.py:288
  827.3 16.0 %reduce-scatter.4.cloned.1.call-done = bf16[192,8]{1,0:T(8,128)(2,1)} async-done(((bf16[768,8]{1,0:T(8,128)(2,1)}), bf16[192,8]{1,0:T(8,128)(2,1)}) %reduce-scatter.4.cloned.1.call-update) | async-done | bytes 3088
  861.4 7.2 all-reduce.7
  868.7 17.4 %all-reduce.5 = (bf16[192,8]{0,1:T(8,128)(2,1)S(1)}, bf16[192]{0:T(256)(128)(2,1)S(1)}, bf16[192]{0:T(256)(128)(2,1)S(1)}, bf16[3,32]{1,0:T(4,128)(2,1)S(1)}) all-reduce(bf16[192,8]{0,1:T(8,128)(2,1)S(1)} %copy.74, bf16[192]{0:T(256)(128)(2,1)S(1)} %dynamic-slice.3, ...), channel_id=1, replica_groups=mesh['expert'=8,'shard'=4] {'expert'}, use_global_device_ids=true, to_apply=%region_19.20 | all-reduce | flops 2016 | bytes 8064 | tf_op jit(solution)/shard_map/psum | solution.py:481
  891.5 42.8 %all-reduce.11.cloned.1.call-done = (bf16[192,2304]{1,0:T(8,128)(2,1)}, bf16[192,768]{1,0:T(8,128)(2,1)}) async-done(((bf16[192,2304]{1,0:T(8,128)(2,1)}, bf16[192,768]{1,0:T(8,128)(2,1)}), (bf16[192,2304]{1,0:T(8,128)(2,1)}, bf16[192,768]{1,0:T(8,128)(2,1)})) %all-reduce.11.cloned.1.call-update) | async-done | bytes 1179664 | tf_op jit(solution)/shard_map/psum | solution.py:507
  (340 shorter events, 300.4 us)
Async XLA Ops:
  7.2 35.9 %all-gather.6.cloned.1.call-start = ((), (), s32[]{:S(2)}) async-start(), calls=%async_computation.6 | async-start | bytes 4423680 | tf_op jit(solution)/shard_map/all_gather | solution.py:353
  7.9 87.5 %all-gather.8.cloned.1.call-start = ((), (), s32[]{:S(2)}) async-start(), calls=%async_computation.7 | async-start | bytes 7864320 | tf_op jit(solution)/shard_map/all_gather | solution.py:371
  60.6 76.9 %all-to-all-start.3 = ((bf16[8,256,768]{2,1,0:T(8,128)(2,1)}), bf16[8,256,768]{2,1,0:T(8,128)(2,1)}, u32[]{:S(2)}, u32[]{:S(2)}) async-start(bf16[8,256,768]{2,1,0:T(8,128)(2,1)} %bitcast.212), calls=%async_computation.3 | async-start | bytes 6291456 | tf_op jit(solution)/shard_map/all_to_all | solution.py:398
  66.2 63.7 %all-gather.10.cloned.1.call-start = ((), (), s32[]{:S(2)}) async-start(), calls=%async_computation.8 | async-start | bytes 1474560 | tf_op jit(solution)/shard_map/all_gather | solution.py:354
  147.8 142.3 %all-to-all-start = ((bf16[8,256,768]{2,1,0:T(8,128)(2,1)}), bf16[8,256,768]{2,1,0:T(8,128)(2,1)}, u32[]{:S(2)}, u32[]{:S(2)}) async-start(bf16[8,256,768]{2,1,0:T(8,128)(2,1)} %bitcast.211), calls=%async_computation | async-start | bytes 6291456 | tf_op jit(solution)/shard_map/all_to_all | solution.py:398
  152.9 71.5 %collective-permute-start.5 = (bf16[768,768]{1,0:T(8,128)(2,1)}, bf16[768,768]{1,0:T(8,128)(2,1)}, u32[]{:S(2)}, u32[]{:S(2)}) collective-permute-start(bf16[768,768]{1,0:T(8,128)(2,1)} %bitcast.6), channel_id=1, source_target_pairs={{0,2},{1,3},{2,0},{3,1},{4,6},{5,7},{6,4},{7,5},{8,10},{9,11},{10,... | collective-permute-start | bytes 3538952 | tf_op jit(solution)/shard_map/ppermute | solution.py:288
  198.5 82.4 %collective-permute-start.2 = (bf16[768,768]{1,0:T(8,128)(2,1)}, bf16[768,768]{1,0:T(8,128)(2,1)S(1)}, u32[]{:S(2)}, u32[]{:S(2)}) collective-permute-start(bf16[768,768]{1,0:T(8,128)(2,1)} %bitcast.6), channel_id=1, source_target_pairs={{0,1},{1,0},{2,3},{3,2},{4,5},{5,4},{6,7},{7,6},{8,9},{9,8},{10,11... | collective-permute-start | bytes 3538952 | tf_op jit(solution)/shard_map/ppermute | solution.py:288
  220.2 121.9 %collective-permute-start.1 = (bf16[768,768]{1,0:T(8,128)(2,1)}, bf16[768,768]{1,0:T(8,128)(2,1)}, u32[]{:S(2)}, u32[]{:S(2)}) collective-permute-start(bf16[768,768]{1,0:T(8,128)(2,1)} %bitcast.5), channel_id=1, source_target_pairs={{0,1},{1,0},{2,3},{3,2},{4,5},{5,4},{6,7},{7,6},{8,9},{9,8},{10,11... | collective-permute-start | bytes 3538952 | tf_op jit(solution)/shard_map/ppermute | solution.py:288
  220.2 54.2 %collective-permute-start.3 = (bf16[768,768]{1,0:T(8,128)(2,1)}, bf16[768,768]{1,0:T(8,128)(2,1)}, u32[]{:S(2)}, u32[]{:S(2)}) collective-permute-start(bf16[768,768]{1,0:T(8,128)(2,1)} %bitcast.4), channel_id=1, source_target_pairs={{0,2},{1,3},{2,0},{3,1},{4,6},{5,7},{6,4},{7,5},{8,10},{9,11},{10,... | collective-permute-start | bytes 3538952 | tf_op jit(solution)/shard_map/ppermute | solution.py:288
  224.4 61.1 %collective-permute-start.8 = (bf16[768,768]{1,0:T(8,128)(2,1)}, bf16[768,768]{1,0:T(8,128)(2,1)S(1)}, u32[]{:S(2)}, u32[]{:S(2)}) collective-permute-start(bf16[768,768]{1,0:T(8,128)(2,1)} %collective-permute-done.5), channel_id=1, source_target_pairs={{0,1},{1,0},{2,3},{3,2},{4,5},{5,4},{6,7},{7,6},{8,9},{9,8},{10,11... | collective-permute-start | bytes 3538952 | tf_op jit(solution)/shard_map/ppermute | solution.py:288
  249.1 97.9 %collective-permute-start = (bf16[768,768]{1,0:T(8,128)(2,1)}, bf16[768,768]{1,0:T(8,128)(2,1)}, u32[]{:S(2)}, u32[]{:S(2)}) collective-permute-start(bf16[768,768]{1,0:T(8,128)(2,1)} %bitcast.4), channel_id=1, source_target_pairs={{0,1},{1,0},{2,3},{3,2},{4,5},{5,4},{6,7},{7,6},{8,9},{9,8},{10,11... | collective-permute-start | bytes 3538952 | tf_op jit(solution)/shard_map/ppermute | solution.py:288
  274.4 60.5 %collective-permute-start.7 = (bf16[768,768]{1,0:T(8,128)(2,1)}, bf16[768,768]{1,0:T(8,128)(2,1)S(1)}, u32[]{:S(2)}, u32[]{:S(2)}) collective-permute-start(bf16[768,768]{1,0:T(8,128)(2,1)} %collective-permute-done.4), channel_id=1, source_target_pairs={{0,1},{1,0},{2,3},{3,2},{4,5},{5,4},{6,7},{7,6},{8,9},{9,8},{10,11... | collective-permute-start | bytes 3538952 | tf_op jit(solution)/shard_map/ppermute | solution.py:288
  280.9 84.9 %collective-permute-start.6 = (bf16[768,768]{1,0:T(8,128)(2,1)}, bf16[768,768]{1,0:T(8,128)(2,1)}, u32[]{:S(2)}, u32[]{:S(2)}) collective-permute-start(bf16[768,768]{1,0:T(8,128)(2,1)} %collective-permute-done.3), channel_id=1, source_target_pairs={{0,1},{1,0},{2,3},{3,2},{4,5},{5,4},{6,7},{7,6},{8,9},{9,8},{10,11... | collective-permute-start | bytes 3538952 | tf_op jit(solution)/shard_map/ppermute | solution.py:288
  386.3 77.3 %all-to-all-start.1 = ((bf16[8,256,768]{2,1,0:T(8,128)(2,1)}), bf16[8,256,768]{2,1,0:T(8,128)(2,1)}, u32[]{:S(2)}, u32[]{:S(2)}) async-start(bf16[8,256,768]{2,1,0:T(8,128)(2,1)} %bitcast.207), calls=%async_computation.1 | async-start | bytes 6291456 | tf_op jit(solution)/shard_map/all_to_all | solution.py:407
  463.6 75.0 %all-to-all-start.4 = ((bf16[8,256,768]{2,1,0:T(8,128)(2,1)}), bf16[8,256,768]{2,1,0:T(8,128)(2,1)}, u32[]{:S(2)}, u32[]{:S(2)}) async-start(bf16[8,256,768]{2,1,0:T(8,128)(2,1)} %bitcast.206), calls=%async_computation.4 | async-start | bytes 6291456 | tf_op jit(solution)/shard_map/all_to_all | solution.py:407
  468.0 375.3 %reduce-scatter.4.cloned.1.call-start = ((), (), s32[]{:S(2)}) async-start(), calls=%async_computation.9 | async-start | bytes 245760
  475.2 176.2 %collective-permute-start.25 = (bf16[768,768]{1,0:T(8,128)(2,1)}, bf16[768,768]{1,0:T(8,128)(2,1)}, u32[]{:S(2)}, u32[]{:S(2)}) collective-permute-start(bf16[768,768]{1,0:T(8,128)(2,1)} %convolution_convert_fusion.3), channel_id=1, source_target_pairs={{0,1},{1,0},{2,3},{3,2},{4,5},{5,4},{6,7},{7,6},{8,9},{9,8},{10,11... | collective-permute-start | bytes 3538952 | tf_op jit(solution)/shard_map/ppermute | solution.py:288
  616.8 88.5 %collective-permute-start.10 = (bf16[512,1536]{1,0:T(8,128)(2,1)S(1)}, bf16[512,1536]{1,0:T(8,128)(2,1)S(1)}, u32[]{:S(2)}, u32[]{:S(2)}) collective-permute-start(bf16[512,1536]{1,0:T(8,128)(2,1)S(1)} %get-tuple-element.63), channel_id=1, source_target_pairs={{0,1},{1,0},{2,3},{3,2},{4,5},{5,4},{6,7},{7,6},{8,9},{9,8},{10,11... | collective-permute-start | bytes 4718600 | tf_op jit(solution)/shard_map/ppermute | solution.py:288
  643.9 72.6 %collective-permute-start.24 = (bf16[768,768]{1,0:T(8,128)(2,1)S(1)}, bf16[768,768]{1,0:T(8,128)(2,1)S(1)}, u32[]{:S(2)}, u32[]{:S(2)}) collective-permute-start(bf16[768,768]{1,0:T(8,128)(2,1)S(1)} %copy-done.56), channel_id=1, source_target_pairs={{0,1},{1,0},{2,3},{3,2},{4,5},{5,4},{6,7},{7,6},{8,9},{9,8},{10,11... | collective-permute-start | bytes 3538952 | tf_op jit(solution)/shard_map/ppermute | solution.py:288
  646.3 59.6 %collective-permute-start.22 = (bf16[768,768]{1,0:T(8,128)(2,1)S(1)}, bf16[768,768]{1,0:T(8,128)(2,1)S(1)}, u32[]{:S(2)}, u32[]{:S(2)}) collective-permute-start(bf16[768,768]{1,0:T(8,128)(2,1)S(1)} %copy-done.58), channel_id=1, source_target_pairs={{0,1},{1,0},{2,3},{3,2},{4,5},{5,4},{6,7},{7,6},{8,9},{9,8},{10,11... | collective-permute-start | bytes 3538952 | tf_op jit(solution)/shard_map/ppermute | solution.py:288
  646.4 64.8 %collective-permute-start.19 = (bf16[768,768]{1,0:T(8,128)(2,1)S(1)}, bf16[768,768]{1,0:T(8,128)(2,1)S(1)}, u32[]{:S(2)}, u32[]{:S(2)}) collective-permute-start(bf16[768,768]{1,0:T(8,128)(2,1)S(1)} %copy-done.57), channel_id=1, source_target_pairs={{0,1},{1,0},{2,3},{3,2},{4,5},{5,4},{6,7},{7,6},{8,9},{9,8},{10,11... | collective-permute-start | bytes 3538952 | tf_op jit(solution)/shard_map/ppermute | solution.py:288
  655.5 76.6 %collective-permute-start.26 = (bf16[768,768]{1,0:T(8,128)(2,1)S(1)}, bf16[768,768]{1,0:T(8,128)(2,1)S(1)}, u32[]{:S(2)}, u32[]{:S(2)}) collective-permute-start(bf16[768,768]{1,0:T(8,128)(2,1)S(1)} %add_convert_fusion.2), channel_id=1, source_target_pairs={{0,2},{1,3},{2,0},{3,1},{4,6},{5,7},{6,4},{7,5},{8,10},{9,11},{10,... | collective-permute-start | bytes 3538952 | tf_op jit(solution)/shard_map/ppermute | solution.py:288
  705.3 30.6 %collective-permute-start.9 = (bf16[512,1536]{1,0:T(8,128)(2,1)S(1)}, bf16[512,1536]{1,0:T(8,128)(2,1)S(1)}, u32[]{:S(2)}, u32[]{:S(2)}) collective-permute-start(bf16[512,1536]{1,0:T(8,128)(2,1)S(1)} %get-tuple-element.62), channel_id=1, source_target_pairs={{0,1},{1,0},{2,3},{3,2},{4,5},{5,4},{6,7},{7,6},{8,9},{9,8},{10,11... | collective-permute-start | bytes 4718600 | tf_op jit(solution)/shard_map/ppermute | solution.py:288
  705.9 59.9 %collective-permute-start.11 = (bf16[512,1536]{1,0:T(8,128)(2,1)S(1)}, bf16[512,1536]{1,0:T(8,128)(2,1)S(1)}, u32[]{:S(2)}, u32[]{:S(2)}) collective-permute-start(bf16[512,1536]{1,0:T(8,128)(2,1)S(1)} %fusion.33), channel_id=1, source_target_pairs={{0,2},{1,3},{2,0},{3,1},{4,6},{5,7},{6,4},{7,5},{8,10},{9,11},{10,... | collective-permute-start | bytes 4718600 | tf_op jit(solution)/shard_map/ppermute | solution.py:288
  711.2 58.6 %collective-permute-start.21 = (bf16[768,768]{1,0:T(8,128)(2,1)S(1)}, bf16[768,768]{1,0:T(8,128)(2,1)S(1)}, u32[]{:S(2)}, u32[]{:S(2)}) collective-permute-start(bf16[768,768]{1,0:T(8,128)(2,1)S(1)} %copy-done.55), channel_id=1, source_target_pairs={{0,1},{1,0},{2,3},{3,2},{4,5},{5,4},{6,7},{7,6},{8,9},{9,8},{10,11... | collective-permute-start | bytes 3538952 | tf_op jit(solution)/shard_map/ppermute | solution.py:288
  716.5 76.3 %collective-permute-start.18 = (bf16[768,768]{1,0:T(8,128)(2,1)S(1)}, bf16[768,768]{1,0:T(8,128)(2,1)S(1)}, u32[]{:S(2)}, u32[]{:S(2)}) collective-permute-start(bf16[768,768]{1,0:T(8,128)(2,1)S(1)} %convolution_convert_fusion.8), channel_id=1, source_target_pairs={{0,1},{1,0},{2,3},{3,2},{4,5},{5,4},{6,7},{7,6},{8,9},{9,8},{10,11... | collective-permute-start | bytes 3538952 | tf_op jit(solution)/shard_map/ppermute | solution.py:288
  732.1 59.0 %collective-permute-start.23 = (bf16[768,768]{1,0:T(8,128)(2,1)S(1)}, bf16[768,768]{1,0:T(8,128)(2,1)S(1)}, u32[]{:S(2)}, u32[]{:S(2)}) collective-permute-start(bf16[768,768]{1,0:T(8,128)(2,1)S(1)} %add_convert_fusion.3), channel_id=1, source_target_pairs={{0,2},{1,3},{2,0},{3,1},{4,6},{5,7},{6,4},{7,5},{8,10},{9,11},{10,... | collective-permute-start | bytes 3538952 | tf_op jit(solution)/shard_map/ppermute | solution.py:288
  735.9 80.2 %collective-permute-start.20 = (bf16[768,768]{1,0:T(8,128)(2,1)S(1)}, bf16[768,768]{1,0:T(8,128)(2,1)S(1)}, u32[]{:S(2)}, u32[]{:S(2)}) collective-permute-start(bf16[768,768]{1,0:T(8,128)(2,1)S(1)} %add_convert_fusion.4), channel_id=1, source_target_pairs={{0,2},{1,3},{2,0},{3,1},{4,6},{5,7},{6,4},{7,5},{8,10},{9,11},{10,... | collective-permute-start | bytes 3538952 | tf_op jit(solution)/shard_map/ppermute | solution.py:288
  769.8 49.6 %collective-permute-start.13 = (bf16[192,2304]{1,0:T(8,128)(2,1)S(1)}, bf16[192,2304]{1,0:T(8,128)(2,1)S(1)}, u32[]{:S(2)}, u32[]{:S(2)}) collective-permute-start(bf16[192,2304]{1,0:T(8,128)(2,1)S(1)} %get-tuple-element.61), channel_id=1, source_target_pairs={{0,1},{1,0},{2,3},{3,2},{4,5},{5,4},{6,7},{7,6},{8,9},{9,8},{10,11... | collective-permute-start | bytes 2654216 | tf_op jit(solution)/shard_map/ppermute | solution.py:288
  819.3 32.8 %collective-permute-start.12 = (bf16[192,2304]{1,0:T(8,128)(2,1)}, bf16[192,2304]{1,0:T(8,128)(2,1)}, u32[]{:S(2)}, u32[]{:S(2)}) collective-permute-start(bf16[192,2304]{1,0:T(8,128)(2,1)} %get-tuple-element.60), channel_id=1, source_target_pairs={{0,1},{1,0},{2,3},{3,2},{4,5},{5,4},{6,7},{7,6},{8,9},{9,8},{10,11... | collective-permute-start | bytes 2654216 | tf_op jit(solution)/shard_map/ppermute | solution.py:288
  820.5 31.7 %collective-permute-start.14 = (bf16[192,2304]{1,0:T(8,128)(2,1)}, bf16[192,2304]{1,0:T(8,128)(2,1)}, u32[]{:S(2)}, u32[]{:S(2)}) collective-permute-start(bf16[192,2304]{1,0:T(8,128)(2,1)} %fusion.54), channel_id=1, source_target_pairs={{0,2},{1,3},{2,0},{3,1},{4,6},{5,7},{6,4},{7,5},{8,10},{9,11},{10,... | collective-permute-start | bytes 2654216 | tf_op jit(solution)/shard_map/ppermute | solution.py:288
  824.4 109.9 %all-reduce.11.cloned.1.call-start = ((), (), s32[]{:S(2)}) async-start(), calls=%async_computation.10 | async-start | bytes 2359296 | tf_op jit(solution)/shard_map/psum | solution.py:507
  (84 other events, 1568.5 us)
Sparse Core Ops, SparseCore 0:
  9.6 33.4 all-gather.5
  48.8 46.4 all-gather.7
  96.9 17.4 all-gather.9
  824.5 18.7 reduce-scatter.3
  855.6 78.5 all-reduce.10

commit v2 on v1

v2 whole, which is shorter than its diff:
```python
import functools

import jax
import jax.numpy as jnp
from jax import lax
from jax.experimental import pallas as pl
from jax.experimental.pallas import tpu as pltpu
from jax.sharding import PartitionSpec as P

norm_epsilon = 1e-06
bucket_borders = (16, 23, 32, 45, 64, 91, 128, 181, 256, 362, 512, 724, 1024, 1448, 2048, 2896)


def bucket_of(distance):
    clipped = jnp.maximum(distance, 0)
    bucket_id = jnp.minimum(clipped, 15)
    for border in bucket_borders:
        bucket_id = bucket_id + (clipped >= border).astype(jnp.int32)
    return bucket_id


tile = 256
low_score = -1e30


def toeplitz_vectors(bias_table, diagonals):
    offsets = jnp.arange(2 * tile, dtype=jnp.int32)
    offsets = jnp.where(offsets < tile, offsets, offsets - 2 * tile)
    distance = jnp.arange(diagonals, dtype=jnp.int32)[:, None] * tile + offsets[None, :]
    onehot = bucket_of(distance)[None] == jnp.arange(bias_table.shape[1])[:, None, None]
    return jnp.einsum(
        "hc,cdm->hdm", bias_table, onehot.astype(jnp.bfloat16), preferred_element_type=jnp.float32
    )


def fill_bias(vector_ref, head, bias_ref, diagonals):
    def fill(delta, carry):
        row = vector_ref[head, pl.ds(delta, 1), :]
        wide = jnp.broadcast_to(row, (tile, 2 * tile))
        rolled = pltpu.roll(wide, 0, 1, stride=1, stride_axis=0)
        bias_ref[delta] = rolled[:, :tile]
        return carry

    lax.fori_loop(0, diagonals, fill, 0)


def start_of(position, first_end, second_end):
    return jnp.where(
        position >= second_end, second_end, jnp.where(position >= first_end, first_end, 0)
    )


def contract(left, right, left_dim, right_dim):
    return lax.dot_general(
        left, right, (((left_dim,), (right_dim,)), ((), ())), preferred_element_type=jnp.float32
    )


def attend_kernel(info_ref, q_ref, k_ref, v_ref, vector_ref, out_ref, log_ref, bias_ref):
    diagonals = vector_ref.shape[1]
    per_device = q_ref.shape[3] // tile
    first_end, second_end = info_ref[0], info_ref[1]
    fill_bias(vector_ref, 0, bias_ref, diagonals)

    def place(index):
        return index // per_device, pl.ds(pl.multiple_of(index % per_device * tile, tile), tile)

    def query_step(query_tile, carry):
        owner, lanes = place(query_tile)
        query = (q_ref[owner, 0, :, lanes] * 0.125).astype(jnp.bfloat16)
        first_tile = start_of(query_tile * tile, first_end, second_end) // tile
        query_pos = query_tile * tile + lax.broadcasted_iota(jnp.int32, (1, tile), 1)
        query_start = start_of(query_pos, first_end, second_end)

        def step(index, carry):
            top, total, blend = carry
            key_owner, keys = place(index)
            key_pos = index * tile + lax.broadcasted_iota(jnp.int32, (tile, 1), 0)
            scores = contract(k_ref[key_owner, 0, :, keys], query, 0, 0)
            scores = scores + bias_ref[query_tile - index]
            allowed = (key_pos >= query_start) & (key_pos <= query_pos)
            scores = jnp.where(allowed, scores, low_score)
            new_top = jnp.maximum(top, jnp.max(scores, axis=0, keepdims=True))
            weights = jnp.exp(scores - new_top)
            scale = jnp.exp(top - new_top)
            total = total * scale + jnp.sum(weights, axis=0, keepdims=True)
            part = contract(v_ref[key_owner, 0, :, keys], weights.astype(jnp.bfloat16), 1, 0)
            return new_top, total, blend * scale + part

        top, total, blend = lax.fori_loop(
            first_tile,
            query_tile + 1,
            step,
            (
                jnp.full((1, tile), low_score, jnp.float32),
                jnp.zeros((1, tile), jnp.float32),
                jnp.zeros((q_ref.shape[2], tile), jnp.float32),
            ),
        )
        out_ref[owner, 0, :, lanes] = (blend / total).astype(jnp.bfloat16)
        log_ref[0, pl.ds(query_tile, 1), :] = top + jnp.log(total)
        return carry

    lax.fori_loop(0, diagonals, query_step, 0)


def attend_back_kernel(
    info_ref,
    q_ref,
    k_ref,
    v_ref,
    g_ref,
    o_ref,
    log_ref,
    vector_ref,
    dq_ref,
    dk_ref,
    dv_ref,
    diag_ref,
    bias_ref,
    grad_bias_ref,
    dk_acc,
    dv_acc,
):
    diagonals = vector_ref.shape[1]
    per_device = q_ref.shape[3] // tile
    first_end, second_end = info_ref[0], info_ref[1]
    dk_acc[...] = jnp.zeros_like(dk_acc)
    dv_acc[...] = jnp.zeros_like(dv_acc)
    grad_bias_ref[...] = jnp.zeros_like(grad_bias_ref)
    fill_bias(vector_ref, 0, bias_ref, diagonals)

    def place(index):
        return index // per_device, pl.ds(pl.multiple_of(index % per_device * tile, tile), tile)

    def query_step(query_tile, carry):
        owner, lanes = place(query_tile)
        query = (q_ref[owner, 0, :, lanes] * 0.125).astype(jnp.bfloat16)
        grad = g_ref[owner, 0, :, lanes]
        product = grad.astype(jnp.float32) * o_ref[owner, 0, :, lanes].astype(jnp.float32)
        delta_row = jnp.sum(product, axis=0, keepdims=True)
        log_row = log_ref[0, pl.ds(query_tile, 1), :]
        first_tile = start_of(query_tile * tile, first_end, second_end) // tile
        query_pos = query_tile * tile + lax.broadcasted_iota(jnp.int32, (1, tile), 1)
        query_start = start_of(query_pos, first_end, second_end)

        def step(index, dq):
            key_owner, keys = place(index)
            key_pos = index * tile + lax.broadcasted_iota(jnp.int32, (tile, 1), 0)
            key = k_ref[key_owner, 0, :, keys]
            scores = contract(key, query, 0, 0) + bias_ref[query_tile - index]
            allowed = (key_pos >= query_start) & (key_pos <= query_pos)
            probs = jnp.exp(jnp.where(allowed, scores - log_row, low_score))
            grad_probs = contract(v_ref[key_owner, 0, :, keys], grad, 0, 0)
            grad_scores = probs * (grad_probs - delta_row)
            grad_bias_ref[query_tile - index] += grad_scores
            low = grad_scores.astype(jnp.bfloat16)
            dv_acc[index] += contract(grad, probs.astype(jnp.bfloat16), 1, 1)
            dk_acc[index] += contract(query, low, 1, 1)
            return dq + contract(key, low, 1, 0)

        dq = lax.fori_loop(
            first_tile, query_tile + 1, step, jnp.zeros((q_ref.shape[2], tile), jnp.float32)
        )
        dq_ref[owner, 0, :, lanes] = (dq * 0.125).astype(jnp.bfloat16)
        return carry

    lax.fori_loop(0, diagonals, query_step, 0)

    def reduce(delta, carry):
        value = grad_bias_ref[delta]
        value = jnp.concatenate([value, jnp.zeros_like(value)], axis=1)
        half = tile // 2
        while half >= 8:
            value = value[:half] + pltpu.roll(value[half:], 2 * tile - half, 1)
            half //= 2
        diag_ref[0, delta] = value
        return carry

    lax.fori_loop(0, diagonals, reduce, 0)
    for index in range(diagonals):
        owner = index // per_device
        lanes = pl.ds(index % per_device * tile, tile)
        dk_ref[owner, 0, :, lanes] = dk_acc[index].astype(jnp.bfloat16)
        dv_ref[owner, 0, :, lanes] = dv_acc[index].astype(jnp.bfloat16)


def part_spec(shape, part, heads):
    return pl.BlockSpec((shape[0], 1, *shape[2:]), lambda h: (0, h + part * heads, 0, 0))


def attend(info, qkv, vectors):
    devices, parts, head_dim, tok_count = qkv.shape
    heads, diagonals = parts // 3, vectors.shape[1]
    pairs = heads * (devices * tok_count) ** 2 * head_dim
    return pl.pallas_call(
        attend_kernel,
        grid=(heads,),
        in_specs=[
            pl.BlockSpec(memory_space=pltpu.SMEM),
            *(part_spec(qkv.shape, part, heads) for part in range(3)),
            pl.BlockSpec((1, diagonals, 2 * tile), lambda h: (h, 0, 0)),
        ],
        out_specs=[
            part_spec(qkv.shape, 0, heads),
            pl.BlockSpec((1, diagonals, tile), lambda h: (h, 0, 0)),
        ],
        out_shape=[
            jax.ShapeDtypeStruct((devices, heads, head_dim, tok_count), jnp.bfloat16),
            jax.ShapeDtypeStruct((heads, diagonals, tile), jnp.float32),
        ],
        scratch_shapes=[pltpu.VMEM((diagonals, tile, tile), jnp.float32)],
        compiler_params=pltpu.CompilerParams(vmem_limit_bytes=40 * 2**20),
        cost_estimate=pl.CostEstimate(
            flops=16 * 4 * pairs, bytes_accessed=2 * qkv.size, transcendentals=0
        ),
        name="attend",
    )(info, qkv, qkv, qkv, vectors)


def attend_back(info, qkv, grad, attended, logs, vectors):
    devices, parts, head_dim, tok_count = qkv.shape
    heads, diagonals = parts // 3, vectors.shape[1]
    pairs = heads * (devices * tok_count) ** 2 * head_dim
    one = part_spec(qkv.shape, 0, heads)
    return pl.pallas_call(
        attend_back_kernel,
        grid=(heads,),
        in_specs=[
            pl.BlockSpec(memory_space=pltpu.SMEM),
            *(part_spec(qkv.shape, part, heads) for part in range(3)),
            one,
            one,
            pl.BlockSpec((1, diagonals, tile), lambda h: (h, 0, 0)),
            pl.BlockSpec((1, diagonals, 2 * tile), lambda h: (h, 0, 0)),
        ],
        out_specs=[
            one,
            one,
            one,
            pl.BlockSpec((1, diagonals, 8, 2 * tile), lambda h: (h, 0, 0, 0)),
        ],
        out_shape=[jax.ShapeDtypeStruct((devices, heads, head_dim, tok_count), jnp.bfloat16)] * 3
        + [jax.ShapeDtypeStruct((heads, diagonals, 8, 2 * tile), jnp.float32)],
        scratch_shapes=[
            pltpu.VMEM((diagonals, tile, tile), jnp.float32),
            pltpu.VMEM((diagonals, tile, tile), jnp.float32),
            pltpu.VMEM((diagonals, head_dim, tile), jnp.float32),
            pltpu.VMEM((diagonals, head_dim, tile), jnp.float32),
        ],
        compiler_params=pltpu.CompilerParams(vmem_limit_bytes=48 * 2**20),
        cost_estimate=pl.CostEstimate(
            flops=16 * 10 * pairs, bytes_accessed=4 * qkv.size, transcendentals=0
        ),
        name="attend_back",
    )(info, qkv, qkv, qkv, grad, attended, logs, vectors)


def table_gradient(diag, bucket_count):
    head_count, diagonals, fold, width = diag.shape
    offsets = jnp.arange(width, dtype=jnp.int32)
    offsets = jnp.where(offsets < tile, offsets, offsets - width)
    distance = (
        jnp.arange(diagonals, dtype=jnp.int32)[:, None, None] * tile
        + offsets[None, None, :]
        - jnp.arange(fold, dtype=jnp.int32)[None, :, None]
    )
    onehot = bucket_of(distance)[None] == jnp.arange(bucket_count)[:, None, None, None]
    return jnp.einsum(
        "hdrc,bdrc->hb",
        diag,
        onehot.astype(jnp.float32),
        precision=lax.Precision.HIGHEST,
        preferred_element_type=jnp.float32,
    )


def partner(value, flip):
    count = lax.axis_size("shard")
    return lax.ppermute(value, "shard", [(i, i ^ flip) for i in range(count)])


def reduce_near(pieces):
    low = [p.astype(jnp.bfloat16) for p in pieces]
    far = (pieces[2] + partner(low[3], 1).astype(jnp.float32)).astype(jnp.bfloat16)
    near = pieces[0] + partner(low[1], 1).astype(jnp.float32)
    return near, partner(far, 2)


def reduce_pieces(pieces):
    near, far = reduce_near(pieces)
    return near + far.astype(jnp.float32)


def swap_heads(value):
    return lax.all_to_all(value, "shard", split_axis=0, concat_axis=0, tiled=True)


def reduce_rows(value, shard_index):
    count = lax.axis_size("shard")
    split = value.reshape(count, value.shape[0] // count, *value.shape[1:])
    return reduce_pieces(
        [
            lax.dynamic_index_in_dim(split, shard_index ^ r, 0, keepdims=False).astype(jnp.float32)
            for r in range(count)
        ]
    )


def dot32(left, right, spec):
    return jnp.einsum(spec, left, right, preferred_element_type=jnp.float32)


def norm_forward(values):
    inverse = lax.rsqrt(jnp.mean(values * values, axis=-1, keepdims=True) + norm_epsilon)
    return (values * inverse, inverse)


def norm_backward(grad_normed, normalized, inverse, gain_vector):
    grad_gain = jnp.sum(grad_normed * normalized, axis=0)
    scaled = grad_normed * gain_vector
    grad_values = inverse * (
        scaled - normalized * jnp.mean(scaled * normalized, axis=-1, keepdims=True)
    )
    return (grad_values, grad_gain)


def gated_unit(gate_value, up_value):
    return jax.nn.gelu(gate_value) * up_value


def local(
    tokens,
    w_qkv,
    w_out,
    router,
    gain_attn,
    gain_ffn,
    rel_bias,
    w_gate,
    w_up,
    w_down,
    routes,
    lengths,
    cotangent,
):
    shard_index = lax.axis_index("shard")
    full_qkv, full_out, full_router, full_gain_attn, full_gain_ffn = (
        lax.all_gather(w_qkv, "shard", axis=0, tiled=True),
        lax.all_gather(w_out, "shard", axis=0, tiled=True),
        lax.all_gather(router, "shard", axis=0, tiled=True),
        lax.all_gather(gain_attn, "shard", axis=0, tiled=True),
        lax.all_gather(gain_ffn, "shard", axis=0, tiled=True),
    )
    tok_count, model_width = tokens.shape
    local_heads, bucket_count = rel_bias.shape
    shard_count = lax.axis_size("shard")
    head_dim = model_width // (local_heads * shard_count)
    expert_count = full_router.shape[1]
    route_count = routes.shape[1]
    capacity = 2 * route_count * tok_count // expert_count
    inputs = tokens.astype(jnp.float32)
    attn_gain = full_gain_attn.astype(jnp.float32)
    ffn_gain = full_gain_ffn.astype(jnp.float32)
    normed_one, inverse_one = norm_forward(inputs)
    normed_attn = (normed_one * attn_gain).astype(jnp.bfloat16)
    qkv = dot32(full_qkv, normed_attn, "df,td->ft").astype(jnp.bfloat16)
    qkv = qkv.reshape(3, shard_count, local_heads, head_dim, tok_count)
    qkv = qkv.transpose(1, 0, 2, 3, 4)
    qkv = swap_heads(qkv.reshape(shard_count, 3 * local_heads, head_dim, tok_count))
    group_tok = shard_count * tok_count
    info = jnp.stack([lengths[0, 0], lengths[0, 0] + lengths[0, 1]]).astype(jnp.int32)
    vectors = toeplitz_vectors(rel_bias, group_tok // tile)
    weights_in = (w_gate[0], w_up[0], w_down[0])
    across = tuple(partner(w, 2) for w in weights_in)
    attended_group, logs = attend(info, qkv, vectors)
    attended_group, across = lax.optimization_barrier((attended_group, across))
    gate_pieces, up_pieces, down_pieces = (
        [w, partner(w, 1), x, partner(x, 1)] for w, x in zip(weights_in, across)
    )
    attended = swap_heads(attended_group).reshape(model_width, tok_count)
    hidden_one = inputs + dot32(attended, full_out, "dt,de->te")
    normed_two, inverse_two = norm_forward(hidden_one)
    normed_ffn = (normed_two * ffn_gain).astype(jnp.bfloat16)
    logits = jnp.dot(normed_ffn, full_router, preferred_element_type=jnp.float32)
    expert_ids = jnp.arange(expert_count, dtype=jnp.int32)
    chosen_mask = routes[:, :, None] == expert_ids[None, None, :]
    chosen = jnp.sum(jnp.where(chosen_mask, logits[:, None, :], 0.0), axis=2)
    gate_weights = jax.nn.softmax(chosen, axis=1)
    flat_routes = routes.reshape(-1)
    onehot_rows = (flat_routes[:, None] == expert_ids[None, :]).astype(jnp.int32)
    earlier = jnp.cumsum(onehot_rows, axis=0) - onehot_rows
    position = jnp.sum(earlier * onehot_rows, axis=1)
    slot_index = flat_routes * capacity + position
    slot_pair = slot_index.reshape(tok_count, route_count)
    slots = jnp.arange(expert_count * capacity, dtype=jnp.int32)
    pick = [(slot_pair[:, k][:, None] == slots[None, :]) for k in range(route_count)]
    pick_any = functools.reduce(jnp.logical_or, pick).astype(jnp.bfloat16)

    def dispatch(rows):
        packed = dot32(pick_any, rows, "ts,td->sd").astype(jnp.bfloat16)
        return lax.all_to_all(
            packed.reshape(expert_count, capacity, model_width),
            "expert",
            split_axis=0,
            concat_axis=0,
            tiled=True,
        ).reshape(expert_count * capacity, model_width)

    def give_back(rows):
        return lax.all_to_all(
            rows.reshape(expert_count, capacity, model_width),
            "expert",
            split_axis=0,
            concat_axis=0,
            tiled=True,
        ).reshape(expert_count * capacity, model_width)

    slot_gates = functools.reduce(
        jnp.add,
        [jnp.sum(jnp.where(pick[k], gate_weights[:, k][:, None], 0.0), axis=0) for k in range(2)],
    )
    slot_gates = lax.all_to_all(
        slot_gates.reshape(expert_count, capacity), "expert", 0, 0, tiled=True
    ).reshape(-1)
    cotangent_rows = dispatch(cotangent)
    rows_in = dispatch(normed_ffn)
    grad_rows_out = (slot_gates[:, None] * cotangent_rows.astype(jnp.float32)).astype(jnp.bfloat16)
    gate_proj = [dot32(rows_in, w, "rd,df->rf") for w in gate_pieces]
    up_proj = [dot32(rows_in, w, "rd,df->rf") for w in up_pieces]
    hidden = [gated_unit(a, b).astype(jnp.bfloat16) for a, b in zip(gate_proj, up_proj)]
    down_sum = sum(dot32(x, w, "rf,fd->rd") for x, w in zip(hidden, down_pieces))
    returned = give_back(down_sum.astype(jnp.bfloat16))
    routed_out = jnp.stack(
        [dot32(p.astype(jnp.bfloat16), returned, "ts,sd->td") for p in pick], axis=1
    )
    mixed_out = hidden_one + jnp.sum(gate_weights[:, :, None] * routed_out, axis=1)
    output = mixed_out.astype(jnp.bfloat16)
    grad_mixed = cotangent.astype(jnp.float32)
    grad_gate_weights = jnp.sum(grad_mixed[:, None, :] * routed_out, axis=2)
    grad_chosen = gate_weights * (
        grad_gate_weights - jnp.sum(gate_weights * grad_gate_weights, axis=1, keepdims=True)
    )
    grad_logits = jnp.sum(jnp.where(chosen_mask, grad_chosen[:, :, None], 0.0), axis=1).astype(
        jnp.bfloat16
    )
    grad_router_full = jnp.einsum(
        "td,te->de", normed_ffn, grad_logits, preferred_element_type=jnp.float32
    )
    grad_normed_ffn = jnp.einsum(
        "te,de->td", grad_logits, full_router, preferred_element_type=jnp.float32
    )
    gate_low, up_low, grad_input = [], [], 0.0
    for r in range(len(hidden)):
        grad_hid = dot32(grad_rows_out, down_pieces[r], "rd,fd->rf")
        unused, pullback = jax.vjp(gated_unit, gate_proj[r], up_proj[r])
        grad_gate_f, grad_up_f = pullback(grad_hid)
        gate_low.append(grad_gate_f.astype(jnp.bfloat16))
        up_low.append(grad_up_f.astype(jnp.bfloat16))
        grad_input = grad_input + dot32(gate_low[r], gate_pieces[r], "rf,df->rd")
        grad_input = grad_input + dot32(up_low[r], up_pieces[r], "rf,df->rd")
    grad_back = give_back(grad_input.astype(jnp.bfloat16))
    grad_gate_w = reduce_near([dot32(rows_in, x, "rd,rf->df") for x in gate_low])
    grad_up_w = reduce_near([dot32(rows_in, x, "rd,rf->df") for x in up_low])
    grad_down_w = reduce_near([dot32(x, grad_rows_out, "rf,rd->fd") for x in hidden])
    grad_normed_ffn = grad_normed_ffn + dot32(pick_any, grad_back, "ts,sd->td")
    grad_two, grad_gain_ffn_full = norm_backward(grad_normed_ffn, normed_two, inverse_two, ffn_gain)
    grad_hidden_one = grad_mixed + grad_two
    grad_attn_low = grad_hidden_one.astype(jnp.bfloat16)
    grad_out_full = dot32(attended, grad_attn_low, "dt,te->de")
    grad_attended = dot32(full_out, grad_attn_low, "de,te->dt").astype(jnp.bfloat16)
    grad_group = swap_heads(grad_attended.reshape(attended_group.shape))
    filler = jnp.zeros((model_width, -(expert_count + 1) % 128), jnp.float32)
    early = jnp.concatenate(
        [grad_out_full, grad_router_full, grad_gain_ffn_full[:, None], filler], axis=1
    )
    early = lax.psum(reduce_rows(early, shard_index).astype(jnp.bfloat16), "expert")
    grad_query, grad_keys, grad_values, diag = attend_back(
        info, qkv, grad_group, attended_group, logs, vectors
    )
    grad_table = table_gradient(diag, bucket_count)
    grad_cols = jnp.concatenate([grad_query, grad_keys, grad_values], axis=1)
    grad_cols, early, grad_gate_w, grad_up_w, grad_down_w = lax.optimization_barrier(
        (grad_cols, early, grad_gate_w, grad_up_w, grad_down_w)
    )
    early = early.astype(jnp.float32)
    grad_gate_w, grad_up_w, grad_down_w = (
        (near + far.astype(jnp.float32))[None]
        for near, far in (grad_gate_w, grad_up_w, grad_down_w)
    )
    grad_cols = swap_heads(grad_cols).reshape(shard_count, 3, local_heads, head_dim, tok_count)
    grad_cols = grad_cols.transpose(1, 0, 2, 3, 4).reshape(3 * model_width, tok_count)
    grad_qkv_full = dot32(normed_attn, grad_cols, "td,ft->df")
    grad_normed_attn = dot32(grad_cols, full_qkv, "ft,df->td")
    grad_one, grad_gain_attn_full = norm_backward(
        grad_normed_attn, normed_one, inverse_one, attn_gain
    )
    grad_tokens = grad_hidden_one + grad_one
    filler = jnp.zeros((model_width, 127), jnp.float32)
    late = jnp.concatenate([grad_qkv_full, grad_gain_attn_full[:, None], filler], axis=1)
    late = reduce_rows(late, shard_index)
    table_column = jnp.pad(grad_table.reshape(-1), (0, late.shape[0] - grad_table.size))
    late = late + jnp.pad(
        table_column[:, None], ((0, 0), (3 * model_width + 1, late.shape[1] - 3 * model_width - 2))
    )
    late = lax.psum(late.astype(jnp.bfloat16), "expert").astype(jnp.float32)
    pieces = (
        late[:, : 3 * model_width],
        early[:, :model_width],
        early[:, model_width : model_width + expert_count],
        late[:, 3 * model_width],
        early[:, model_width + expert_count],
        late[: grad_table.size, 3 * model_width + 1].reshape(grad_table.shape),
    )
    return (
        output,
        grad_tokens,
        pieces[0],
        pieces[1],
        pieces[2],
        pieces[3],
        pieces[4],
        pieces[5],
        grad_gate_w,
        grad_up_w,
        grad_down_w,
    )


def solution(mesh):
    in_specs = (
        P(("expert", "shard"), None),
        P("shard", None),
        P("shard", None),
        P("shard", None),
        P("shard"),
        P("shard"),
        P("shard", None),
        P("expert", None, "shard"),
        P("expert", None, "shard"),
        P("expert", "shard", None),
        P(("expert", "shard"), None),
        P("expert", None),
        P(("expert", "shard"), None),
    )
    out_specs = (
        P(("expert", "shard"), None),
        P(("expert", "shard"), None),
        P("shard", None),
        P("shard", None),
        P("shard", None),
        P("shard"),
        P("shard"),
        P("shard", None),
        P("expert", None, "shard"),
        P("expert", None, "shard"),
        P("expert", "shard", None),
    )
    return jax.shard_map(local, mesh=mesh, in_specs=in_specs, out_specs=out_specs, check_vma=False)
```

time: 958 us -> 920 us (0.960)
  starting transfers between devices: 207 us -> 47.6 us
  waiting for transfers between devices: 245 us -> 322 us
  local copies, waits for them, and re-layouts: 19.4 us -> 42.8 us
  matrix products: 274 us -> 294 us
    ppermute x27 -> x24, starting transfers between devices: 181 us -> 13.1 us  [partner(): return lax.ppermute(value, 'shard', [(i, i ^ flip) for i in range(count)])]
    all_to_all x2, waiting for transfers between devices: 0.72 us -> 85.8 us  [dispatch(): lax.all_to_all(packed.reshape(expert_count, capacity, model_width), 'expe...]
    ppermute x27 -> x24, waiting for transfers between devices: 112 us -> 50.9 us  [partner(): return lax.ppermute(value, 'shard', [(i, i ^ flip) for i in range(count)])]
    psum x1 -> x2, waiting for transfers between devices: 42.8 us -> 85.7 us  [the longest x1 70.1 us: local(): late = lax.psum(late.astype(jnp.bfloat16), 'expert').astype(jnp.float32)]
    dot_general x41 -> x47, matrix products: 253 us -> 288 us  [dot32(): return jnp.einsum(spec, left, right, preferred_element_type=jnp.float32)]
    all_to_all x0 -> x1, blocking collectives: none -> 31.3 us  [swap_heads(): lax.all_to_all(value, 'shard', split_axis=0, concat_axis=0, tiled=True)]
    all_to_all x0 -> x3, waiting for transfers between devices: none -> 25.5 us  [swap_heads(): lax.all_to_all(value, 'shard', split_axis=0, concat_axis=0, tiled=True)]
    psum x1 -> x0, blocking collectives: 17.4 us -> none  [local(): early = lax.psum(early, 'expert')]
  transfers between devices with their start and end apart: 37 -> 36, of which waited for: 15 -> 16; matrix products, arithmetic and copies ran while one was open for 31% -> 34% of each run, Pallas kernels for 10% -> 11%
where the time goes in v2:
time: 920 us; the launch traced here: 912 us
  waiting for transfers between devices  322 us (35%)
  matrix products  294 us (32%)
  Pallas kernels  98.2 us (11%)
  starting transfers between devices  47.6 us (5%)
  blocking collectives  44.8 us (5%)
  other arithmetic  44.4 us (5%)
  local copies, waits for them, and re-layouts  42.8 us (5%)
  between operations  17.4 us (2%)
    dot_general x47, matrix products, dot32(): return jnp.einsum(spec, left, right, preferred_element_type=jnp.float32)  288 us
    all_to_all x2, waiting for transfers between devices, dispatch(): lax.all_to_all(packed.reshape(expert_count, capacity, model_width), 'expe...  85.8 us
    psum x1, waiting for transfers between devices, local(): late = lax.psum(late.astype(jnp.bfloat16), 'expert').astype(jnp.float32)  70.1 us
    pallas_call x1, Pallas kernels, attend_back(): pl.pallas_call(attend_back_kernel, grid=(heads,), in_specs=[pl.BlockSpec(...  54.2 us
    ppermute x24, waiting for transfers between devices, partner(): return lax.ppermute(value, 'shard', [(i, i ^ flip) for i in range(count)])  50.9 us
    pallas_call x1, Pallas kernels, attend(): pl.pallas_call(attend_kernel, grid=(heads,), in_specs=[pl.BlockSpec(memor...  44.1 us
    all_to_all x2, waiting for transfers between devices, give_back(): lax.all_to_all(rows.reshape(expert_count, capacity, model_width), 'expert...  34.3 us
    all_to_all x1, blocking collectives, swap_heads(): lax.all_to_all(value, 'shard', split_axis=0, concat_axis=0, tiled=True)  31.3 us
  transfers between devices with their start and end apart: 36, of which 16 were waited for; matrix products, arithmetic and copies ran while one was open for 34% of the time, Pallas kernels for 11%

profile of v2, /device:TPU:0, one launch (start us, length us, event | category | flops | bytes accessed | tf_op | source)
XLA Modules:
  0.0 911.6 jit_solution(9331860261762019834)
XLA Ops:
  11.5 8.3 all-reduce.4
  21.3 21.8 %all-gather.4.cloned.1.call-done = bf16[768,2304]{1,0:T(8,128)(2,1)} async-done(((bf16[192,2304]{1,0:T(8,128)(2,1)}), bf16[768,2304]{1,0:T(8,128)(2,1)}) %all-gather.4.cloned.1.call-update) | async-done | bytes 3538960 | tf_op jit(solution)/shard_map/all_gather | solution.py:349
  68.2 17.7 %all-to-all-done.q_ref.k_ref.v_ref = bf16[4,9,64,512]{3,2,1,0:T(8,128)(2,1)S(1)} async-done(((bf16[4,9,64,512]{3,2,1,0:T(8,128)(2,1)}), bf16[4,9,64,512]{3,2,1,0:T(8,128)(2,1)S(1)}, u32[]{:S(2)}, u32[]{:S(2)}) %all-to-all-start) | async-done | bytes 2359328 | tf_op jit(solution)/shard_map/all_to_all | solution.py:296
  86.0 44.1 %attend.1 = (bf16[4,3,64,512]{3,2,1,0:T(8,128)(2,1)}, f32[3,8,256]{2,1,0:T(8,128)S(1)}) custom-call(s32[2]{0:T(128)S(1)} %pad_add_fusion.info_ref, bf16[4,9,64,512]{3,2,1,0:T(8,128)(2,1)S(1)} %all-to-all-done.q_ref.k_ref.v_ref, bf16[4,9,64,512]{3,2,1,0:T(8,128)(2,1)S(1)} %all-to-all-done.q_ref.k_ref.v_ref, ...), custom_call_target="tpu_custom_call" | custom-call | flops 51539607552 | bytes 2359296 | tf_op jit(solution)/shard_map/attend/pallas_call | solution.py:196
  136.7 24.8 %collective-permute-done = bf16[768,768]{1,0:T(8,128)(2,1)} collective-permute-done((bf16[768,768]{1,0:T(8,128)(2,1)}, bf16[768,768]{1,0:T(8,128)(2,1)}, u32[]{:S(2)}, u32[]{:S(2)}) %collective-permute-start) | collective-permute-done | bytes 1179680 | tf_op jit(solution)/shard_map/ppermute | solution.py:280
  168.8 7.8 all-to-all-done.1
  188.3 14.3 %all-gather.6.cloned.1.call-done = bf16[768,768]{1,0:T(8,128)(2,1)} async-done(((bf16[192,768]{1,0:T(8,128)(2,1)}), bf16[768,768]{1,0:T(8,128)(2,1)}) %all-gather.6.cloned.1.call-update) | async-done | bytes 1179664 | tf_op jit(solution)/shard_map/all_gather | solution.py:350
  209.2 43.6 %all-to-all-done.5 = bf16[8,256,768]{2,1,0:T(8,128)(2,1)} async-done(((bf16[8,256,768]{2,1,0:T(8,128)(2,1)}), bf16[8,256,768]{2,1,0:T(8,128)(2,1)}, u32[]{:S(2)}, u32[]{:S(2)}) %all-to-all-start.5) | async-done | bytes 3145760 | tf_op jit(solution)/shard_map/all_to_all | solution.py:402
  295.6 42.1 %all-to-all-done.2 = bf16[8,256,768]{2,1,0:T(8,128)(2,1)} async-done(((bf16[8,256,768]{2,1,0:T(8,128)(2,1)}), bf16[8,256,768]{2,1,0:T(8,128)(2,1)}, u32[]{:S(2)}, u32[]{:S(2)}) %all-to-all-start.2) | async-done | bytes 3145760 | tf_op jit(solution)/shard_map/all_to_all | solution.py:402
  342.7 7.7 fusion.115
  350.4 7.6 fusion.119
  357.9 10.2 %fusion.20 = (bf16[2048,768]{1,0:T(8,128)(2,1)}, bf16[2048,768]{1,0:T(8,128)(2,1)S(1)}, bf16[2048,768]{1,0:T(8,128)(2,1)S(1)}) fusion(f32[2048,768]{1,0:T(8,128)S(1)} %bitcast.256, f32[2048,768]{1,0:T(8,128)S(1)} %fusion.127, bf16[2048,768]{1,0:T(8,128)(2,1)} %bitcast.18, bf16[768,768]{1,0:T(8,128)(2,1)} %collective-permute-done), kind=kOutput, calls=%fused_computation.28 | convolution fusion | flops 2456813568 | bytes 26345472 | tf_op jit(solution)/shard_map/rd,df->rf/dot_general | solution.py:311
  379.0 9.5 %multiply_convert_fusion.3 = (bf16[2048,768]{1,0:T(8,128)(2,1)S(1)}, bf16[2048,768]{1,0:T(8,128)(2,1)S(1)}, bf16[2048,768]{1,0:T(8,128)(2,1)S(1)}) fusion(f32[2048,768]{1,0:T(8,128)} %fusion.119, f32[2048,768]{1,0:T(8,128)} %fusion.115, bf16[2048,768]{1,0:T(8,128)(2,1)S(1)} %bitcast.233, bf16[1,768,768]{2,1,0:T(8,128)(2,1)} %param.22), kind=kOutput, calls=%fused_computation.42 | convolution fusion | flops 2456813568 | bytes 26345472 | tf_op jit(solution)/shard_map/rd,fd->rf/dot_general | solution.py:311
  388.6 10.6 %fusion.134 = f32[2048,768]{1,0:T(8,128)} fusion(bf16[2048,768]{1,0:T(8,128)(2,1)} %get-tuple-element.127, bf16[768,768]{1,0:T(8,128)(2,1)} %collective-permute-done), kind=kOutput, calls=%fused_computation.238 | convolution fusion | flops 2415919104 | bytes 10616832 | tf_op jit(solution)/shard_map/rf,df->rd/dot_general | solution.py:311
  410.0 11.7 %fusion.13 = (bf16[2048,768]{1,0:T(8,128)(2,1)}, bf16[2048,768]{1,0:T(8,128)(2,1)}, bf16[2048,768]{1,0:T(8,128)(2,1)S(1)}) fusion(f32[2048,768]{1,0:T(8,128)} %fusion.130, f32[2048,768]{1,0:T(8,128)S(1)} %fusion.125, bf16[2048,768]{1,0:T(8,128)(2,1)} %bitcast.18, bf16[768,768]{1,0:T(8,128)(2,1)} %collective-permute-done.3), kind=kOutput, calls=%fused_computation.21 | convolution fusion | flops 2456813568 | bytes 26345472 | tf_op jit(solution)/shard_map/rd,df->rf/dot_general | solution.py:311
  421.6 6.7 fusion.113
  432.2 7.6 fusion.129
  443.8 13.5 %fusion.27 = (bf16[2048,768]{1,0:T(8,128)(2,1)}, bf16[2048,768]{1,0:T(8,128)(2,1)}, bf16[2048,768]{1,0:T(8,128)(2,1)}) fusion(f32[2048,768]{1,0:T(8,128)} %fusion.136, f32[2048,768]{1,0:T(8,128)} %fusion.129, bf16[2048,768]{1,0:T(8,128)(2,1)} %bitcast.18, bf16[768,768]{1,0:T(8,128)(2,1)} %collective-permute-done.6), kind=kOutput, calls=%fused_computation.35 | convolution fusion | flops 2456813568 | bytes 26345472 | tf_op jit(solution)/shard_map/rd,df->rf/dot_general | solution.py:311
  457.3 7.3 add_convert_fusion.1
  469.1 7.8 fusion.137
  504.1 20.4 %add_convert_fusion = bf16[2048,768]{1,0:T(8,128)(2,1)} fusion(f32[2048,768]{1,0:T(8,128)} %fusion.137, f32[2048,768]{1,0:T(8,128)} %fusion.135, f32[2048,768]{1,0:T(8,128)} %fusion.134, f32[2048,768]{1,0:T(8,128)} %fusion.132, f32[2048,768]{1,0:T(8,128)} %fusion.131, f32[2048,768]{1,0:T(8,128)} %fusion.117, f32[2048,768]{1,0:T(8,128)} %fusion.113, ...), kind=kOutput, calls=%fused_computation.38 | convolution fusion | flops 2428502016 | bytes 51511296 | tf_op jit(solution)/shard_map/rf,df->rd/dot_general | solution.py:311
  524.5 14.8 %all-to-all-done.3 = bf16[8,256,768]{2,1,0:T(8,128)(2,1)} async-done(((bf16[8,256,768]{2,1,0:T(8,128)(2,1)}), bf16[8,256,768]{2,1,0:T(8,128)(2,1)}, u32[]{:S(2)}, u32[]{:S(2)}) %all-to-all-start.3) | async-done | bytes 3145760 | tf_op jit(solution)/shard_map/all_to_all | solution.py:411
  594.3 19.6 %all-to-all-done.6 = bf16[8,256,768]{2,1,0:T(8,128)(2,1)} async-done(((bf16[8,256,768]{2,1,0:T(8,128)(2,1)}), bf16[8,256,768]{2,1,0:T(8,128)(2,1)}, u32[]{:S(2)}, u32[]{:S(2)}) %all-to-all-start.6) | async-done | bytes 3145760 | tf_op jit(solution)/shard_map/all_to_all | solution.py:411
  646.6 7.2 convert_add_fusion.3
  653.8 8.4 collective-permute-done.11
  664.3 54.2 %attend_back.1 = (bf16[4,3,64,512]{3,2,1,0:T(8,128)(2,1)S(1)}, bf16[4,3,64,512]{3,2,1,0:T(8,128)(2,1)S(1)}, bf16[4,3,64,512]{3,2,1,0:T(8,128)(2,1)S(1)}, f32[3,8,8,512]{3,2,1,0:T(8,128)S(1)}) custom-call(s32[2]{0:T(128)S(1)} %copy-done.4, bf16[4,9,64,512]{3,2,1,0:T(8,128)(2,1)} %copy-done.2, bf16[4,9,64,512]{3,2,1,0:T(8,128)(2,1)} %copy-done.2, ...), custom_call_target="tpu_custom_call" | custom-call | flops 128849018880 | bytes 4718592 | tf_op jit(solution)/shard_map/attend_back/pallas_call | solution.py:226
  718.7 15.6 %all-reduce.8.cloned.1.call-done = bf16[192,896]{1,0:T(8,128)(2,1)} async-done(((bf16[192,896]{1,0:T(8,128)(2,1)}), bf16[192,896]{1,0:T(8,128)(2,1)}) %all-reduce.8.cloned.1.call-update) | async-done | bytes 344080 | tf_op jit(solution)/shard_map/psum | solution.py:477
  734.3 31.3 %all_to_all.46 = bf16[4,9,64,512]{3,2,1,0:T(8,128)(2,1)S(1)} all-to-all(bf16[4,9,64,512]{3,2,1,0:T(8,128)(2,1)S(1)} %pad_maximum_fusion.1), channel_id=1, replica_groups=mesh['expert'=8,'shard'=4] {'shard'}, dimensions={0} | all-to-all | bytes 4718592 | tf_op jit(solution)/shard_map/all_to_all | solution.py:296
  774.6 6.9 fusion.139
  782.2 8.5 concatenate.22
  812.7 9.4 %collective-permute-done.23 = bf16[192,2432]{1,0:T(8,128)(2,1)} collective-permute-done((bf16[192,2432]{1,0:T(8,128)(2,1)}, bf16[192,2432]{1,0:T(8,128)(2,1)}, u32[]{:S(2)}, u32[]{:S(2)}) %collective-permute-start.23) | collective-permute-done | bytes 933920 | tf_op jit(solution)/shard_map/ppermute | solution.py:280
  830.3 70.1 %all-reduce.10.cloned.1.call-done = bf16[192,2432]{1,0:T(8,128)(2,1)} async-done(((bf16[192,2432]{1,0:T(8,128)(2,1)}), bf16[192,2432]{1,0:T(8,128)(2,1)}) %all-reduce.10.cloned.1.call-update) | async-done | bytes 933904 | tf_op jit(solution)/shard_map/psum | solution.py:506
  (358 shorter events, 303.2 us)
Async XLA Ops:
  7.2 35.9 %all-gather.4.cloned.1.call-start = ((), (), s32[]{:S(2)}) async-start(), calls=%async_computation.9 | async-start | bytes 4423680 | tf_op jit(solution)/shard_map/all_gather | solution.py:349
  53.3 32.7 %all-to-all-start = ((bf16[4,9,64,512]{3,2,1,0:T(8,128)(2,1)}), bf16[4,9,64,512]{3,2,1,0:T(8,128)(2,1)S(1)}, u32[]{:S(2)}, u32[]{:S(2)}) async-start(bf16[4,9,64,512]{3,2,1,0:T(8,128)(2,1)} %bitcast.226), calls=%async_computation | async-start | bytes 4718592 | tf_op jit(solution)/shard_map/all_to_all | solution.py:296
  57.0 73.0 %collective-permute-start.2 = (bf16[768,768]{1,0:T(8,128)(2,1)}, bf16[768,768]{1,0:T(8,128)(2,1)}, u32[]{:S(2)}, u32[]{:S(2)}) collective-permute-start(bf16[768,768]{1,0:T(8,128)(2,1)} %bitcast.11), channel_id=1, source_target_pairs={{0,2},{1,3},{2,0},{3,1},{4,6},{5,7},{6,4},{7,5},{8,10},{9,11},{10,... | collective-permute-start | bytes 3538952 | tf_op jit(solution)/shard_map/ppermute | solution.py:280
  59.0 77.6 %collective-permute-start.1 = (bf16[768,768]{1,0:T(8,128)(2,1)}, bf16[768,768]{1,0:T(8,128)(2,1)}, u32[]{:S(2)}, u32[]{:S(2)}) collective-permute-start(bf16[768,768]{1,0:T(8,128)(2,1)} %bitcast.10), channel_id=1, source_target_pairs={{0,2},{1,3},{2,0},{3,1},{4,6},{5,7},{6,4},{7,5},{8,10},{9,11},{10,... | collective-permute-start | bytes 3538952 | tf_op jit(solution)/shard_map/ppermute | solution.py:280
  59.1 102.3 %collective-permute-start = (bf16[768,768]{1,0:T(8,128)(2,1)}, bf16[768,768]{1,0:T(8,128)(2,1)}, u32[]{:S(2)}, u32[]{:S(2)}) collective-permute-start(bf16[768,768]{1,0:T(8,128)(2,1)} %bitcast.9), channel_id=1, source_target_pairs={{0,2},{1,3},{2,0},{3,1},{4,6},{5,7},{6,4},{7,5},{8,10},{9,11},{10,... | collective-permute-start | bytes 3538952 | tf_op jit(solution)/shard_map/ppermute | solution.py:280
  161.5 15.1 %all-to-all-start.1 = ((bf16[4,3,64,512]{3,2,1,0:T(8,128)(2,1)}), bf16[4,3,64,512]{3,2,1,0:T(8,128)(2,1)S(1)}, u32[]{:S(2)}, u32[]{:S(2)}) async-start(bf16[4,3,64,512]{3,2,1,0:T(8,128)(2,1)} %get-tuple-element.30.o_ref), calls=%async_computation.1 | async-start | bytes 1572864 | tf_op jit(solution)/shard_map/all_to_all | solution.py:296
  176.6 76.3 %all-to-all-start.5 = ((bf16[8,256,768]{2,1,0:T(8,128)(2,1)}), bf16[8,256,768]{2,1,0:T(8,128)(2,1)}, u32[]{:S(2)}, u32[]{:S(2)}) async-start(bf16[8,256,768]{2,1,0:T(8,128)(2,1)} %bitcast.232), calls=%async_computation.5 | async-start | bytes 6291456 | tf_op jit(solution)/shard_map/all_to_all | solution.py:402
  182.2 20.4 %all-gather.6.cloned.1.call-start = ((), (), s32[]{:S(2)}) async-start(), calls=%async_computation.10 | async-start | bytes 1474560 | tf_op jit(solution)/shard_map/all_gather | solution.py:350
  263.5 74.2 %all-to-all-start.2 = ((bf16[8,256,768]{2,1,0:T(8,128)(2,1)}), bf16[8,256,768]{2,1,0:T(8,128)(2,1)}, u32[]{:S(2)}, u32[]{:S(2)}) async-start(bf16[8,256,768]{2,1,0:T(8,128)(2,1)} %bitcast.231), calls=%async_computation.2 | async-start | bytes 6291456 | tf_op jit(solution)/shard_map/all_to_all | solution.py:402
  268.0 15.5 %collective-permute-start.5 = (bf16[768,768]{1,0:T(8,128)(2,1)}, bf16[768,768]{1,0:T(8,128)(2,1)}, u32[]{:S(2)}, u32[]{:S(2)}) collective-permute-start(bf16[768,768]{1,0:T(8,128)(2,1)} %bitcast.11), channel_id=1, source_target_pairs={{0,1},{1,0},{2,3},{3,2},{4,5},{5,4},{6,7},{7,6},{8,9},{9,8},{10,11... | collective-permute-start | bytes 3538952 | tf_op jit(solution)/shard_map/ppermute | solution.py:280
  268.0 137.0 %collective-permute-start.4 = (bf16[768,768]{1,0:T(8,128)(2,1)}, bf16[768,768]{1,0:T(8,128)(2,1)}, u32[]{:S(2)}, u32[]{:S(2)}) collective-permute-start(bf16[768,768]{1,0:T(8,128)(2,1)} %bitcast.10), channel_id=1, source_target_pairs={{0,1},{1,0},{2,3},{3,2},{4,5},{5,4},{6,7},{7,6},{8,9},{9,8},{10,11... | collective-permute-start | bytes 3538952 | tf_op jit(solution)/shard_map/ppermute | solution.py:280
  268.5 141.4 %collective-permute-start.3 = (bf16[768,768]{1,0:T(8,128)(2,1)}, bf16[768,768]{1,0:T(8,128)(2,1)}, u32[]{:S(2)}, u32[]{:S(2)}) collective-permute-start(bf16[768,768]{1,0:T(8,128)(2,1)} %bitcast.9), channel_id=1, source_target_pairs={{0,1},{1,0},{2,3},{3,2},{4,5},{5,4},{6,7},{7,6},{8,9},{9,8},{10,11... | collective-permute-start | bytes 3538952 | tf_op jit(solution)/shard_map/ppermute | solution.py:280
  270.5 173.2 %collective-permute-start.6 = (bf16[768,768]{1,0:T(8,128)(2,1)}, bf16[768,768]{1,0:T(8,128)(2,1)}, u32[]{:S(2)}, u32[]{:S(2)}) collective-permute-start(bf16[768,768]{1,0:T(8,128)(2,1)} %collective-permute-done), channel_id=1, source_target_pairs={{0,1},{1,0},{2,3},{3,2},{4,5},{5,4},{6,7},{7,6},{8,9},{9,8},{10,11... | collective-permute-start | bytes 3538952 | tf_op jit(solution)/shard_map/ppermute | solution.py:280
  271.0 18.8 %collective-permute-start.8 = (bf16[768,768]{1,0:T(8,128)(2,1)}, bf16[768,768]{1,0:T(8,128)(2,1)S(1)}, u32[]{:S(2)}, u32[]{:S(2)}) collective-permute-start(bf16[768,768]{1,0:T(8,128)(2,1)} %collective-permute-done.2), channel_id=1, source_target_pairs={{0,1},{1,0},{2,3},{3,2},{4,5},{5,4},{6,7},{7,6},{8,9},{9,8},{10,11... | collective-permute-start | bytes 3538952 | tf_op jit(solution)/shard_map/ppermute | solution.py:280
  283.5 148.7 %collective-permute-start.7 = (bf16[768,768]{1,0:T(8,128)(2,1)}, bf16[768,768]{1,0:T(8,128)(2,1)}, u32[]{:S(2)}, u32[]{:S(2)}) collective-permute-start(bf16[768,768]{1,0:T(8,128)(2,1)} %collective-permute-done.1), channel_id=1, source_target_pairs={{0,1},{1,0},{2,3},{3,2},{4,5},{5,4},{6,7},{7,6},{8,9},{9,8},{10,11... | collective-permute-start | bytes 3538952 | tf_op jit(solution)/shard_map/ppermute | solution.py:280
  464.6 74.6 %all-to-all-start.3 = ((bf16[8,256,768]{2,1,0:T(8,128)(2,1)}), bf16[8,256,768]{2,1,0:T(8,128)(2,1)}, u32[]{:S(2)}, u32[]{:S(2)}) async-start(bf16[8,256,768]{2,1,0:T(8,128)(2,1)} %bitcast.19), calls=%async_computation.3 | async-start | bytes 6291456 | tf_op jit(solution)/shard_map/all_to_all | solution.py:411
  539.3 74.6 %all-to-all-start.6 = ((bf16[8,256,768]{2,1,0:T(8,128)(2,1)}), bf16[8,256,768]{2,1,0:T(8,128)(2,1)}, u32[]{:S(2)}, u32[]{:S(2)}) async-start(bf16[8,256,768]{2,1,0:T(8,128)(2,1)} %bitcast.30), calls=%async_computation.6 | async-start | bytes 6291456 | tf_op jit(solution)/shard_map/all_to_all | solution.py:411
  549.1 16.7 %collective-permute-start.16 = (bf16[768,768]{1,0:T(8,128)(2,1)S(1)}, bf16[768,768]{1,0:T(8,128)(2,1)S(1)}, u32[]{:S(2)}, u32[]{:S(2)}) collective-permute-start(bf16[768,768]{1,0:T(8,128)(2,1)S(1)} %copy-done.69), channel_id=1, source_target_pairs={{0,1},{1,0},{2,3},{3,2},{4,5},{5,4},{6,7},{7,6},{8,9},{9,8},{10,11... | collective-permute-start | bytes 3538952 | tf_op jit(solution)/shard_map/ppermute | solution.py:280
  549.6 22.9 %collective-permute-start.13 = (bf16[768,768]{1,0:T(8,128)(2,1)S(1)}, bf16[768,768]{1,0:T(8,128)(2,1)S(1)}, u32[]{:S(2)}, u32[]{:S(2)}) collective-permute-start(bf16[768,768]{1,0:T(8,128)(2,1)S(1)} %copy-done.68), channel_id=1, source_target_pairs={{0,1},{1,0},{2,3},{3,2},{4,5},{5,4},{6,7},{7,6},{8,9},{9,8},{10,11... | collective-permute-start | bytes 3538952 | tf_op jit(solution)/shard_map/ppermute | solution.py:280
  549.7 29.5 %collective-permute-start.18 = (bf16[768,768]{1,0:T(8,128)(2,1)S(1)}, bf16[768,768]{1,0:T(8,128)(2,1)S(1)}, u32[]{:S(2)}, u32[]{:S(2)}) collective-permute-start(bf16[768,768]{1,0:T(8,128)(2,1)S(1)} %convolution_convert_fusion.4), channel_id=1, source_target_pairs={{0,1},{1,0},{2,3},{3,2},{4,5},{5,4},{6,7},{7,6},{8,9},{9,8},{10,11... | collective-permute-start | bytes 3538952 | tf_op jit(solution)/shard_map/ppermute | solution.py:280
  555.7 73.2 %collective-permute-start.15 = (bf16[768,768]{1,0:T(8,128)(2,1)}, bf16[768,768]{1,0:T(8,128)(2,1)}, u32[]{:S(2)}, u32[]{:S(2)}) collective-permute-start(bf16[768,768]{1,0:T(8,128)(2,1)} %convolution_convert_fusion.6), channel_id=1, source_target_pairs={{0,1},{1,0},{2,3},{3,2},{4,5},{5,4},{6,7},{7,6},{8,9},{9,8},{10,11... | collective-permute-start | bytes 3538952 | tf_op jit(solution)/shard_map/ppermute | solution.py:280
  561.5 83.4 %collective-permute-start.12 = (bf16[768,768]{1,0:T(8,128)(2,1)}, bf16[768,768]{1,0:T(8,128)(2,1)}, u32[]{:S(2)}, u32[]{:S(2)}) collective-permute-start(bf16[768,768]{1,0:T(8,128)(2,1)} %convolution_convert_fusion.8), channel_id=1, source_target_pairs={{0,1},{1,0},{2,3},{3,2},{4,5},{5,4},{6,7},{7,6},{8,9},{9,8},{10,11... | collective-permute-start | bytes 3538952 | tf_op jit(solution)/shard_map/ppermute | solution.py:280
  565.8 152.9 %collective-permute-start.20 = (bf16[768,768]{1,0:T(8,128)(2,1)}, bf16[768,768]{1,0:T(8,128)(2,1)}, u32[]{:S(2)}, u32[]{:S(2)}) collective-permute-start(bf16[768,768]{1,0:T(8,128)(2,1)} %add_convert_fusion.2), channel_id=1, source_target_pairs={{0,2},{1,3},{2,0},{3,1},{4,6},{5,7},{6,4},{7,5},{8,10},{9,11},{10,... | collective-permute-start | bytes 3538952 | tf_op jit(solution)/shard_map/ppermute | solution.py:280
  572.5 146.2 %collective-permute-start.17 = (bf16[768,768]{1,0:T(8,128)(2,1)}, bf16[768,768]{1,0:T(8,128)(2,1)}, u32[]{:S(2)}, u32[]{:S(2)}) collective-permute-start(bf16[768,768]{1,0:T(8,128)(2,1)} %add_convert_fusion.3), channel_id=1, source_target_pairs={{0,2},{1,3},{2,0},{3,1},{4,6},{5,7},{6,4},{7,5},{8,10},{9,11},{10,... | collective-permute-start | bytes 3538952 | tf_op jit(solution)/shard_map/ppermute | solution.py:280
  579.2 139.5 %collective-permute-start.14 = (bf16[768,768]{1,0:T(8,128)(2,1)}, bf16[768,768]{1,0:T(8,128)(2,1)}, u32[]{:S(2)}, u32[]{:S(2)}) collective-permute-start(bf16[768,768]{1,0:T(8,128)(2,1)} %add_convert_fusion.4), channel_id=1, source_target_pairs={{0,2},{1,3},{2,0},{3,1},{4,6},{5,7},{6,4},{7,5},{8,10},{9,11},{10,... | collective-permute-start | bytes 3538952 | tf_op jit(solution)/shard_map/ppermute | solution.py:280
  628.9 14.4 %collective-permute-start.10 = (bf16[192,896]{1,0:T(8,128)(2,1)S(1)}, bf16[192,896]{1,0:T(8,128)(2,1)S(1)}, u32[]{:S(2)}, u32[]{:S(2)}) collective-permute-start(bf16[192,896]{1,0:T(8,128)(2,1)S(1)} %get-tuple-element.136), channel_id=1, source_target_pairs={{0,1},{1,0},{2,3},{3,2},{4,5},{5,4},{6,7},{7,6},{8,9},{9,8},{10,11... | collective-permute-start | bytes 1032200 | tf_op jit(solution)/shard_map/ppermute | solution.py:280
  639.7 24.5 %all-to-all-start.7 = ((bf16[4,3,64,512]{3,2,1,0:T(8,128)(2,1)}), bf16[4,3,64,512]{3,2,1,0:T(8,128)(2,1)S(1)}, u32[]{:S(2)}, u32[]{:S(2)}) async-start(bf16[4,3,64,512]{3,2,1,0:T(8,128)(2,1)} %bitcast.33), calls=%async_computation.7 | async-start | bytes 1572864 | tf_op jit(solution)/shard_map/all_to_all | solution.py:296
  643.2 91.1 %all-reduce.8.cloned.1.call-start = ((), (), s32[]{:S(2)}) async-start(), calls=%async_computation.11 | async-start | bytes 688128 | tf_op jit(solution)/shard_map/psum | solution.py:477
  644.9 17.3 %collective-permute-start.11 = (bf16[192,896]{1,0:T(8,128)(2,1)S(1)}, bf16[192,896]{1,0:T(8,128)(2,1)S(1)}, u32[]{:S(2)}, u32[]{:S(2)}) collective-permute-start(bf16[192,896]{1,0:T(8,128)(2,1)S(1)} %fusion.70), channel_id=1, source_target_pairs={{0,2},{1,3},{2,0},{3,1},{4,6},{5,7},{6,4},{7,5},{8,10},{9,11},{10,... | collective-permute-start | bytes 1032200 | tf_op jit(solution)/shard_map/ppermute | solution.py:280
  664.2 236.2 %all-reduce.10.cloned.1.call-start = ((), (), s32[]{:S(2)}) async-start(), calls=%async_computation.12 | async-start | bytes 1867776 | tf_op jit(solution)/shard_map/psum | solution.py:506
  794.2 18.5 %collective-permute-start.21 = (bf16[192,2432]{1,0:T(8,128)(2,1)}, bf16[192,2432]{1,0:T(8,128)(2,1)}, u32[]{:S(2)}, u32[]{:S(2)}) collective-permute-start(bf16[192,2432]{1,0:T(8,128)(2,1)} %get-tuple-element.133), channel_id=1, source_target_pairs={{0,1},{1,0},{2,3},{3,2},{4,5},{5,4},{6,7},{7,6},{8,9},{9,8},{10,11... | collective-permute-start | bytes 2801672 | tf_op jit(solution)/shard_map/ppermute | solution.py:280
  799.1 23.1 %collective-permute-start.23 = (bf16[192,2432]{1,0:T(8,128)(2,1)}, bf16[192,2432]{1,0:T(8,128)(2,1)}, u32[]{:S(2)}, u32[]{:S(2)}) collective-permute-start(bf16[192,2432]{1,0:T(8,128)(2,1)} %fusion.51), channel_id=1, source_target_pairs={{0,2},{1,3},{2,0},{3,1},{4,6},{5,7},{6,4},{7,5},{8,10},{9,11},{10,... | collective-permute-start | bytes 2801672 | tf_op jit(solution)/shard_map/ppermute | solution.py:280
  (88 other events, 1321.8 us)
Sparse Core Ops, SparseCore 0:
  9.6 33.4 all-gather.3
  184.6 17.9 all-gather.5
  664.3 69.9 all-reduce.7
  825.6 74.6 all-reduce.9

commit v3 on v2

--- a/solution.py
+++ b/solution.py
@@ -284,27 +284,48 @@
     low = [p.astype(jnp.bfloat16) for p in pieces]
     far = (pieces[2] + partner(low[3], 1).astype(jnp.float32)).astype(jnp.bfloat16)
     near = pieces[0] + partner(low[1], 1).astype(jnp.float32)
-    return near, partner(far, 2)
+    return near, far
 
 
 def reduce_pieces(pieces):
     near, far = reduce_near(pieces)
-    return near + far.astype(jnp.float32)
+    return near + partner(far, 2).astype(jnp.float32)
 
 
 def swap_heads(value):
     return lax.all_to_all(value, "shard", split_axis=0, concat_axis=0, tiled=True)
 
 
-def reduce_rows(value, shard_index):
+def reduce_rows(value, columns, shard_index):
     count = lax.axis_size("shard")
-    split = value.reshape(count, value.shape[0] // count, *value.shape[1:])
-    return reduce_pieces(
-        [
-            lax.dynamic_index_in_dim(split, shard_index ^ r, 0, keepdims=False).astype(jnp.float32)
-            for r in range(count)
-        ]
-    )
+    rows = value.shape[0] // count
+    filler = jnp.zeros((rows, -columns.shape[1] % 128), jnp.bfloat16)
+
+    def piece(r):
+        first = (shard_index ^ r) * rows
+        return jnp.concatenate(
+            [
+                lax.dynamic_slice_in_dim(value, first, rows, 0),
+                lax.dynamic_slice_in_dim(columns, first, rows, 0),
+                filler,
+            ],
+            axis=1,
+        ).astype(jnp.float32)
+
+    return reduce_pieces([piece(r) for r in range(count)])
+
+
+def sum_over_expert(value):
+    count = lax.axis_size("expert")
+    parts = lax.all_to_all(
+        value.reshape(count, value.shape[0] // count, value.shape[1]),
+        "expert",
+        split_axis=0,
+        concat_axis=0,
+        tiled=True,
+    )
+    total = jnp.sum(parts.astype(jnp.float32), axis=0).astype(jnp.bfloat16)
+    return lax.all_gather(total, "expert", axis=0, tiled=True)
 
 
 def dot32(left, right, spec):
@@ -371,22 +392,7 @@
     group_tok = shard_count * tok_count
     info = jnp.stack([lengths[0, 0], lengths[0, 0] + lengths[0, 1]]).astype(jnp.int32)
     vectors = toeplitz_vectors(rel_bias, group_tok // tile)
-    weights_in = (w_gate[0], w_up[0], w_down[0])
-    across = tuple(partner(w, 2) for w in weights_in)
-    attended_group, logs = attend(info, qkv, vectors)
-    attended_group, across = lax.optimization_barrier((attended_group, across))
-    gate_pieces, up_pieces, down_pieces = (
-        [w, partner(w, 1), x, partner(x, 1)] for w, x in zip(weights_in, across)
-    )
-    attended = swap_heads(attended_group).reshape(model_width, tok_count)
-    hidden_one = inputs + dot32(attended, full_out, "dt,de->te")
-    normed_two, inverse_two = norm_forward(hidden_one)
-    normed_ffn = (normed_two * ffn_gain).astype(jnp.bfloat16)
-    logits = jnp.dot(normed_ffn, full_router, preferred_element_type=jnp.float32)
     expert_ids = jnp.arange(expert_count, dtype=jnp.int32)
-    chosen_mask = routes[:, :, None] == expert_ids[None, None, :]
-    chosen = jnp.sum(jnp.where(chosen_mask, logits[:, None, :], 0.0), axis=2)
-    gate_weights = jax.nn.softmax(chosen, axis=1)
     flat_routes = routes.reshape(-1)
     onehot_rows = (flat_routes[:, None] == expert_ids[None, :]).astype(jnp.int32)
     earlier = jnp.cumsum(onehot_rows, axis=0) - onehot_rows
@@ -407,6 +413,28 @@
             tiled=True,
         ).reshape(expert_count * capacity, model_width)
 
+    cotangent_rows = dispatch(cotangent)
+    weights_in = (w_gate[0], w_up[0], w_down[0])
+    across = tuple(partner(w, 2) for w in weights_in)
+    attended_group, logs = attend(info, qkv, vectors)
+    attended_group, across_gate, across_up, cotangent_rows, full_out, full_router = (
+        lax.optimization_barrier(
+            (attended_group, across[0], across[1], cotangent_rows, full_out, full_router)
+        )
+    )
+    attended = swap_heads(attended_group).reshape(model_width, tok_count)
+    hidden_one = inputs + dot32(attended, full_out, "dt,de->te")
+    hidden_one, across_down = lax.optimization_barrier((hidden_one, across[2]))
+    gate_pieces, up_pieces, down_pieces = (
+        [w, partner(w, 1), x, partner(x, 1)]
+        for w, x in zip(weights_in, (across_gate, across_up, across_down))
+    )
+    normed_two, inverse_two = norm_forward(hidden_one)
+    normed_ffn = (normed_two * ffn_gain).astype(jnp.bfloat16)
+    logits = jnp.dot(normed_ffn, full_router, preferred_element_type=jnp.float32)
+    chosen_mask = routes[:, :, None] == expert_ids[None, None, :]
+    chosen = jnp.sum(jnp.where(chosen_mask, logits[:, None, :], 0.0), axis=2)
+    gate_weights = jax.nn.softmax(chosen, axis=1)
     def give_back(rows):
         return lax.all_to_all(
             rows.reshape(expert_count, capacity, model_width),
@@ -423,14 +451,16 @@
     slot_gates = lax.all_to_all(
         slot_gates.reshape(expert_count, capacity), "expert", 0, 0, tiled=True
     ).reshape(-1)
-    cotangent_rows = dispatch(cotangent)
     rows_in = dispatch(normed_ffn)
     grad_rows_out = (slot_gates[:, None] * cotangent_rows.astype(jnp.float32)).astype(jnp.bfloat16)
     gate_proj = [dot32(rows_in, w, "rd,df->rf") for w in gate_pieces]
     up_proj = [dot32(rows_in, w, "rd,df->rf") for w in up_pieces]
     hidden = [gated_unit(a, b).astype(jnp.bfloat16) for a, b in zip(gate_proj, up_proj)]
     down_sum = sum(dot32(x, w, "rf,fd->rd") for x, w in zip(hidden, down_pieces))
-    returned = give_back(down_sum.astype(jnp.bfloat16))
+    down_low, grad_rows_out = lax.optimization_barrier(
+        (down_sum.astype(jnp.bfloat16), grad_rows_out)
+    )
+    returned = give_back(down_low)
     routed_out = jnp.stack(
         [dot32(p.astype(jnp.bfloat16), returned, "ts,sd->td") for p in pick], axis=1
     )
@@ -459,7 +489,10 @@
         up_low.append(grad_up_f.astype(jnp.bfloat16))
         grad_input = grad_input + dot32(gate_low[r], gate_pieces[r], "rf,df->rd")
         grad_input = grad_input + dot32(up_low[r], up_pieces[r], "rf,df->rd")
-    grad_back = give_back(grad_input.astype(jnp.bfloat16))
+    grad_low, rows_in, grad_rows_out = lax.optimization_barrier(
+        (grad_input.astype(jnp.bfloat16), rows_in, grad_rows_out)
+    )
+    grad_back = give_back(grad_low)
     grad_gate_w = reduce_near([dot32(rows_in, x, "rd,rf->df") for x in gate_low])
     grad_up_w = reduce_near([dot32(rows_in, x, "rd,rf->df") for x in up_low])
     grad_down_w = reduce_near([dot32(x, grad_rows_out, "rf,rd->fd") for x in hidden])
@@ -469,26 +502,36 @@
     grad_attn_low = grad_hidden_one.astype(jnp.bfloat16)
     grad_out_full = dot32(attended, grad_attn_low, "dt,te->de")
     grad_attended = dot32(full_out, grad_attn_low, "de,te->dt").astype(jnp.bfloat16)
+    grad_attended, grad_gate_w, grad_up_w, grad_down_w = lax.optimization_barrier(
+        (grad_attended, grad_gate_w, grad_up_w, grad_down_w)
+    )
     grad_group = swap_heads(grad_attended.reshape(attended_group.shape))
-    filler = jnp.zeros((model_width, -(expert_count + 1) % 128), jnp.float32)
-    early = jnp.concatenate(
-        [grad_out_full, grad_router_full, grad_gain_ffn_full[:, None], filler], axis=1
-    )
-    early = lax.psum(reduce_rows(early, shard_index).astype(jnp.bfloat16), "expert")
+    grad_gate_w, grad_up_w, grad_down_w = (
+        (near, partner(far, 2)) for near, far in (grad_gate_w, grad_up_w, grad_down_w)
+    )
+    early = reduce_rows(
+        grad_out_full.astype(jnp.bfloat16),
+        jnp.concatenate([grad_router_full, grad_gain_ffn_full[:, None]], axis=1).astype(
+            jnp.bfloat16
+        ),
+        shard_index,
+    )
+    early = lax.psum(early.astype(jnp.bfloat16), "expert")
     grad_query, grad_keys, grad_values, diag = attend_back(
         info, qkv, grad_group, attended_group, logs, vectors
     )
     grad_table = table_gradient(diag, bucket_count)
     grad_cols = jnp.concatenate([grad_query, grad_keys, grad_values], axis=1)
-    grad_cols, early, grad_gate_w, grad_up_w, grad_down_w = lax.optimization_barrier(
-        (grad_cols, early, grad_gate_w, grad_up_w, grad_down_w)
-    )
-    early = early.astype(jnp.float32)
+    grad_cols, grad_gate_w, grad_up_w, grad_down_w = lax.optimization_barrier(
+        (grad_cols, grad_gate_w, grad_up_w, grad_down_w)
+    )
     grad_gate_w, grad_up_w, grad_down_w = (
         (near + far.astype(jnp.float32))[None]
         for near, far in (grad_gate_w, grad_up_w, grad_down_w)
     )
-    grad_cols = swap_heads(grad_cols).reshape(shard_count, 3, local_heads, head_dim, tok_count)
+    grad_cols, early = lax.optimization_barrier((swap_heads(grad_cols), early))
+    early = early.astype(jnp.float32)
+    grad_cols = grad_cols.reshape(shard_count, 3, local_heads, head_dim, tok_count)
     grad_cols = grad_cols.transpose(1, 0, 2, 3, 4).reshape(3 * model_width, tok_count)
     grad_qkv_full = dot32(normed_attn, grad_cols, "td,ft->df")
     grad_normed_attn = dot32(grad_cols, full_qkv, "ft,df->td")
@@ -496,14 +539,19 @@
         grad_normed_attn, normed_one, inverse_one, attn_gain
     )
     grad_tokens = grad_hidden_one + grad_one
-    filler = jnp.zeros((model_width, 127), jnp.float32)
-    late = jnp.concatenate([grad_qkv_full, grad_gain_attn_full[:, None], filler], axis=1)
-    late = reduce_rows(late, shard_index)
+    late = reduce_rows(
+        grad_qkv_full.astype(jnp.bfloat16),
+        grad_gain_attn_full[:, None].astype(jnp.bfloat16),
+        shard_index,
+    )
     table_column = jnp.pad(grad_table.reshape(-1), (0, late.shape[0] - grad_table.size))
     late = late + jnp.pad(
         table_column[:, None], ((0, 0), (3 * model_width + 1, late.shape[1] - 3 * model_width - 2))
     )
-    late = lax.psum(late.astype(jnp.bfloat16), "expert").astype(jnp.float32)
+    row_count = late.shape[0]
+    late = late.astype(jnp.bfloat16)
+    late = jnp.pad(late, ((0, -row_count % lax.axis_size("expert")), (0, 0)))
+    late = sum_over_expert(late)[:row_count].astype(jnp.float32)
     pieces = (
         late[:, : 3 * model_width],
         early[:, :model_width],

time: 920 us -> 966 us (1.050)
  blocking collectives: 44.8 us -> 111 us
  waiting for transfers between devices: 322 us -> 299 us
  starting transfers between devices: 47.6 us -> 67.2 us
  local copies, waits for them, and re-layouts: 42.8 us -> 27.3 us
    all_gather x1, blocking collectives: 5.19 us -> 69.8 us  [local(): lax.all_gather(router, 'shard', axis=0, tiled=True)]
    all_gather x0 -> x1, blocking collectives: none -> 32.7 us  [sum_over_expert(): return lax.all_gather(total, 'expert', axis=0, tiled=True)]
    all_to_all x1 -> x0, blocking collectives: 31.3 us -> none  [swap_heads(): lax.all_to_all(value, 'shard', split_axis=0, concat_axis=0, tiled=True)]
    all_to_all x2, waiting for transfers between devices: 85.8 us -> 63.6 us  [dispatch(): lax.all_to_all(packed.reshape(expert_count, capacity, model_width), 'expe...]
    ppermute x24, waiting for transfers between devices: 50.9 us -> 67.7 us  [partner(): return lax.ppermute(value, 'shard', [(i, i ^ flip) for i in range(count)])]
    psum x2 -> x1, waiting for transfers between devices: 85.7 us -> 69.4 us  [local(): early = lax.psum(early.astype(jnp.bfloat16), 'expert')]
    all_to_all x3 -> x4, waiting for transfers between devices: 25.5 us -> 41.5 us  [swap_heads(): lax.all_to_all(value, 'shard', split_axis=0, concat_axis=0, tiled=True)]
    all_gather x1, waiting for transfers between devices: 14.3 us -> 0.02 us  [local(): lax.all_gather(w_out, 'shard', axis=0, tiled=True)]
  transfers between devices with their start and end apart: 36 -> 37, of which waited for: 16 -> 14; matrix products, arithmetic and copies ran while one was open for 34% -> 28% of each run, Pallas kernels for 11% -> 10%
where the time goes in v3:
time: 966 us; the launch traced here: 955 us
  waiting for transfers between devices  299 us (31%)
  matrix products  295 us (31%)
  blocking collectives  111 us (11%)
  Pallas kernels  98.1 us (10%)
  starting transfers between devices  67.2 us (7%)
  other arithmetic  40.4 us (4%)
  local copies, waits for them, and re-layouts  27.3 us (3%)
  between operations  17.2 us (2%)
    dot_general x47, matrix products, dot32(): return jnp.einsum(spec, left, right, preferred_element_type=jnp.float32)  291 us
    all_gather x1, blocking collectives, local(): lax.all_gather(router, 'shard', axis=0, tiled=True)  69.8 us
    psum x1, waiting for transfers between devices, local(): early = lax.psum(early.astype(jnp.bfloat16), 'expert')  69.4 us
    ppermute x24, waiting for transfers between devices, partner(): return lax.ppermute(value, 'shard', [(i, i ^ flip) for i in range(count)])  67.7 us
    all_to_all x2, waiting for transfers between devices, dispatch(): lax.all_to_all(packed.reshape(expert_count, capacity, model_width), 'expe...  63.6 us
    pallas_call x1, Pallas kernels, attend_back(): pl.pallas_call(attend_back_kernel, grid=(heads,), in_specs=[pl.BlockSpec(...  54 us
    pallas_call x1, Pallas kernels, attend(): pl.pallas_call(attend_kernel, grid=(heads,), in_specs=[pl.BlockSpec(memor...  44.1 us
    all_to_all x4, waiting for transfers between devices, swap_heads(): lax.all_to_all(value, 'shard', split_axis=0, concat_axis=0, tiled=True)  41.5 us
  transfers between devices with their start and end apart: 37, of which 14 were waited for; matrix products, arithmetic and copies ran while one was open for 28% of the time, Pallas kernels for 10%

profile of v3, /device:TPU:0, one launch (start us, length us, event | category | flops | bytes accessed | tf_op | source)
XLA Modules:
  0.0 954.8 jit_solution(8405336313113741157)
XLA Ops:
  11.5 8.3 all-reduce.4
  21.3 21.8 %all-gather.4.cloned.1.call-done = bf16[768,2304]{1,0:T(8,128)(2,1)} async-done(((bf16[192,2304]{1,0:T(8,128)(2,1)}), bf16[768,2304]{1,0:T(8,128)(2,1)}) %all-gather.4.cloned.1.call-update) | async-done | bytes 3538960 | tf_op jit(solution)/shard_map/all_gather | solution.py:370
  68.6 23.7 %all-to-all-done.q_ref.k_ref.v_ref = bf16[4,9,64,512]{3,2,1,0:T(8,128)(2,1)S(1)} async-done(((bf16[4,9,64,512]{3,2,1,0:T(8,128)(2,1)}), bf16[4,9,64,512]{3,2,1,0:T(8,128)(2,1)S(1)}, u32[]{:S(2)}, u32[]{:S(2)}) %all-to-all-start) | async-done | bytes 2359328 | tf_op jit(solution)/shard_map/all_to_all | solution.py:296
  98.9 69.8 %all-gather = bf16[4,192,8]{1,2,0:T(8,128)(2,1)S(1)} all-gather(bf16[1,192,8]{1,2,0:T(8,128)(2,1)S(1)} %bitcast.205), channel_id=1, replica_groups=mesh['expert'=8,'shard'=4] {'shard'}, dimensions={0}, use_global_device_ids=true | all-gather | bytes 15360 | tf_op jit(solution)/shard_map/all_gather | solution.py:372
  171.4 44.1 %attend.1 = (bf16[4,3,64,512]{3,2,1,0:T(8,128)(2,1)}, f32[3,8,256]{2,1,0:T(8,128)S(1)}) custom-call(s32[2]{0:T(128)S(1)} %pad_add_fusion.info_ref, bf16[4,9,64,512]{3,2,1,0:T(8,128)(2,1)S(1)} %all-to-all-done.q_ref.k_ref.v_ref, bf16[4,9,64,512]{3,2,1,0:T(8,128)(2,1)S(1)} %all-to-all-done.q_ref.k_ref.v_ref, ...), custom_call_target="tpu_custom_call" | custom-call | flops 51539607552 | bytes 2359296 | tf_op jit(solution)/shard_map/attend/pallas_call | solution.py:196
  219.1 11.6 %all-to-all-done.2 = bf16[4,3,64,512]{3,2,1,0:T(8,128)(2,1)S(1)} async-done(((bf16[4,3,64,512]{3,2,1,0:T(8,128)(2,1)}), bf16[4,3,64,512]{3,2,1,0:T(8,128)(2,1)S(1)}, u32[]{:S(2)}, u32[]{:S(2)}) %all-to-all-start.2) | async-done | bytes 786464 | tf_op jit(solution)/shard_map/all_to_all | solution.py:296
  238.2 13.0 %all-to-all-start.4 = ((f32[8,1,256]{2,1,0:T(1,128)}), f32[8,1,256]{2,1,0:T(1,128)S(1)}, u32[]{:S(2)}, u32[]{:S(2)}) async-start(f32[8,1,256]{2,1,0:T(1,128)} %bitcast.23), calls=%async_computation.4 | async-start | bytes 16384 | tf_op jit(solution)/shard_map/all_to_all | solution.py:451
  268.0 63.6 %all-to-all-done.3 = bf16[8,256,768]{2,1,0:T(8,128)(2,1)} async-done(((bf16[8,256,768]{2,1,0:T(8,128)(2,1)}), bf16[8,256,768]{2,1,0:T(8,128)(2,1)}, u32[]{:S(2)}, u32[]{:S(2)}) %all-to-all-start.3) | async-done | bytes 3145760 | tf_op jit(solution)/shard_map/all_to_all | solution.py:408
  336.4 7.1 fusion.107
  343.6 10.8 %multiply_convert_fusion.6 = (bf16[2048,768]{1,0:T(8,128)(2,1)S(1)}, f32[2048,768]{1,0:T(8,128)}) fusion(f32[2048,768]{1,0:T(8,128)S(1)} %fusion.116, bf16[2048,768]{1,0:T(8,128)(2,1)} %bitcast.20, bf16[768,768]{1,0:T(8,128)(2,1)} %collective-permute-done.1), kind=kOutput, calls=%fused_computation.44 | convolution fusion | flops 2431647744 | bytes 20054016 | tf_op jit(solution)/shard_map/rd,df->rf/dot_general | solution.py:332
  360.4 11.0 %multiply_convert_fusion.8 = (bf16[2048,768]{1,0:T(8,128)(2,1)S(1)}, f32[2048,768]{1,0:T(8,128)}) fusion(f32[2048,768]{1,0:T(8,128)S(1)} %fusion.107, bf16[2048,768]{1,0:T(8,128)(2,1)} %bitcast.20, bf16[1,768,768]{2,1,0:T(8,128)(2,1)} %param.21), kind=kOutput, calls=%fused_computation.46 | convolution fusion | flops 2431647744 | bytes 20054016 | tf_op jit(solution)/shard_map/rd,df->rf/dot_general | solution.py:332
  371.5 9.7 %multiply_convert_fusion.7 = (bf16[2048,768]{1,0:T(8,128)(2,1)S(1)}, f32[2048,768]{1,0:T(8,128)}) fusion(f32[2048,768]{1,0:T(8,128)S(1)} %fusion.114, bf16[2048,768]{1,0:T(8,128)(2,1)} %bitcast.20, bf16[768,768]{1,0:T(8,128)(2,1)} %collective-permute-done.4), kind=kOutput, calls=%fused_computation.45 | convolution fusion | flops 2431647744 | bytes 20054016 | tf_op jit(solution)/shard_map/rd,df->rf/dot_general | solution.py:332
  400.0 9.5 multiply_convert_fusion.5
  409.5 6.7 add_convert_fusion.1
  416.2 9.8 %fusion.20 = (bf16[2048,768]{1,0:T(8,128)(2,1)S(1)}, bf16[2048,768]{1,0:T(8,128)(2,1)S(1)}) fusion(f32[2048,768]{1,0:T(8,128)} %copy-done.77, f32[2048,768]{1,0:T(8,128)} %get-tuple-element.194, bf16[2048,768]{1,0:T(8,128)(2,1)S(1)} %multiply_convert_fusion.4, bf16[768,768]{1,0:T(8,128)(2,1)} %collective-permute-done.2), kind=kOutput, calls=%fused_computation.28 | convolution fusion | flops 2453667840 | bytes 23199744 | tf_op jit(solution)/shard_map/rd,fd->rf/dot_general | solution.py:332
  426.1 7.0 fusion.122
  439.3 8.3 multiply_convert_fusion.3
  447.6 6.7 fusion.105
  464.9 10.8 %fusion.27 = (bf16[2048,768]{1,0:T(8,128)(2,1)S(1)}, bf16[2048,768]{1,0:T(8,128)(2,1)}) fusion(f32[2048,768]{1,0:T(8,128)} %copy-done.78, f32[2048,768]{1,0:T(8,128)} %get-tuple-element.192, bf16[2048,768]{1,0:T(8,128)(2,1)S(1)} %multiply_convert_fusion.4, bf16[768,768]{1,0:T(8,128)(2,1)} %collective-permute-done.8), kind=kOutput, calls=%fused_computation.35 | convolution fusion | flops 2453667840 | bytes 23199744 | tf_op jit(solution)/shard_map/rd,fd->rf/dot_general | solution.py:332
  475.6 6.7 fusion.123
  482.3 9.6 %fusion.13 = (bf16[2048,768]{1,0:T(8,128)(2,1)S(1)}, bf16[2048,768]{1,0:T(8,128)(2,1)S(1)}) fusion(f32[2048,768]{1,0:T(8,128)} %copy-done.75, f32[2048,768]{1,0:T(8,128)} %get-tuple-element.198, bf16[2048,768]{1,0:T(8,128)(2,1)S(1)} %multiply_convert_fusion.4, bf16[768,768]{1,0:T(8,128)(2,1)} %collective-permute-done.5), kind=kOutput, calls=%fused_computation.21 | convolution fusion | flops 2453667840 | bytes 23199744 | tf_op jit(solution)/shard_map/rd,fd->rf/dot_general | solution.py:332
  491.9 6.7 fusion.120
  505.0 20.5 %add_convert_fusion = bf16[2048,768]{1,0:T(8,128)(2,1)} fusion(f32[2048,768]{1,0:T(8,128)} %fusion.123, f32[2048,768]{1,0:T(8,128)} %fusion.122, f32[2048,768]{1,0:T(8,128)} %fusion.121, f32[2048,768]{1,0:T(8,128)} %fusion.120, f32[2048,768]{1,0:T(8,128)} %fusion.119, f32[2048,768]{1,0:T(8,128)} %fusion.105, f32[2048,768]{1,0:T(8,128)} %fusion.101, ...), kind=kOutput, calls=%fused_computation.36 | convolution fusion | flops 2428502016 | bytes 51511296 | tf_op jit(solution)/shard_map/rf,df->rd/dot_general | solution.py:332
  525.6 6.7 convolution_convert_fusion.10
  606.2 24.7 %all-to-all-done.6 = bf16[8,256,768]{2,1,0:T(8,128)(2,1)} async-done(((bf16[8,256,768]{2,1,0:T(8,128)(2,1)}), bf16[8,256,768]{2,1,0:T(8,128)(2,1)}, u32[]{:S(2)}, u32[]{:S(2)}) %all-to-all-start.6) | async-done | bytes 3145760 | tf_op jit(solution)/shard_map/all_to_all | solution.py:439
  656.2 54.0 %attend_back.1 = (bf16[4,3,64,512]{3,2,1,0:T(8,128)(2,1)S(1)}, bf16[4,3,64,512]{3,2,1,0:T(8,128)(2,1)S(1)}, bf16[4,3,64,512]{3,2,1,0:T(8,128)(2,1)S(1)}, f32[3,8,8,512]{3,2,1,0:T(8,128)S(1)}) custom-call(s32[2]{0:T(128)S(1)} %copy-done.4, bf16[4,9,64,512]{3,2,1,0:T(8,128)(2,1)} %copy-done.2, bf16[4,9,64,512]{3,2,1,0:T(8,128)(2,1)} %copy-done.2, ...), custom_call_target="tpu_custom_call" | custom-call | flops 128849018880 | bytes 4718592 | tf_op jit(solution)/shard_map/attend_back/pallas_call | solution.py:226
  711.9 19.7 %collective-permute-done.17 = bf16[768,768]{1,0:T(8,128)(2,1)} collective-permute-done((bf16[768,768]{1,0:T(8,128)(2,1)}, bf16[768,768]{1,0:T(8,128)(2,1)}, u32[]{:S(2)}, u32[]{:S(2)}) %collective-permute-start.17) | collective-permute-done | bytes 1179680 | tf_op jit(solution)/shard_map/ppermute | solution.py:280
  743.6 27.5 %collective-permute-done.20 = bf16[192,896]{1,0:T(8,128)(2,1)S(1)} collective-permute-done((bf16[192,896]{1,0:T(8,128)(2,1)}, bf16[192,896]{1,0:T(8,128)(2,1)S(1)}, u32[]{:S(2)}, u32[]{:S(2)}) %collective-permute-start.20) | collective-permute-done | bytes 344096 | tf_op jit(solution)/shard_map/ppermute | solution.py:280
  773.0 69.4 %all-reduce.7.cloned.1.call-done = bf16[192,896]{1,0:T(8,128)(2,1)} async-done(((bf16[192,896]{1,0:T(8,128)(2,1)}), bf16[192,896]{1,0:T(8,128)(2,1)}) %all-reduce.7.cloned.1.call-update) | async-done | bytes 344080 | tf_op jit(solution)/shard_map/psum | solution.py:519
  864.4 18.4 %collective-permute-done.23 = bf16[192,2432]{1,0:T(8,128)(2,1)} collective-permute-done((bf16[192,2432]{1,0:T(8,128)(2,1)}, bf16[192,2432]{1,0:T(8,128)(2,1)}, u32[]{:S(2)}, u32[]{:S(2)}) %collective-permute-start.23) | collective-permute-done | bytes 933920 | tf_op jit(solution)/shard_map/ppermute | solution.py:280
  905.7 6.5 all-to-all-done.9
  912.4 32.7 %all_gather.23 = bf16[192,2432]{1,0:T(8,128)(2,1)S(1)} all-gather(bf16[24,2432]{1,0:T(8,128)(2,1)S(1)} %reduce_sum.165), channel_id=1, replica_groups=mesh['expert'=8,'shard'=4] {'expert'}, dimensions={0}, use_global_device_ids=true | all-gather | bytes 1050624 | tf_op jit(solution)/shard_map/all_gather | solution.py:328
  (367 shorter events, 281.0 us)
Async XLA Ops:
  7.2 35.9 %all-gather.4.cloned.1.call-start = ((), (), s32[]{:S(2)}) async-start(), calls=%async_computation.10 | async-start | bytes 4423680 | tf_op jit(solution)/shard_map/all_gather | solution.py:370
  53.3 39.0 %all-to-all-start = ((bf16[4,9,64,512]{3,2,1,0:T(8,128)(2,1)}), bf16[4,9,64,512]{3,2,1,0:T(8,128)(2,1)S(1)}, u32[]{:S(2)}, u32[]{:S(2)}) async-start(bf16[4,9,64,512]{3,2,1,0:T(8,128)(2,1)} %bitcast.180), calls=%async_computation | async-start | bytes 4718592 | tf_op jit(solution)/shard_map/all_to_all | solution.py:296
  57.0 158.5 %all-gather.6.cloned.1.call-start = ((), (), s32[]{:S(2)}) async-start(), calls=%async_computation.11 | async-start | bytes 1474560 | tf_op jit(solution)/shard_map/all_gather | solution.py:371
  57.1 158.4 %collective-permute-start = (bf16[768,768]{1,0:T(8,128)(2,1)}, bf16[768,768]{1,0:T(8,128)(2,1)}, u32[]{:S(2)}, u32[]{:S(2)}) collective-permute-start(bf16[768,768]{1,0:T(8,128)(2,1)} %bitcast.9), channel_id=1, source_target_pairs={{0,2},{1,3},{2,0},{3,1},{4,6},{5,7},{6,4},{7,5},{8,10},{9,11},{10,... | collective-permute-start | bytes 3538952 | tf_op jit(solution)/shard_map/ppermute | solution.py:280
  59.0 156.5 %collective-permute-start.1 = (bf16[768,768]{1,0:T(8,128)(2,1)}, bf16[768,768]{1,0:T(8,128)(2,1)}, u32[]{:S(2)}, u32[]{:S(2)}) collective-permute-start(bf16[768,768]{1,0:T(8,128)(2,1)} %bitcast.10), channel_id=1, source_target_pairs={{0,2},{1,3},{2,0},{3,1},{4,6},{5,7},{6,4},{7,5},{8,10},{9,11},{10,... | collective-permute-start | bytes 3538952 | tf_op jit(solution)/shard_map/ppermute | solution.py:280
  59.2 174.1 %collective-permute-start.2 = (bf16[768,768]{1,0:T(8,128)(2,1)}, bf16[768,768]{1,0:T(8,128)(2,1)}, u32[]{:S(2)}, u32[]{:S(2)}) collective-permute-start(bf16[768,768]{1,0:T(8,128)(2,1)} %bitcast.18), channel_id=1, source_target_pairs={{0,2},{1,3},{2,0},{3,1},{4,6},{5,7},{6,4},{7,5},{8,10},{9,11},{10,... | collective-permute-start | bytes 3538952 | tf_op jit(solution)/shard_map/ppermute | solution.py:280
  92.3 123.2 %all-to-all-start.1 = ((bf16[8,256,768]{2,1,0:T(8,128)(2,1)}), bf16[8,256,768]{2,1,0:T(8,128)(2,1)}, u32[]{:S(2)}, u32[]{:S(2)}) async-start(bf16[8,256,768]{2,1,0:T(8,128)(2,1)} %bitcast.186), calls=%async_computation.1 | async-start | bytes 6291456 | tf_op jit(solution)/shard_map/all_to_all | solution.py:408
  215.5 15.1 %all-to-all-start.2 = ((bf16[4,3,64,512]{3,2,1,0:T(8,128)(2,1)}), bf16[4,3,64,512]{3,2,1,0:T(8,128)(2,1)S(1)}, u32[]{:S(2)}, u32[]{:S(2)}) async-start(bf16[4,3,64,512]{3,2,1,0:T(8,128)(2,1)} %get-tuple-element.47.o_ref), calls=%async_computation.2 | async-start | bytes 1572864 | tf_op jit(solution)/shard_map/all_to_all | solution.py:296
  238.2 19.5 %all-to-all-start.4 = ((f32[8,1,256]{2,1,0:T(1,128)}), f32[8,1,256]{2,1,0:T(1,128)S(1)}, u32[]{:S(2)}, u32[]{:S(2)}) async-start(f32[8,1,256]{2,1,0:T(1,128)} %bitcast.23), calls=%async_computation.4 | async-start | bytes 16384 | tf_op jit(solution)/shard_map/all_to_all | solution.py:451
  257.8 73.8 %all-to-all-start.3 = ((bf16[8,256,768]{2,1,0:T(8,128)(2,1)}), bf16[8,256,768]{2,1,0:T(8,128)(2,1)}, u32[]{:S(2)}, u32[]{:S(2)}) async-start(bf16[8,256,768]{2,1,0:T(8,128)(2,1)} %bitcast.185), calls=%async_computation.3 | async-start | bytes 6291456 | tf_op jit(solution)/shard_map/all_to_all | solution.py:408
  262.4 92.0 %collective-permute-start.3 = (bf16[768,768]{1,0:T(8,128)(2,1)}, bf16[768,768]{1,0:T(8,128)(2,1)}, u32[]{:S(2)}, u32[]{:S(2)}) collective-permute-start(bf16[768,768]{1,0:T(8,128)(2,1)} %bitcast.9), channel_id=1, source_target_pairs={{0,1},{1,0},{2,3},{3,2},{4,5},{5,4},{6,7},{7,6},{8,9},{9,8},{10,11... | collective-permute-start | bytes 3538952 | tf_op jit(solution)/shard_map/ppermute | solution.py:280
  262.5 109.0 %collective-permute-start.4 = (bf16[768,768]{1,0:T(8,128)(2,1)}, bf16[768,768]{1,0:T(8,128)(2,1)}, u32[]{:S(2)}, u32[]{:S(2)}) collective-permute-start(bf16[768,768]{1,0:T(8,128)(2,1)} %bitcast.10), channel_id=1, source_target_pairs={{0,1},{1,0},{2,3},{3,2},{4,5},{5,4},{6,7},{7,6},{8,9},{9,8},{10,11... | collective-permute-start | bytes 3538952 | tf_op jit(solution)/shard_map/ppermute | solution.py:280
  263.0 132.2 %collective-permute-start.5 = (bf16[768,768]{1,0:T(8,128)(2,1)}, bf16[768,768]{1,0:T(8,128)(2,1)}, u32[]{:S(2)}, u32[]{:S(2)}) collective-permute-start(bf16[768,768]{1,0:T(8,128)(2,1)} %bitcast.18), channel_id=1, source_target_pairs={{0,1},{1,0},{2,3},{3,2},{4,5},{5,4},{6,7},{7,6},{8,9},{9,8},{10,11... | collective-permute-start | bytes 3538952 | tf_op jit(solution)/shard_map/ppermute | solution.py:280
  265.0 124.9 %collective-permute-start.6 = (bf16[768,768]{1,0:T(8,128)(2,1)}, bf16[768,768]{1,0:T(8,128)(2,1)}, u32[]{:S(2)}, u32[]{:S(2)}) collective-permute-start(bf16[768,768]{1,0:T(8,128)(2,1)} %collective-permute-done), channel_id=1, source_target_pairs={{0,1},{1,0},{2,3},{3,2},{4,5},{5,4},{6,7},{7,6},{8,9},{9,8},{10,11... | collective-permute-start | bytes 3538952 | tf_op jit(solution)/shard_map/ppermute | solution.py:280
  265.4 134.6 %collective-permute-start.7 = (bf16[768,768]{1,0:T(8,128)(2,1)}, bf16[768,768]{1,0:T(8,128)(2,1)}, u32[]{:S(2)}, u32[]{:S(2)}) collective-permute-start(bf16[768,768]{1,0:T(8,128)(2,1)} %collective-permute-done.1), channel_id=1, source_target_pairs={{0,1},{1,0},{2,3},{3,2},{4,5},{5,4},{6,7},{7,6},{8,9},{9,8},{10,11... | collective-permute-start | bytes 3538952 | tf_op jit(solution)/shard_map/ppermute | solution.py:280
  354.4 55.1 %collective-permute-start.8 = (bf16[768,768]{1,0:T(8,128)(2,1)}, bf16[768,768]{1,0:T(8,128)(2,1)}, u32[]{:S(2)}, u32[]{:S(2)}) collective-permute-start(bf16[768,768]{1,0:T(8,128)(2,1)} %collective-permute-done.2), channel_id=1, source_target_pairs={{0,1},{1,0},{2,3},{3,2},{4,5},{5,4},{6,7},{7,6},{8,9},{9,8},{10,11... | collective-permute-start | bytes 3538952 | tf_op jit(solution)/shard_map/ppermute | solution.py:280
  460.2 93.7 %all-to-all-start.5 = ((bf16[8,256,768]{2,1,0:T(8,128)(2,1)}), bf16[8,256,768]{2,1,0:T(8,128)(2,1)}, u32[]{:S(2)}, u32[]{:S(2)}) async-start(bf16[8,256,768]{2,1,0:T(8,128)(2,1)} %bitcast.25), calls=%async_computation.5 | async-start | bytes 6291456 | tf_op jit(solution)/shard_map/all_to_all | solution.py:439
  532.3 33.0 %collective-permute-start.9 = (bf16[768,768]{1,0:T(8,128)(2,1)}, bf16[768,768]{1,0:T(8,128)(2,1)}, u32[]{:S(2)}, u32[]{:S(2)}) collective-permute-start(bf16[768,768]{1,0:T(8,128)(2,1)} %convolution_convert_fusion.10), channel_id=1, source_target_pairs={{0,1},{1,0},{2,3},{3,2},{4,5},{5,4},{6,7},{7,6},{8,9},{9,8},{10,11... | collective-permute-start | bytes 3538952 | tf_op jit(solution)/shard_map/ppermute | solution.py:280
  538.0 34.0 %collective-permute-start.10 = (bf16[768,768]{1,0:T(8,128)(2,1)}, bf16[768,768]{1,0:T(8,128)(2,1)}, u32[]{:S(2)}, u32[]{:S(2)}) collective-permute-start(bf16[768,768]{1,0:T(8,128)(2,1)} %convolution_convert_fusion.9), channel_id=1, source_target_pairs={{0,1},{1,0},{2,3},{3,2},{4,5},{5,4},{6,7},{7,6},{8,9},{9,8},{10,11... | collective-permute-start | bytes 3538952 | tf_op jit(solution)/shard_map/ppermute | solution.py:280
  553.9 77.1 %all-to-all-start.6 = ((bf16[8,256,768]{2,1,0:T(8,128)(2,1)}), bf16[8,256,768]{2,1,0:T(8,128)(2,1)}, u32[]{:S(2)}, u32[]{:S(2)}) async-start(bf16[8,256,768]{2,1,0:T(8,128)(2,1)} %bitcast.29), calls=%async_computation.6 | async-start | bytes 6291456 | tf_op jit(solution)/shard_map/all_to_all | solution.py:439
  564.7 19.6 %collective-permute-start.12 = (bf16[768,768]{1,0:T(8,128)(2,1)S(1)}, bf16[768,768]{1,0:T(8,128)(2,1)S(1)}, u32[]{:S(2)}, u32[]{:S(2)}) collective-permute-start(bf16[768,768]{1,0:T(8,128)(2,1)S(1)} %copy-done.60), channel_id=1, source_target_pairs={{0,1},{1,0},{2,3},{3,2},{4,5},{5,4},{6,7},{7,6},{8,9},{9,8},{10,11... | collective-permute-start | bytes 3538952 | tf_op jit(solution)/shard_map/ppermute | solution.py:280
  565.2 25.3 %collective-permute-start.13 = (bf16[768,768]{1,0:T(8,128)(2,1)S(1)}, bf16[768,768]{1,0:T(8,128)(2,1)S(1)}, u32[]{:S(2)}, u32[]{:S(2)}) collective-permute-start(bf16[768,768]{1,0:T(8,128)(2,1)S(1)} %copy-done.59), channel_id=1, source_target_pairs={{0,1},{1,0},{2,3},{3,2},{4,5},{5,4},{6,7},{7,6},{8,9},{9,8},{10,11... | collective-permute-start | bytes 3538952 | tf_op jit(solution)/shard_map/ppermute | solution.py:280
  565.3 29.4 %collective-permute-start.14 = (bf16[768,768]{1,0:T(8,128)(2,1)S(1)}, bf16[768,768]{1,0:T(8,128)(2,1)S(1)}, u32[]{:S(2)}, u32[]{:S(2)}) collective-permute-start(bf16[768,768]{1,0:T(8,128)(2,1)S(1)} %convolution_convert_fusion.5), channel_id=1, source_target_pairs={{0,1},{1,0},{2,3},{3,2},{4,5},{5,4},{6,7},{7,6},{8,9},{9,8},{10,11... | collective-permute-start | bytes 3538952 | tf_op jit(solution)/shard_map/ppermute | solution.py:280
  640.6 15.6 %all-to-all-start.7 = ((bf16[4,3,64,512]{3,2,1,0:T(8,128)(2,1)}), bf16[4,3,64,512]{3,2,1,0:T(8,128)(2,1)S(1)}, u32[]{:S(2)}, u32[]{:S(2)}) async-start(bf16[4,3,64,512]{3,2,1,0:T(8,128)(2,1)} %bitcast.189), calls=%async_computation.7 | async-start | bytes 1572864 | tf_op jit(solution)/shard_map/all_to_all | solution.py:296
  644.1 67.8 %collective-permute-start.15 = (bf16[768,768]{1,0:T(8,128)(2,1)}, bf16[768,768]{1,0:T(8,128)(2,1)}, u32[]{:S(2)}, u32[]{:S(2)}) collective-permute-start(bf16[768,768]{1,0:T(8,128)(2,1)} %add_convert_fusion.4), channel_id=1, source_target_pairs={{0,2},{1,3},{2,0},{3,1},{4,6},{5,7},{6,4},{7,5},{8,10},{9,11},{10,... | collective-permute-start | bytes 3538952 | tf_op jit(solution)/shard_map/ppermute | solution.py:280
  646.1 65.8 %collective-permute-start.16 = (bf16[768,768]{1,0:T(8,128)(2,1)}, bf16[768,768]{1,0:T(8,128)(2,1)}, u32[]{:S(2)}, u32[]{:S(2)}) collective-permute-start(bf16[768,768]{1,0:T(8,128)(2,1)} %add_convert_fusion.3), channel_id=1, source_target_pairs={{0,2},{1,3},{2,0},{3,1},{4,6},{5,7},{6,4},{7,5},{8,10},{9,11},{10,... | collective-permute-start | bytes 3538952 | tf_op jit(solution)/shard_map/ppermute | solution.py:280
  646.2 85.5 %collective-permute-start.17 = (bf16[768,768]{1,0:T(8,128)(2,1)}, bf16[768,768]{1,0:T(8,128)(2,1)}, u32[]{:S(2)}, u32[]{:S(2)}) collective-permute-start(bf16[768,768]{1,0:T(8,128)(2,1)} %add_convert_fusion.2), channel_id=1, source_target_pairs={{0,2},{1,3},{2,0},{3,1},{4,6},{5,7},{6,4},{7,5},{8,10},{9,11},{10,... | collective-permute-start | bytes 3538952 | tf_op jit(solution)/shard_map/ppermute | solution.py:280
  731.6 110.8 %all-to-all-start.8 = ((bf16[4,9,64,512]{3,2,1,0:T(8,128)(2,1)}), bf16[4,9,64,512]{3,2,1,0:T(8,128)(2,1)S(1)}, u32[]{:S(2)}, u32[]{:S(2)}) async-start(bf16[4,9,64,512]{3,2,1,0:T(8,128)(2,1)} %pad_maximum_fusion.1), calls=%async_computation.8 | async-start | bytes 4718592 | tf_op jit(solution)/shard_map/all_to_all | solution.py:296
  735.3 107.1 %all-reduce.7.cloned.1.call-start = ((), (), s32[]{:S(2)}) async-start(), calls=%async_computation.12 | async-start | bytes 688128 | tf_op jit(solution)/shard_map/psum | solution.py:519
  741.6 29.5 %collective-permute-start.20 = (bf16[192,896]{1,0:T(8,128)(2,1)}, bf16[192,896]{1,0:T(8,128)(2,1)S(1)}, u32[]{:S(2)}, u32[]{:S(2)}) collective-permute-start(bf16[192,896]{1,0:T(8,128)(2,1)} %add_convert_fusion.9), channel_id=1, source_target_pairs={{0,2},{1,3},{2,0},{3,1},{4,6},{5,7},{6,4},{7,5},{8,10},{9,11},{10,... | collective-permute-start | bytes 1032200 | tf_op jit(solution)/shard_map/ppermute | solution.py:280
  859.6 23.1 %collective-permute-start.23 = (bf16[192,2432]{1,0:T(8,128)(2,1)}, bf16[192,2432]{1,0:T(8,128)(2,1)}, u32[]{:S(2)}, u32[]{:S(2)}) collective-permute-start(bf16[192,2432]{1,0:T(8,128)(2,1)} %add_convert_fusion.6), channel_id=1, source_target_pairs={{0,2},{1,3},{2,0},{3,1},{4,6},{5,7},{6,4},{7,5},{8,10},{9,11},{10,... | collective-permute-start | bytes 2801672 | tf_op jit(solution)/shard_map/ppermute | solution.py:280
  885.5 26.7 %all-to-all-start.9 = ((bf16[8,24,2432]{2,1,0:T(8,128)(2,1)}), bf16[8,24,2432]{2,1,0:T(8,128)(2,1)S(1)}, u32[]{:S(2)}, u32[]{:S(2)}) async-start(bf16[8,24,2432]{2,1,0:T(8,128)(2,1)} %bitcast.182), calls=%async_computation.9 | async-start | bytes 1867776 | tf_op jit(solution)/shard_map/all_to_all | solution.py:320
  (88 other events, 1513.7 us)
Sparse Core Ops, SparseCore 0:
  9.6 33.4 all-gather.3
  59.4 25.3 all-gather.5
  773.2 69.2 all-reduce.6
